TPU v7x, 32 devices: a whole 2x2x4 slice. The times are simulated.
32 devices in a mesh: groups: 2 (over y), region: 16 (over z, x, core).
Axes of the slice: x: 2, y: 2, z: 4, core: 2. Of those that a mesh axis runs over, the one named last changes fastest.
Arguments:
- point_feats: bfloat16 [32768, 128], P(('groups', 'region')), parts along dimension 0, may hold values from -6 to 6
- point_owner: int32 [32768, 1], P(('groups', 'region')), parts along dimension 0, may hold values from 0 to 15; in each aligned block of 1024 rows (0 to 1023, 1024 to 2047, ...) at most 160 rows name the same one
- point_slot: int32 [32768], P(('groups', 'region')), parts along dimension 0, may hold values from 0 to 2047
- adjacency: int32 [512, 27], P(('groups', 'region')), parts along dimension 0, may hold values from -1 to 255, as said below
- kernel: bfloat16 [27, 128, 128], replicated, may hold values from -0.109375 to 0.109375
- cotangent: bfloat16 [512, 128, 128], P(('groups', 'region')), parts along dimension 0, may hold values from -6 to 6
Outputs:
- out_tiles: bfloat16 [512, 128, 128], P(('groups', 'region')), parts along dimension 0
- grad_points: bfloat16 [32768, 128], P(('groups', 'region')), parts along dimension 0
- grad_weight: float32 [54, 128, 128], P('groups'), parts along dimension 0
There are 2 independent parts, one for each index of `groups`. A program takes and returns all parts, laid end to end along the dimension named above; an argument that names none is the same for every part. Nothing has to cross between parts.
Inputs may be any that keep to these rules, and one draw needn't show every extreme that they name: `point_owner`: no device's points name one owner more than 160 times. `adjacency`: bricks occupy a grid of 32 x 4 x 2 brick positions; the 16 bricks stored on device r (ids r * 16 on) fill the x positions r * 2 to (r + 1) * 2 - 1 in an arbitrary storage order; entry k = 9 (a + 1) + 3 (b + 1) + (c + 1) of brick t is the brick at t's position plus (a, b, c), or -1 where that lies outside the grid.
All inputs are finite; a program needn't handle non-finite values.
Results may differ from a plain program's by a relative error of at most 0.0039.
Values may be sent and summed in bfloat16 or wider, within the bound.
No kernel may reach another device: no remote copies, remote signals or barrier semaphores. Data moves between devices by JAX's collectives and lax.ppermute only.
A program may use at most 128 MiB of HBM per device.

v0:
```python
import functools
import math

import jax
import jax.numpy as jnp
from jax import lax
from jax.experimental import pallas as pl
from jax.experimental.pallas import tpu as pltpu
from jax.sharding import PartitionSpec as P

VX = 4
VY = 4
VZ = 8
GY = 4
GZ = 2
SX = 2
KOFF = 27
NY = GY * VY
NZ = GZ * VZ
NX = SX * VX
SLAB = NY * NZ
DENSE = NX * SLAB
LANES = 128
BF = jnp.bfloat16
F32 = jnp.float32
VMEM = pl.BlockSpec(memory_space=pltpu.VMEM)
SMEM = pl.BlockSpec(memory_space=pltpu.SMEM)
PARAMS = pltpu.CompilerParams(vmem_limit_bytes=48 * 1024 * 1024)


def up_to(value, unit):
    return (value + unit - 1) // unit * unit


def iota(shape, dim, dtype=jnp.int32):
    return lax.broadcasted_iota(jnp.int32, shape, dim).astype(dtype)


def call(body, outs, args, smem=(), scratch=(), flops=0):
    moved = sum(math.prod(o.shape) * o.dtype.itemsize for o in outs)
    moved += sum(math.prod(a.shape) * a.dtype.itemsize for a in args)
    return pl.pallas_call(
        body,
        out_shape=outs,
        in_specs=[SMEM if i in smem else VMEM for i in range(len(args))],
        out_specs=[VMEM] * len(outs),
        scratch_shapes=list(scratch),
        compiler_params=PARAMS,
        cost_estimate=pl.CostEstimate(flops=flops, bytes_accessed=moved, transcendentals=0),
    )(*args)


def corner(adj_ref, t, lowest):
    tiles = adj_ref.shape[0]
    left = adj_ref[t, 4]
    layer = jnp.where((left >= lowest) & (left < lowest + tiles), 1, 0)
    before = adj_ref[t, 10]
    second = adj_ref[jnp.clip(before - lowest, 0, tiles - 1), 10] < 0
    inner = jnp.where(second, 1, 2)
    across = jnp.where(before < 0, 0, jnp.where(adj_ref[t, 16] < 0, GY - 1, inner))
    height = jnp.where(adj_ref[t, 12] >= 0, 1, 0)
    return layer * VX, across * VY, height * VZ


def pack_body(cap_rows, owner_ref, slot_ref, feats_ref, msg_ref, place_ref, table_ref):
    regions = msg_ref.shape[0]
    points = feats_ref.shape[0]
    segs = up_to(cap_rows, LANES) // LANES
    owner = owner_ref[...]
    slot = slot_ref[...]
    mine = iota((regions, points), 0) == owner
    marks = jnp.where(mine, 1.0, 0.0)
    marks_bf = marks.astype(BF)
    earlier = jnp.where(iota((LANES, LANES), 0) < iota((LANES, LANES), 1), 1.0, 0.0).astype(BF)
    carry = jnp.zeros((regions, 1), F32)
    ranks = []
    for start in range(0, points, LANES):
        seg = marks[:, start : start + LANES]
        pre = jnp.dot(marks_bf[:, start : start + LANES], earlier, preferred_element_type=F32)
        ranks.append(jnp.sum((pre + carry) * seg, axis=0, keepdims=True))
        carry = carry + jnp.sum(seg, axis=1, keepdims=True)
    rank = jnp.concatenate(ranks, axis=1).astype(jnp.int32)
    place = owner * cap_rows + rank
    place_ref[...] = jnp.broadcast_to(place, (8, points)).astype(F32)
    block = jnp.broadcast_to((place >> 7).astype(F32), (LANES, points)).astype(BF)
    within = jnp.broadcast_to((place & (LANES - 1)).astype(F32), (LANES, points)).astype(BF)
    row = iota((LANES, points), 0, F32).astype(BF)
    one = jnp.where(row == within, jnp.ones_like(row), jnp.zeros_like(row))
    feats = feats_ref[...]
    chunk = math.lcm(cap_rows, LANES)
    for start in range(0, regions * cap_rows, chunk):
        picks = [
            jnp.where(block == jnp.asarray(q, BF), one, jnp.zeros_like(one))
            for q in range(start // LANES, (start + chunk) // LANES)
        ]
        picker = jnp.concatenate(picks, axis=0)
        rows = jnp.dot(picker, feats, preferred_element_type=F32).astype(BF)
        for i in range(chunk // cap_rows):
            msg_ref[start // cap_rows + i, 0:cap_rows, :] = rows[i * cap_rows : (i + 1) * cap_rows]
    high = jnp.where(mine, (slot >> 7) + 1, 0).astype(F32)
    low = jnp.where(mine, slot & (LANES - 1), 0).astype(F32)
    values = jnp.concatenate([high, low], axis=0).astype(BF)
    by_rank = jnp.where(iota((segs * LANES, points), 0) == rank, 1.0, 0.0).astype(BF)
    table_ref[...] = lax.dot_general(
        values, by_rank, (((1,), (1,)), ((), ())), preferred_element_type=F32
    )
    line = iota((16, LANES), 0)
    for o in range(regions):
        tile = jnp.zeros((16, LANES), F32)
        for s in range(segs):
            lanes = slice(s * LANES, (s + 1) * LANES)
            tile = jnp.where(line == s, table_ref[o : o + 1, lanes], tile)
            tile = jnp.where(line == segs + s, table_ref[regions + o : regions + o + 1, lanes], tile)
        msg_ref[o, cap_rows : cap_rows + 16, :] = tile.astype(BF)


def pack(owner, slot, feats, regions, cap_rows):
    points, channels = feats.shape
    segs = up_to(cap_rows, LANES) // LANES
    return call(
        functools.partial(pack_body, cap_rows),
        [
            jax.ShapeDtypeStruct((regions, cap_rows + 16, channels), BF),
            jax.ShapeDtypeStruct((8, points), F32),
        ],
        [owner, slot, feats],
        scratch=[pltpu.VMEM((2 * regions, segs * LANES), F32)],
        flops=2 * regions * cap_rows * points * channels,
    )


def dense_body(adj_ref, bricks_ref, dense_ref, low_ref, high_ref, grid_ref):
    tiles, vox, channels = bricks_ref.shape
    lowest = lax.axis_index("region") * tiles
    for t in range(tiles):
        x, y, z = corner(adj_ref, t, lowest)
        brick = bricks_ref[t].astype(F32).reshape(VX, VY, VZ, channels)
        grid_ref[pl.ds(x, VX), pl.ds(y, VY), pl.ds(pl.multiple_of(z, VZ), VZ), :] = brick
    for x in range(NX):
        slab = grid_ref[x].reshape(SLAB, channels).astype(BF)
        dense_ref[x] = slab
        if x == 0:
            low_ref[...] = slab
        if x == NX - 1:
            high_ref[...] = slab


def to_dense(adjacency, bricks):
    channels = bricks.shape[2]
    face = jax.ShapeDtypeStruct((SLAB, channels), BF)
    return call(
        dense_body,
        [jax.ShapeDtypeStruct((NX, SLAB, channels), BF), face, face],
        [adjacency, bricks],
        smem=(0,),
        scratch=[pltpu.VMEM((NX, NY, NZ, channels), F32)],
    )


def fill_shifts(shift_ref, dense_ref, low_ref, high_ref):
    channels = dense_ref.shape[2]
    border = jnp.zeros((NZ, channels), BF)
    height = iota((SLAB, channels), 0) % NZ
    for x in range(NX + 2):
        if x == 0:
            slab = low_ref[...]
        elif x == NX + 1:
            slab = high_ref[...]
        else:
            slab = dense_ref[x - 1]
        wide = slab.astype(F32)
        lower = jnp.where(height == 0, 0.0, pltpu.roll(wide, 1, 0))
        upper = jnp.where(height == NZ - 1, 0.0, pltpu.roll(wide, SLAB - 1, 0))
        for c, copy in enumerate((lower.astype(BF), slab, upper.astype(BF))):
            shift_ref[c, x, 0:NZ, :] = border
            shift_ref[c, x, NZ : NZ + SLAB, :] = copy
            shift_ref[c, x, NZ + SLAB : NZ + SLAB + NZ, :] = border


def conv_slab(shift_ref, weights_ref, x):
    pieces = []
    for k in range(KOFF):
        a, b, c = k // 9, k // 3 % 3, k % 3
        pieces.append(shift_ref[c, x + a, b * NZ : b * NZ + SLAB, :])
    return jnp.dot(
        jnp.concatenate(pieces, axis=1), weights_ref[...], preferred_element_type=F32
    )


SHIFTS = (3, NX + 2, SLAB + 2 * NZ)


def gradient_body(dense_ref, low_ref, high_ref, weights_ref, grad_ref, shift_ref):
    fill_shifts(shift_ref, dense_ref, low_ref, high_ref)

    def step(x, carry):
        grad_ref[x] = conv_slab(shift_ref, weights_ref, x)
        return carry

    lax.fori_loop(0, NX, step, 0)


def gradient(dense, low, high, weights):
    channels = dense.shape[2]
    return call(
        gradient_body,
        [
            jax.ShapeDtypeStruct((NX, SLAB, channels), F32),
            jax.ShapeDtypeStruct(SHIFTS + (channels,), BF),
        ],
        [dense, low, high, weights],
        flops=2 * DENSE * KOFF * channels * channels,
    )


def forward_body(adj_ref, dense_ref, low_ref, high_ref, weights_ref, out_ref, shift_ref, grid_ref):
    tiles, vox, channels = out_ref.shape
    lowest = lax.axis_index("region") * tiles
    fill_shifts(shift_ref, dense_ref, low_ref, high_ref)

    def step(x, carry):
        grid_ref[x] = conv_slab(shift_ref, weights_ref, x).reshape(NY, NZ, channels)
        return carry

    lax.fori_loop(0, NX, step, 0)
    for t in range(tiles):
        x, y, z = corner(adj_ref, t, lowest)
        brick = grid_ref[pl.ds(x, VX), pl.ds(y, VY), pl.ds(pl.multiple_of(z, VZ), VZ), :]
        out_ref[t] = brick.reshape(vox, channels).astype(BF)


def forward(adjacency, dense, low, high, weights, tiles):
    channels = dense.shape[2]
    return call(
        forward_body,
        [jax.ShapeDtypeStruct((tiles, VX * VY * VZ, channels), BF)],
        [adjacency, dense, low, high, weights],
        smem=(0,),
        scratch=[
            pltpu.VMEM(SHIFTS + (channels,), BF),
            pltpu.VMEM((NX, NY, NZ, channels), F32),
        ],
        flops=2 * DENSE * KOFF * channels * channels,
    )[0]


def voxel_body(
    cap_rows, adj_ref, msg_ref, grad_ref, turned_ref, dense_ref, low_ref, high_ref, back_ref,
    table_ref, feats_ref, pick_ref,
):
    regions, rows, channels = msg_ref.shape
    tiles = adj_ref.shape[0]
    segs = up_to(cap_rows, LANES) // LANES
    lowest = lax.axis_index("region") * tiles
    for r in range(regions):
        feats_ref[r * cap_rows : (r + 1) * cap_rows, :] = msg_ref[r, 0:cap_rows, :]
        tile = msg_ref[r, cap_rows : cap_rows + 16, :].astype(F32)
        for s in range(segs):
            lanes = slice(s * LANES, (s + 1) * LANES)
            table_ref[r : r + 1, lanes] = tile[s : s + 1]
            table_ref[regions + r : regions + r + 1, lanes] = tile[segs + s : segs + s + 1]
    high = table_ref[0:regions, :].astype(jnp.int32)
    low = table_ref[regions : 2 * regions, :].astype(jnp.int32)
    start = jnp.full(high.shape, -DENSE, jnp.int32)
    for t in range(tiles):
        x, y, z = corner(adj_ref, t, lowest)
        start = jnp.where(high == t + 1, (x * NY + y) * NZ + z, start)
    inside = ((low >> 5) * NY + ((low >> 3) & 3)) * NZ + (low & 7)
    spot = jnp.where(start < 0, -LANES, start + inside)
    blocks = (spot >> 7).astype(F32)
    withins = (spot & (LANES - 1)).astype(F32)
    turned = jnp.transpose(jnp.concatenate([blocks, withins], axis=0))
    lane = iota((cap_rows, LANES), 1, F32).astype(BF)
    for r in range(regions):
        block = jnp.broadcast_to(turned[0:cap_rows, r : r + 1], (cap_rows, LANES)).astype(BF)
        within = jnp.broadcast_to(
            turned[0:cap_rows, regions + r : regions + r + 1], (cap_rows, LANES)
        ).astype(BF)
        one = jnp.where(lane == within, jnp.ones_like(lane), jnp.zeros_like(lane))
        for q in range(DENSE // LANES):
            pick_ref[r * cap_rows : (r + 1) * cap_rows, q * LANES : (q + 1) * LANES] = jnp.where(
                block == jnp.asarray(q, BF), one, jnp.zeros_like(one)
            )
    total = regions * cap_rows
    flipped = jnp.transpose(feats_ref[...].astype(F32)).astype(BF)
    left = jnp.concatenate([flipped, jnp.ones((16, total), BF)], axis=0)
    width = 2 * LANES
    for q in range(0, DENSE, width):
        part = jnp.dot(left, pick_ref[:, q : q + width], preferred_element_type=F32)
        denom = jnp.maximum(part[channels : channels + 8], 1.0)
        mean = part[0:channels] / denom[0:1]
        turned_ref[:, q : q + width] = mean.astype(BF)
        upright = jnp.transpose(mean).astype(BF)
        dense_ref[q // SLAB, q % SLAB : q % SLAB + width, :] = upright
        if q == 0:
            low_ref[...] = upright
        if q == DENSE - width:
            high_ref[...] = upright
        column = jnp.transpose(denom)[:, 0:1]
        grad_ref[q // SLAB, q % SLAB : q % SLAB + width, :] = (
            grad_ref[q // SLAB, q % SLAB : q % SLAB + width, :] / column
        )
    voxel_grad = grad_ref[...].reshape(DENSE, channels).astype(BF)
    chunk = total // 4
    for start in range(0, total, chunk):
        picked = jnp.dot(
            pick_ref[start : start + chunk, :], voxel_grad, preferred_element_type=F32
        )
        for r in range(start // cap_rows, (start + chunk) // cap_rows):
            back_ref[r] = picked[r * cap_rows - start : (r + 1) * cap_rows - start].astype(BF)


def voxels(adjacency, msg, grad, cap_rows):
    regions, rows, channels = msg.shape
    segs = up_to(cap_rows, LANES) // LANES
    face = jax.ShapeDtypeStruct((SLAB, channels), BF)
    total = regions * cap_rows
    return call(
        functools.partial(voxel_body, cap_rows),
        [
            jax.ShapeDtypeStruct((channels, DENSE), BF),
            jax.ShapeDtypeStruct((NX, SLAB, channels), BF),
            face,
            face,
            jax.ShapeDtypeStruct((regions, cap_rows, channels), BF),
        ],
        [adjacency, msg, grad],
        smem=(0,),
        scratch=[
            pltpu.VMEM((2 * regions, segs * LANES), F32),
            pltpu.VMEM((total, channels), BF),
            pltpu.VMEM((total, DENSE), BF),
        ],
        flops=4 * total * DENSE * channels,
    )


def weight_body(scaling, turned_ref, shift_ref, keep_ref, send_ref, all_ref):
    channels = turned_ref.shape[0]
    half = keep_ref.shape[0]
    core = lax.rem(lax.axis_index("region"), 2)
    left = turned_ref[...]
    for k in range(0, KOFF, 2):
        pieces = []
        for j in range(k, min(k + 2, KOFF)):
            a, b, c = j // 9, j // 3 % 3, j % 3
            window = shift_ref[c, a : a + NX, b * NZ : b * NZ + SLAB, :]
            pieces.append(window.reshape(DENSE, channels))
        right = jnp.concatenate(pieces, axis=1)
        term = jnp.dot(left, right, preferred_element_type=F32) * scaling
        for i in range(len(pieces)):
            at = (KOFF - 1 - k - i) * channels
            all_ref[at : at + channels, :] = term[:, i * channels : (i + 1) * channels]
    keep_ref[...] = all_ref[pl.ds(pl.multiple_of(core * half, 8), half), :]
    send_ref[...] = all_ref[pl.ds(pl.multiple_of((1 - core) * half, 8), half), :]


def weight_terms(turned, shifts, scaling):
    channels = turned.shape[0]
    half = jax.ShapeDtypeStruct((KOFF * channels // 2, channels), F32)
    return call(
        functools.partial(weight_body, scaling),
        [half, half],
        [turned, shifts],
        scratch=[pltpu.VMEM((KOFF * channels, channels), F32)],
        flops=2 * DENSE * KOFF * channels * channels,
    )


def unpack_body(place_ref, rows_ref, out_ref):
    regions, cap_rows, channels = rows_ref.shape
    points = out_ref.shape[0]
    total = regions * cap_rows
    place = jnp.transpose(place_ref[...])[:, 0:1].astype(jnp.int32)
    block = jnp.broadcast_to((place >> 7).astype(F32), (points, LANES)).astype(BF)
    within = jnp.broadcast_to((place & (LANES - 1)).astype(F32), (points, LANES)).astype(BF)
    lane = iota((points, LANES), 1, F32).astype(BF)
    one = jnp.where(lane == within, jnp.ones_like(lane), jnp.zeros_like(lane))
    rows = rows_ref[...].reshape(total, channels)
    chunk = 256
    for start in range(0, points, chunk):
        keep = slice(start, start + chunk)
        picks = [
            jnp.where(block[keep] == jnp.asarray(q, BF), one[keep], jnp.zeros_like(one[keep]))
            for q in range(total // LANES)
        ]
        picker = jnp.concatenate(picks, axis=1)
        out_ref[keep, :] = jnp.dot(picker, rows, preferred_element_type=F32).astype(BF)


def unpack(place, rows, points):
    regions, cap_rows, channels = rows.shape
    return call(
        unpack_body,
        [jax.ShapeDtypeStruct((points, channels), BF)],
        [place, rows],
        flops=2 * regions * cap_rows * points * channels,
    )[0]


def from_sides(low, high):
    count = lax.axis_size("region")
    up = [(i, i + 1) for i in range(count - 1)]
    down = [(j, i) for i, j in up]
    return lax.ppermute(high, "region", up), lax.ppermute(low, "region", down)


def swapped(array, bit):
    count = lax.axis_size("region")
    return lax.ppermute(array, "region", [(i, i ^ bit) for i in range(count)])


def total_over_region(keep, send):
    count = lax.axis_size("region")
    me = lax.axis_index("region")
    term = keep + swapped(send, 1)
    bit = 2
    while bit < count:
        half = term.shape[0] // 2
        side = (me // bit) % 2
        sent = lax.dynamic_slice_in_dim(term, (1 - side) * half, half).astype(BF)
        kept = lax.dynamic_slice_in_dim(term, side * half, half)
        term = kept + swapped(sent, bit).astype(F32)
        bit *= 2
    term = term.astype(BF)
    while bit > 1:
        bit //= 2
        other = swapped(term, bit)
        side = (me // bit) % 2
        term = jnp.where(
            side == 0,
            jnp.concatenate([term, other], axis=0),
            jnp.concatenate([other, term], axis=0),
        )
    return term.astype(F32)


def exchange(array):
    return lax.all_to_all(array, "region", split_axis=0, concat_axis=0, tiled=True)


def local(point_feats, point_owner, point_slot, adjacency, kernel, cotangent):
    regions = lax.axis_size("region")
    points, channels = point_feats.shape
    tiles, vox = cotangent.shape[0], cotangent.shape[1]
    capacity = (5 * points + 2 * regions - 1) // (2 * regions)
    cap_rows = up_to(capacity, 16)
    msg, place = pack(
        point_owner.reshape(1, points), point_slot.reshape(1, points), point_feats, regions, cap_rows
    )
    received = exchange(msg)
    cot, cot_low, cot_high = to_dense(adjacency, cotangent)
    below, above = from_sides(cot_low, cot_high)
    mirrored = jnp.transpose(kernel[::-1], (0, 2, 1)).reshape(KOFF * channels, channels)
    grad, shifts = gradient(cot, below, above, mirrored)
    turned, feats, low, high, back = voxels(adjacency, received, grad, cap_rows)
    scaling = 1.0 / math.sqrt(tiles * regions * vox)
    keep, send = weight_terms(turned, shifts, scaling)
    grad_weight = total_over_region(keep, send).reshape(KOFF, channels, channels)
    feats_below, feats_above = from_sides(low, high)
    weights = kernel.reshape(KOFF * channels, channels)
    out_tiles = forward(adjacency, feats, feats_below, feats_above, weights, tiles)
    grad_points = unpack(place, exchange(back), points)
    return out_tiles, grad_points, grad_weight


def solution(mesh):
    placed = (
        P(("groups", "region"), None),
        P(("groups", "region"), None),
        P(("groups", "region")),
        P(("groups", "region"), None),
        P(),
        P(("groups", "region"), None, None),
    )
    return jax.shard_map(
        local,
        mesh=mesh,
        in_specs=placed,
        out_specs=(
            P(("groups", "region"), None, None),
            P(("groups", "region"), None),
            P("groups", None, None),
        ),
        check_vma=False,
    )
```

profile of v0, /device:TPU:11, one launch (start us, length us, event | category | flops | bytes accessed | tf_op | source)
XLA Modules:
  0.0 123.7 jit_solution(3308317046490373159)
XLA Ops:
  0.6 0.9 copy-done.3
  3.0 2.7 %shard_map.85 = (bf16[16,176,128]{2,1,0:T(8,128)(2,1)}, f32[8,1024]{1,0:T(8,128)S(1)}) custom-call(s32[1,1024]{1,0:T(1,128)S(1)} %bitcast.10, s32[1,1024]{1,0:T(1,128)S(1)} %bitcast.11, bf16[1024,128]{1,0:T(8,128)(2,1)S(1)} %copy-done.3), custom_call_target="tpu_custom_call" | custom-call | flops 671088640 | bytes 1024000 | tf_op jit(solution)/shard_map/pallas_call | solution.py:42
  5.6 6.6 %all-to-all-start = ((bf16[16,176,128]{2,1,0:T(8,128)(2,1)}), bf16[16,176,128]{2,1,0:T(8,128)(2,1)S(1)}, u32[]{:S(2)}, u32[]{:S(2)}) async-start(bf16[16,176,128]{2,1,0:T(8,128)(2,1)} %get-tuple-element.17), calls=%async_computation | async-start | bytes 1441792 | tf_op jit(solution)/shard_map/all_to_all | solution.py:439
  12.2 0.9 shard_map.86
  13.1 3.3 %collective-permute-start = (bf16[256,128]{1,0:T(8,128)(2,1)S(1)}, bf16[256,128]{1,0:T(8,128)(2,1)S(1)}, u32[]{:S(2)}, u32[]{:S(2)}) collective-permute-start(bf16[256,128]{1,0:T(8,128)(2,1)S(1)} %get-tuple-element.19), channel_id=1, source_target_pairs={{0,1},{1,2},{2,3},{3,4},{4,5},{5,6},{6,7},{7,8},{8,9},{9,10},{10,1... | collective-permute-start | bytes 196616 | tf_op jit(solution)/shard_map/ppermute | solution.py:405
  16.4 1.9 %collective-permute-start.1 = (bf16[256,128]{1,0:T(8,128)(2,1)S(1)}, bf16[256,128]{1,0:T(8,128)(2,1)S(1)}, u32[]{:S(2)}, u32[]{:S(2)}) collective-permute-start(bf16[256,128]{1,0:T(8,128)(2,1)S(1)} %get-tuple-element.20), channel_id=1, source_target_pairs={{1,0},{2,1},{3,2},{4,3},{5,4},{6,5},{7,6},{8,7},{9,8},{10,9},{11,1... | collective-permute-start | bytes 196616 | tf_op jit(solution)/shard_map/ppermute | solution.py:405
  18.4 1.0 reverse_bitcast_fusion
  19.4 1.9 %copy.9 = bf16[27,128,128]{2,1,0:T(8,128)(2,1)S(1)} copy(bf16[27,128,128]{1,2,0:T(8,128)(2,1)} %reverse_bitcast_fusion) | data formatting | bytes 1769472 | tf_op jit(solution)/shard_map/transpose | solution.py:454
  21.2 7.9 %collective-permute-done.low_ref = bf16[256,128]{1,0:T(8,128)(2,1)S(1)} collective-permute-done((bf16[256,128]{1,0:T(8,128)(2,1)S(1)}, bf16[256,128]{1,0:T(8,128)(2,1)S(1)}, u32[]{:S(2)}, u32[]{:S(2)}) %collective-permute-start) | collective-permute-done | bytes 65568 | tf_op jit(solution)/shard_map/ppermute | solution.py:405
  29.1 1.6 %collective-permute-done.1.high_ref = bf16[256,128]{1,0:T(8,128)(2,1)S(1)} collective-permute-done((bf16[256,128]{1,0:T(8,128)(2,1)S(1)}, bf16[256,128]{1,0:T(8,128)(2,1)S(1)}, u32[]{:S(2)}, u32[]{:S(2)}) %collective-permute-start.1) | collective-permute-done | bytes 65568 | tf_op jit(solution)/shard_map/ppermute | solution.py:405
  30.7 5.4 %shard_map.87 = (f32[8,256,128]{2,1,0:T(8,128)S(1)}, bf16[3,10,288,128]{3,2,1,0:T(8,128)(2,1)S(1)}) custom-call(bf16[8,256,128]{2,1,0:T(8,128)(2,1)S(1)} %get-tuple-element.18.dense_ref, bf16[256,128]{1,0:T(8,128)(2,1)S(1)} %collective-permute-done.low_ref, bf16[256,128]{1,0:T(8,128)(2,1)S(1)} %collective-permute-done.1.high_ref, bf16[3456,128]{1,0:T(8,128)(2,1)S(1)} %bitcast.9), custom_call_target="tpu_custom_call" | custom-call | flops 1811939328 | bytes 4800512 | tf_op jit(solution)/shard_map/pallas_call | solution.py:42
  36.2 1.4 %copy-done.6 = bf16[3,10,288,128]{3,2,1,0:T(8,128)(2,1)} copy-done((bf16[3,10,288,128]{3,2,1,0:T(8,128)(2,1)}, bf16[3,10,288,128]{3,2,1,0:T(8,128)(2,1)S(1)}, u32[]{:S(2)}) %copy-start.6) | copy-done | bytes 2211864
  37.6 1.0 copy-done.8
  38.6 1.2 copy-done.9
  39.8 8.2 %shard_map.88 = (bf16[128,2048]{1,0:T(8,128)(2,1)S(1)}, bf16[8,256,128]{2,1,0:T(8,128)(2,1)S(1)}, bf16[256,128]{1,0:T(8,128)(2,1)S(1)}, bf16[256,128]{1,0:T(8,128)(2,1)S(1)}, bf16[16,160,128]{2,1,0:T(8,128)(2,1)}) custom-call(s32[16,27]{1,0:T(8,128)S(1)} %copy-done.2, bf16[16,176,128]{2,1,0:T(8,128)(2,1)S(1)} %all-to-all-done.msg_ref, ...), custom_call_target="tpu_custom_call" | custom-call | flops 2684354560 | bytes 3606208 | tf_op jit(solution)/shard_map/pallas_call | solution.py:42
  48.0 0.8 copy-done.10
  48.8 2.5 %shard_map.91 = (f32[1728,128]{1,0:T(8,128)S(1)}, f32[1728,128]{1,0:T(8,128)S(1)}) custom-call(bf16[128,2048]{1,0:T(8,128)(2,1)S(1)} %get-tuple-element.27.turned_ref, bf16[3,10,288,128]{3,2,1,0:T(8,128)(2,1)S(1)} %copy-done.7), custom_call_target="tpu_custom_call" | custom-call | flops 1811939328 | bytes 4505600 | tf_op jit(solution)/shard_map/pallas_call | solution.py:42
  51.4 2.5 %collective-permute-done.4 = f32[1728,128]{1,0:T(8,128)} collective-permute-done((f32[1728,128]{1,0:T(8,128)S(1)}, f32[1728,128]{1,0:T(8,128)}, u32[]{:S(2)}, u32[]{:S(2)}) %collective-permute-start.4) | collective-permute-done | bytes 884768 | tf_op jit(solution)/shard_map/ppermute | solution.py:410
  53.9 1.3 %add.54 = f32[1728,128]{1,0:T(8,128)S(1)} add(f32[1728,128]{1,0:T(8,128)S(1)} %get-tuple-element.29, f32[1728,128]{1,0:T(8,128)} %collective-permute-done.4) | non-fusion elementwise | flops 221184 | bytes 2654208 | tf_op jit(solution)/shard_map/add | solution.py:416
  55.4 6.8 %collective-permute-done.5 = bf16[864,128]{1,0:T(8,128)(2,1)S(1)} collective-permute-done((bf16[864,128]{1,0:T(8,128)(2,1)S(1)}, bf16[864,128]{1,0:T(8,128)(2,1)S(1)}, u32[]{:S(2)}, u32[]{:S(2)}) %collective-permute-start.5) | collective-permute-done | bytes 221216 | tf_op jit(solution)/shard_map/ppermute | solution.py:410
  62.5 3.5 %collective-permute-done.6 = bf16[432,128]{1,0:T(8,128)(2,1)S(1)} collective-permute-done((bf16[432,128]{1,0:T(8,128)(2,1)S(1)}, bf16[432,128]{1,0:T(8,128)(2,1)S(1)}, u32[]{:S(2)}, u32[]{:S(2)}) %collective-permute-start.6) | collective-permute-done | bytes 110624 | tf_op jit(solution)/shard_map/ppermute | solution.py:410
  66.6 3.4 %collective-permute-done.7 = bf16[216,128]{1,0:T(8,128)(2,1)S(1)} collective-permute-done((bf16[216,128]{1,0:T(8,128)(2,1)S(1)}, bf16[216,128]{1,0:T(8,128)(2,1)S(1)}, u32[]{:S(2)}, u32[]{:S(2)}) %collective-permute-start.7) | collective-permute-done | bytes 55328 | tf_op jit(solution)/shard_map/ppermute | solution.py:410
  70.6 9.1 %all-to-all-start.1 = ((bf16[16,160,128]{2,1,0:T(8,128)(2,1)}), bf16[16,160,128]{2,1,0:T(8,128)(2,1)S(1)}, u32[]{:S(2)}, u32[]{:S(2)}) async-start(bf16[16,160,128]{2,1,0:T(8,128)(2,1)} %get-tuple-element.26), calls=%async_computation.1 | async-start | bytes 1310720 | tf_op jit(solution)/shard_map/all_to_all | solution.py:439
  80.1 13.8 %collective-permute-done.9 = bf16[432,128]{1,0:T(8,128)(2,1)S(1)} collective-permute-done((bf16[432,128]{1,0:T(8,128)(2,1)S(1)}, bf16[432,128]{1,0:T(8,128)(2,1)S(1)}, u32[]{:S(2)}, u32[]{:S(2)}) %collective-permute-start.9) | collective-permute-done | bytes 110624 | tf_op jit(solution)/shard_map/ppermute | solution.py:410
  94.2 5.9 %collective-permute-done.10 = bf16[864,128]{1,0:T(8,128)(2,1)S(1)} collective-permute-done((bf16[864,128]{1,0:T(8,128)(2,1)S(1)}, bf16[864,128]{1,0:T(8,128)(2,1)S(1)}, u32[]{:S(2)}, u32[]{:S(2)}) %collective-permute-start.10) | collective-permute-done | bytes 221216 | tf_op jit(solution)/shard_map/ppermute | solution.py:410
  100.2 1.8 %collective-permute-start.11 = (bf16[1728,128]{1,0:T(8,128)(2,1)S(1)}, bf16[1728,128]{1,0:T(8,128)(2,1)S(1)}, u32[]{:S(2)}, u32[]{:S(2)}) collective-permute-start(bf16[1728,128]{1,0:T(8,128)(2,1)S(1)} %maximum_select_fusion.1), channel_id=1, source_target_pairs={{0,1},{1,0},{2,3},{3,2},{4,5},{5,4},{6,7},{7,6},{8,9},{9,8},{10,11... | collective-permute-start | bytes 1327112 | tf_op jit(solution)/shard_map/ppermute | solution.py:410
  102.0 4.0 %collective-permute-start.2 = (bf16[256,128]{1,0:T(8,128)(2,1)S(1)}, bf16[256,128]{1,0:T(8,128)(2,1)S(1)}, u32[]{:S(2)}, u32[]{:S(2)}) collective-permute-start(bf16[256,128]{1,0:T(8,128)(2,1)S(1)} %get-tuple-element.23), channel_id=1, source_target_pairs={{0,1},{1,2},{2,3},{3,4},{4,5},{5,6},{6,7},{7,8},{8,9},{9,10},{10,1... | collective-permute-start | bytes 196616 | tf_op jit(solution)/shard_map/ppermute | solution.py:405
  106.1 1.9 %collective-permute-start.3 = (bf16[256,128]{1,0:T(8,128)(2,1)S(1)}, bf16[256,128]{1,0:T(8,128)(2,1)S(1)}, u32[]{:S(2)}, u32[]{:S(2)}) collective-permute-start(bf16[256,128]{1,0:T(8,128)(2,1)S(1)} %get-tuple-element.24), channel_id=1, source_target_pairs={{1,0},{2,1},{3,2},{4,3},{5,4},{6,5},{7,6},{8,7},{9,8},{10,9},{11,1... | collective-permute-start | bytes 196616 | tf_op jit(solution)/shard_map/ppermute | solution.py:405
  108.0 4.5 %collective-permute-done.3.high_ref = bf16[256,128]{1,0:T(8,128)(2,1)S(1)} collective-permute-done((bf16[256,128]{1,0:T(8,128)(2,1)S(1)}, bf16[256,128]{1,0:T(8,128)(2,1)S(1)}, u32[]{:S(2)}, u32[]{:S(2)}) %collective-permute-start.3) | collective-permute-done | bytes 65568 | tf_op jit(solution)/shard_map/ppermute | solution.py:405
  112.6 7.0 %shard_map.89 = bf16[16,128,128]{2,1,0:T(8,128)(2,1)} custom-call(s32[16,27]{1,0:T(8,128)S(1)} %copy-done.2, bf16[8,256,128]{2,1,0:T(8,128)(2,1)S(1)} %copy-done.11, bf16[256,128]{1,0:T(8,128)(2,1)S(1)} %collective-permute-done.2.low_ref, bf16[256,128]{1,0:T(8,128)(2,1)S(1)} %collective-permute-done.3.high_ref, bf16[3456,128]{1,0:T(8,128)(2,1)S(1)} %bitcast.8), custom_call_target="tpu_custom_call" | custom-call | flops 1811939328 | bytes 2066112 | tf_op jit(solution)/shard_map/pallas_call | solution.py:42
  119.6 2.4 %shard_map.90 = bf16[1024,128]{1,0:T(8,128)(2,1)} custom-call(f32[8,1024]{1,0:T(8,128)S(1)} %get-tuple-element.25.place_ref, bf16[16,160,128]{2,1,0:T(8,128)(2,1)S(1)} %all-to-all-done.1.rows_ref), custom_call_target="tpu_custom_call" | custom-call | flops 671088640 | bytes 950272 | tf_op jit(solution)/shard_map/pallas_call | solution.py:42
  122.3 1.4 %convert.1 = f32[27,128,128]{2,1,0:T(8,128)} convert(bf16[27,128,128]{2,1,0:T(8,128)(2,1)S(1)} %bitcast.12) | non-fusion elementwise | flops 442368 | bytes 2654208 | tf_op jit(solution)/shard_map/convert_element_type | solution.py:435
  (41 shorter events, 4.0 us)
Async XLA Ops:
  0.6 1.0 copy-start.3
  1.6 0.7 copy-start.4
  2.3 0.7 copy-start.5
  3.0 9.2 %copy-start.1 = (bf16[16,128,128]{2,1,0:T(8,128)(2,1)S(1)}, bf16[16,128,128]{2,1,0:T(8,128)(2,1)}, u32[]{:S(2)}) copy-start(bf16[16,128,128]{2,1,0:T(8,128)(2,1)} %bricks_ref.1) | copy-start | bytes 1572868
  3.0 9.3 %copy-start.2 = (s32[16,27]{1,0:T(8,128)S(1)}, s32[16,27]{1,0:T(8,128)}, u32[]{:S(2)}) copy-start(s32[16,27]{1,0:T(8,128)} %adj_ref.5) | copy-start | bytes 5188
  3.0 15.4 %copy-start = (bf16[27,128,128]{2,1,0:T(8,128)(2,1)S(1)}, bf16[27,128,128]{2,1,0:T(8,128)(2,1)}, u32[]{:S(2)}) copy-start(bf16[27,128,128]{2,1,0:T(8,128)(2,1)} %param.10) | copy-start | bytes 2654212
  5.6 32.9 %all-to-all-start = ((bf16[16,176,128]{2,1,0:T(8,128)(2,1)}), bf16[16,176,128]{2,1,0:T(8,128)(2,1)S(1)}, u32[]{:S(2)}, u32[]{:S(2)}) async-start(bf16[16,176,128]{2,1,0:T(8,128)(2,1)} %get-tuple-element.17), calls=%async_computation | async-start | bytes 1441792 | tf_op jit(solution)/shard_map/all_to_all | solution.py:439
  13.1 16.0 %collective-permute-start = (bf16[256,128]{1,0:T(8,128)(2,1)S(1)}, bf16[256,128]{1,0:T(8,128)(2,1)S(1)}, u32[]{:S(2)}, u32[]{:S(2)}) collective-permute-start(bf16[256,128]{1,0:T(8,128)(2,1)S(1)} %get-tuple-element.19), channel_id=1, source_target_pairs={{0,1},{1,2},{2,3},{3,4},{4,5},{5,6},{6,7},{7,8},{8,9},{9,10},{10,1... | collective-permute-start | bytes 196616 | tf_op jit(solution)/shard_map/ppermute | solution.py:405
  16.4 14.3 %collective-permute-start.1 = (bf16[256,128]{1,0:T(8,128)(2,1)S(1)}, bf16[256,128]{1,0:T(8,128)(2,1)S(1)}, u32[]{:S(2)}, u32[]{:S(2)}) collective-permute-start(bf16[256,128]{1,0:T(8,128)(2,1)S(1)} %get-tuple-element.20), channel_id=1, source_target_pairs={{1,0},{2,1},{3,2},{4,3},{5,4},{6,5},{7,6},{8,7},{9,8},{10,9},{11,1... | collective-permute-start | bytes 196616 | tf_op jit(solution)/shard_map/ppermute | solution.py:405
  36.2 1.4 %copy-start.6 = (bf16[3,10,288,128]{3,2,1,0:T(8,128)(2,1)}, bf16[3,10,288,128]{3,2,1,0:T(8,128)(2,1)S(1)}, u32[]{:S(2)}) copy-start(bf16[3,10,288,128]{3,2,1,0:T(8,128)(2,1)S(1)} %get-tuple-element.28.shift_ref) | copy-start | bytes 6635524
  37.6 1.0 copy-start.8
  38.6 1.2 copy-start.9
  39.8 9.0 %copy-start.7 = (bf16[3,10,288,128]{3,2,1,0:T(8,128)(2,1)S(1)}, bf16[3,10,288,128]{3,2,1,0:T(8,128)(2,1)}, u32[]{:S(2)}) copy-start(bf16[3,10,288,128]{3,2,1,0:T(8,128)(2,1)} %copy-done.6) | copy-start | bytes 6635524
  48.0 0.8 copy-start.10
  51.3 2.6 %collective-permute-start.4 = (f32[1728,128]{1,0:T(8,128)S(1)}, f32[1728,128]{1,0:T(8,128)}, u32[]{:S(2)}, u32[]{:S(2)}) collective-permute-start(f32[1728,128]{1,0:T(8,128)S(1)} %get-tuple-element.30), channel_id=1, source_target_pairs={{0,1},{1,0},{2,3},{3,2},{4,5},{5,4},{6,7},{7,6},{8,9},{9,8},{10,11... | collective-permute-start | bytes 2654216 | tf_op jit(solution)/shard_map/ppermute | solution.py:410
  55.3 7.0 %collective-permute-start.5 = (bf16[864,128]{1,0:T(8,128)(2,1)S(1)}, bf16[864,128]{1,0:T(8,128)(2,1)S(1)}, u32[]{:S(2)}, u32[]{:S(2)}) collective-permute-start(bf16[864,128]{1,0:T(8,128)(2,1)S(1)} %dynamic-slice_convert_fusion), channel_id=1, source_target_pairs={{0,2},{1,3},{2,0},{3,1},{4,6},{5,7},{6,4},{7,5},{8,10},{9,11},{10,... | collective-permute-start | bytes 663560 | tf_op jit(solution)/shard_map/ppermute | solution.py:410
  62.3 3.7 %collective-permute-start.6 = (bf16[432,128]{1,0:T(8,128)(2,1)S(1)}, bf16[432,128]{1,0:T(8,128)(2,1)S(1)}, u32[]{:S(2)}, u32[]{:S(2)}) collective-permute-start(bf16[432,128]{1,0:T(8,128)(2,1)S(1)} %dynamic-slice_convert_fusion.1), channel_id=1, source_target_pairs={{0,4},{1,5},{2,6},{3,7},{4,0},{5,1},{6,2},{7,3},{8,12},{9,13},{10,... | collective-permute-start | bytes 331784 | tf_op jit(solution)/shard_map/ppermute | solution.py:410
  62.4 50.1 %copy-start.11 = (bf16[8,256,128]{2,1,0:T(8,128)(2,1)S(1)}, bf16[8,256,128]{2,1,0:T(8,128)(2,1)}, u32[]{:S(2)}) copy-start(bf16[8,256,128]{2,1,0:T(8,128)(2,1)} %copy-done.10) | copy-start | bytes 1572868
  66.0 4.0 %collective-permute-start.7 = (bf16[216,128]{1,0:T(8,128)(2,1)S(1)}, bf16[216,128]{1,0:T(8,128)(2,1)S(1)}, u32[]{:S(2)}, u32[]{:S(2)}) collective-permute-start(bf16[216,128]{1,0:T(8,128)(2,1)S(1)} %dynamic-slice_convert_fusion.2), channel_id=1, source_target_pairs={{0,8},{1,9},{2,10},{3,11},{4,12},{5,13},{6,14},{7,15},{8,0},{9,1},... | collective-permute-start | bytes 165896 | tf_op jit(solution)/shard_map/ppermute | solution.py:410
  70.0 9.7 %collective-permute-start.8 = (bf16[216,128]{1,0:T(8,128)(2,1)S(1)}, bf16[216,128]{1,0:T(8,128)(2,1)S(1)}, u32[]{:S(2)}, u32[]{:S(2)}) collective-permute-start(bf16[216,128]{1,0:T(8,128)(2,1)S(1)} %add_convert_fusion), channel_id=1, source_target_pairs={{0,8},{1,9},{2,10},{3,11},{4,12},{5,13},{6,14},{7,15},{8,0},{9,1},... | collective-permute-start | bytes 165896 | tf_op jit(solution)/shard_map/ppermute | solution.py:410
  70.6 49.0 %all-to-all-start.1 = ((bf16[16,160,128]{2,1,0:T(8,128)(2,1)}), bf16[16,160,128]{2,1,0:T(8,128)(2,1)S(1)}, u32[]{:S(2)}, u32[]{:S(2)}) async-start(bf16[16,160,128]{2,1,0:T(8,128)(2,1)} %get-tuple-element.26), calls=%async_computation.1 | async-start | bytes 1310720 | tf_op jit(solution)/shard_map/all_to_all | solution.py:439
  79.7 14.1 %collective-permute-start.9 = (bf16[432,128]{1,0:T(8,128)(2,1)S(1)}, bf16[432,128]{1,0:T(8,128)(2,1)S(1)}, u32[]{:S(2)}, u32[]{:S(2)}) collective-permute-start(bf16[432,128]{1,0:T(8,128)(2,1)S(1)} %maximum_select_fusion.3), channel_id=1, source_target_pairs={{0,4},{1,5},{2,6},{3,7},{4,0},{5,1},{6,2},{7,3},{8,12},{9,13},{10,... | collective-permute-start | bytes 331784 | tf_op jit(solution)/shard_map/ppermute | solution.py:410
  94.0 6.1 %collective-permute-start.10 = (bf16[864,128]{1,0:T(8,128)(2,1)S(1)}, bf16[864,128]{1,0:T(8,128)(2,1)S(1)}, u32[]{:S(2)}, u32[]{:S(2)}) collective-permute-start(bf16[864,128]{1,0:T(8,128)(2,1)S(1)} %maximum_select_fusion.2), channel_id=1, source_target_pairs={{0,2},{1,3},{2,0},{3,1},{4,6},{5,7},{6,4},{7,5},{8,10},{9,11},{10,... | collective-permute-start | bytes 663560 | tf_op jit(solution)/shard_map/ppermute | solution.py:410
  100.2 21.9 %collective-permute-start.11 = (bf16[1728,128]{1,0:T(8,128)(2,1)S(1)}, bf16[1728,128]{1,0:T(8,128)(2,1)S(1)}, u32[]{:S(2)}, u32[]{:S(2)}) collective-permute-start(bf16[1728,128]{1,0:T(8,128)(2,1)S(1)} %maximum_select_fusion.1), channel_id=1, source_target_pairs={{0,1},{1,0},{2,3},{3,2},{4,5},{5,4},{6,7},{7,6},{8,9},{9,8},{10,11... | collective-permute-start | bytes 1327112 | tf_op jit(solution)/shard_map/ppermute | solution.py:410
  102.0 6.0 %collective-permute-start.2 = (bf16[256,128]{1,0:T(8,128)(2,1)S(1)}, bf16[256,128]{1,0:T(8,128)(2,1)S(1)}, u32[]{:S(2)}, u32[]{:S(2)}) collective-permute-start(bf16[256,128]{1,0:T(8,128)(2,1)S(1)} %get-tuple-element.23), channel_id=1, source_target_pairs={{0,1},{1,2},{2,3},{3,4},{4,5},{5,6},{6,7},{7,8},{8,9},{9,10},{10,1... | collective-permute-start | bytes 196616 | tf_op jit(solution)/shard_map/ppermute | solution.py:405
  106.1 6.5 %collective-permute-start.3 = (bf16[256,128]{1,0:T(8,128)(2,1)S(1)}, bf16[256,128]{1,0:T(8,128)(2,1)S(1)}, u32[]{:S(2)}, u32[]{:S(2)}) collective-permute-start(bf16[256,128]{1,0:T(8,128)(2,1)S(1)} %get-tuple-element.24), channel_id=1, source_target_pairs={{1,0},{2,1},{3,2},{4,3},{5,4},{6,5},{7,6},{8,7},{9,8},{10,9},{11,1... | collective-permute-start | bytes 196616 | tf_op jit(solution)/shard_map/ppermute | solution.py:405
where the time goes:
time: 124 us
  waiting for transfers between devices  50 us (40%)
  starting transfers between devices  30.7 us (25%)
  Pallas kernels  29.2 us (24%)
  local copies, waits for them, and re-layouts  9.63 us (8%)
  other arithmetic  3.26 us (3%)
    ppermute x8, waiting for transfers between devices, swapped(): return lax.ppermute(array, 'region', [(i, i ^ bit) for i in range(count)])  35.9 us
    pallas_call x7, Pallas kernels, call(): pl.pallas_call(body, out_shape=outs, in_specs=[SMEM if i in smem else VME...  29.2 us
    all_to_all x2, starting transfers between devices, exchange(): lax.all_to_all(array, 'region', split_axis=0, concat_axis=0, tiled=True)  15.6 us
    ppermute x4, waiting for transfers between devices, from_sides(): return (lax.ppermute(high, 'region', up), lax.ppermute(low, 'region', down))  14 us
    ppermute x4, starting transfers between devices, from_sides(): return (lax.ppermute(high, 'region', up), lax.ppermute(low, 'region', down))  11.2 us
    unnamed x24, local copies, waits for them, and re-layouts  6.71 us
    ppermute x8, starting transfers between devices, swapped(): return lax.ppermute(array, 'region', [(i, i ^ bit) for i in range(count)])  3.82 us
    transpose x2, local copies, waits for them, and re-layouts, local(): jnp.transpose(kernel[::-1], (0, 2, 1)).reshape(KOFF * channels, channels)  2.85 us
  transfers between devices with their start and end apart: 14, of which 9 were waited for; matrix products, arithmetic and copies ran while one was open for 2% of the time, Pallas kernels for 13%

commit v1 on v0

--- a/solution.py
+++ b/solution.py
@@ -25,7 +25,8 @@
 F32 = jnp.float32
 VMEM = pl.BlockSpec(memory_space=pltpu.VMEM)
 SMEM = pl.BlockSpec(memory_space=pltpu.SMEM)
-PARAMS = pltpu.CompilerParams(vmem_limit_bytes=48 * 1024 * 1024)
+FAR = pl.BlockSpec(memory_space=pltpu.HBM)
+MIB = 1024 * 1024
 
 
 def up_to(value, unit):
@@ -36,16 +37,16 @@
     return lax.broadcasted_iota(jnp.int32, shape, dim).astype(dtype)
 
 
-def call(body, outs, args, smem=(), scratch=(), flops=0):
+def call(body, outs, args, smem=(), far=(), far_outs=(), scratch=(), flops=0, limit=16):
     moved = sum(math.prod(o.shape) * o.dtype.itemsize for o in outs)
     moved += sum(math.prod(a.shape) * a.dtype.itemsize for a in args)
     return pl.pallas_call(
         body,
         out_shape=outs,
-        in_specs=[SMEM if i in smem else VMEM for i in range(len(args))],
-        out_specs=[VMEM] * len(outs),
+        in_specs=[SMEM if i in smem else FAR if i in far else VMEM for i in range(len(args))],
+        out_specs=[FAR if i in far_outs else VMEM for i in range(len(outs))],
         scratch_shapes=list(scratch),
-        compiler_params=PARAMS,
+        compiler_params=pltpu.CompilerParams(vmem_limit_bytes=limit * MIB),
         cost_estimate=pl.CostEstimate(flops=flops, bytes_accessed=moved, transcendentals=0),
     )(*args)
 
@@ -62,9 +63,17 @@
     return layer * VX, across * VY, height * VZ
 
 
-def pack_body(cap_rows, owner_ref, slot_ref, feats_ref, msg_ref, place_ref, table_ref):
+def pack_body(
+    cap_rows, owner_far, slot_far, feats_far, msg_ref, place_ref, table_ref, owner_ref, slot_ref, feats_ref, sems
+):
     regions = msg_ref.shape[0]
     points = feats_ref.shape[0]
+    pairs = ((owner_far, owner_ref), (slot_far, slot_ref), (feats_far, feats_ref))
+    copies = [pltpu.make_async_copy(a, b, sems.at[i]) for i, (a, b) in enumerate(pairs)]
+    for copy in copies:
+        copy.start()
+    copies[0].wait()
+    copies[1].wait()
     segs = up_to(cap_rows, LANES) // LANES
     owner = owner_ref[...]
     slot = slot_ref[...]
@@ -86,6 +95,7 @@
     within = jnp.broadcast_to((place & (LANES - 1)).astype(F32), (LANES, points)).astype(BF)
     row = iota((LANES, points), 0, F32).astype(BF)
     one = jnp.where(row == within, jnp.ones_like(row), jnp.zeros_like(row))
+    copies[2].wait()
     feats = feats_ref[...]
     chunk = math.lcm(cap_rows, LANES)
     for start in range(0, regions * cap_rows, chunk):
@@ -124,7 +134,15 @@
             jax.ShapeDtypeStruct((8, points), F32),
         ],
         [owner, slot, feats],
-        scratch=[pltpu.VMEM((2 * regions, segs * LANES), F32)],
+        far=(0, 1, 2),
+        scratch=[
+            pltpu.VMEM((2 * regions, segs * LANES), F32),
+            pltpu.VMEM((1, points), jnp.int32),
+            pltpu.VMEM((1, points), jnp.int32),
+            pltpu.VMEM((points, channels), BF),
+            pltpu.SemaphoreType.DMA((3,)),
+        ],
+        limit=60,
         flops=2 * regions * cap_rows * points * channels,
     )
 
@@ -157,24 +175,20 @@
     )
 
 
-def fill_shifts(shift_ref, dense_ref, low_ref, high_ref):
-    channels = dense_ref.shape[2]
-    border = jnp.zeros((NZ, channels), BF)
-    height = iota((SLAB, channels), 0) % NZ
-    for x in range(NX + 2):
-        if x == 0:
-            slab = low_ref[...]
-        elif x == NX + 1:
-            slab = high_ref[...]
-        else:
-            slab = dense_ref[x - 1]
-        wide = slab.astype(F32)
-        lower = jnp.where(height == 0, 0.0, pltpu.roll(wide, 1, 0))
-        upper = jnp.where(height == NZ - 1, 0.0, pltpu.roll(wide, SLAB - 1, 0))
-        for c, copy in enumerate((lower.astype(BF), slab, upper.astype(BF))):
-            shift_ref[c, x, 0:NZ, :] = border
-            shift_ref[c, x, NZ : NZ + SLAB, :] = copy
-            shift_ref[c, x, NZ + SLAB : NZ + SLAB + NZ, :] = border
+SHIFTED = SLAB + 2 * NZ
+INNER = NX - 2
+
+
+def put_shifts(shift_ref, x, slab):
+    border = jnp.zeros((NZ, slab.shape[1]), BF)
+    height = iota(slab.shape, 0) % NZ
+    wide = slab.astype(F32)
+    lower = jnp.where(height == 0, 0.0, pltpu.roll(wide, 1, 0))
+    upper = jnp.where(height == NZ - 1, 0.0, pltpu.roll(wide, SLAB - 1, 0))
+    for c, copy in enumerate((lower.astype(BF), slab, upper.astype(BF))):
+        shift_ref[c, x, 0:NZ, :] = border
+        shift_ref[c, x, NZ : NZ + SLAB, :] = copy
+        shift_ref[c, x, NZ + SLAB : SHIFTED, :] = border
 
 
 def conv_slab(shift_ref, weights_ref, x):
@@ -187,73 +201,172 @@
     )
 
 
-SHIFTS = (3, NX + 2, SLAB + 2 * NZ)
-
-
-def gradient_body(dense_ref, low_ref, high_ref, weights_ref, grad_ref, shift_ref):
-    fill_shifts(shift_ref, dense_ref, low_ref, high_ref)
-
+def conv_inner(shift_ref, weights_ref, store):
     def step(x, carry):
-        grad_ref[x] = conv_slab(shift_ref, weights_ref, x)
+        store(x, conv_slab(shift_ref, weights_ref, x))
         return carry
 
-    lax.fori_loop(0, NX, step, 0)
-
-
-def gradient(dense, low, high, weights):
+    lax.fori_loop(0, INNER, step, 0)
+
+
+def conv_edges(shift_ref, weights_ref, slabs):
+    for i, slab in enumerate(slabs):
+        put_shifts(shift_ref, i, slab)
+    return conv_slab(shift_ref, weights_ref, 0), conv_slab(shift_ref, weights_ref, 3)
+
+
+def inner_gradient_body(dense_ref, weights_ref, grad_far, shift_far, grad_ref, shift_ref, sems):
+    for x in range(NX):
+        put_shifts(shift_ref, x, dense_ref[x])
+    shift_out = pltpu.make_async_copy(shift_ref, shift_far, sems.at[0])
+    shift_out.start()
+
+    def store(x, value):
+        grad_ref[x] = value
+
+    conv_inner(shift_ref, weights_ref, store)
+    grad_out = pltpu.make_async_copy(grad_ref, grad_far, sems.at[1])
+    grad_out.start()
+    shift_out.wait()
+    grad_out.wait()
+
+
+def inner_gradient(dense, weights):
     channels = dense.shape[2]
-    return call(
-        gradient_body,
+    grads, shifts = (INNER, SLAB, channels), (3, NX, SHIFTED, channels)
+    return call(
+        inner_gradient_body,
+        [jax.ShapeDtypeStruct(grads, F32), jax.ShapeDtypeStruct(shifts, BF)],
+        [dense, weights],
+        far_outs=(0, 1),
+        scratch=[
+            pltpu.VMEM(grads, F32),
+            pltpu.VMEM(shifts, BF),
+            pltpu.SemaphoreType.DMA((2,)),
+        ],
+        flops=2 * INNER * SLAB * KOFF * channels * channels,
+        limit=60,
+    )
+
+
+def edge_gradient_body(dense_ref, low_ref, high_ref, weights_ref, grad_ref, edge_ref, shift_ref):
+    slabs = [low_ref[...]] + [dense_ref[x] for x in (0, 1, NX - 2, NX - 1)] + [high_ref[...]]
+    first, last = conv_edges(shift_ref, weights_ref, slabs)
+    grad_ref[0] = first
+    grad_ref[1] = last
+    edge_ref[0] = shift_ref[:, 0]
+    edge_ref[1] = shift_ref[:, 5]
+
+
+def edge_gradient(dense, low, high, weights):
+    channels = dense.shape[2]
+    return call(
+        edge_gradient_body,
         [
-            jax.ShapeDtypeStruct((NX, SLAB, channels), F32),
-            jax.ShapeDtypeStruct(SHIFTS + (channels,), BF),
+            jax.ShapeDtypeStruct((2, SLAB, channels), F32),
+            jax.ShapeDtypeStruct((2, 3, SHIFTED, channels), BF),
         ],
         [dense, low, high, weights],
-        flops=2 * DENSE * KOFF * channels * channels,
-    )
-
-
-def forward_body(adj_ref, dense_ref, low_ref, high_ref, weights_ref, out_ref, shift_ref, grid_ref):
+        scratch=[pltpu.VMEM((3, 6, SHIFTED, channels), BF)],
+        flops=4 * SLAB * KOFF * channels * channels,
+    )
+
+
+def upright(turned):
+    return jnp.transpose(turned.astype(F32)).astype(BF)
+
+
+def inner_forward_body(turned_far, weights_far, out_ref, shift_ref, turned_ref, weights_ref, sems):
+    turned_in = pltpu.make_async_copy(turned_far, turned_ref, sems.at[0])
+    weights_in = pltpu.make_async_copy(weights_far, weights_ref, sems.at[1])
+    turned_in.start()
+    weights_in.start()
+    turned_in.wait()
+    for x in range(NX):
+        put_shifts(shift_ref, x, upright(turned_ref[:, x * SLAB : (x + 1) * SLAB]))
+    weights_in.wait()
+
+    def store(x, value):
+        out_ref[x] = value.astype(BF)
+
+    conv_inner(shift_ref, weights_ref, store)
+
+
+def inner_forward(turned, weights):
+    channels = turned.shape[0]
+    return call(
+        inner_forward_body,
+        [jax.ShapeDtypeStruct((INNER, SLAB, channels), BF)],
+        [turned, weights],
+        far=(0, 1),
+        scratch=[
+            pltpu.VMEM((3, NX, SHIFTED, channels), BF),
+            pltpu.VMEM(turned.shape, BF),
+            pltpu.VMEM(weights.shape, BF),
+            pltpu.SemaphoreType.DMA((2,)),
+        ],
+        flops=2 * INNER * SLAB * KOFF * channels * channels,
+        limit=58,
+    )[0]
+
+
+def edge_forward_body(
+    adj_ref, turned_far, low_ref, high_ref, weights_far, inner_far, out_ref,
+    shift_ref, grid_ref, turned_ref, weights_ref, inner_ref, sems,
+):
+    ends = ((0, 2 * SLAB), (DENSE - 2 * SLAB, DENSE))
+    copies = [
+        pltpu.make_async_copy(turned_far.at[:, a:b], turned_ref.at[i], sems.at[i])
+        for i, (a, b) in enumerate(ends)
+    ]
+    copies.append(pltpu.make_async_copy(weights_far, weights_ref, sems.at[2]))
+    copies.append(pltpu.make_async_copy(inner_far, inner_ref, sems.at[3]))
+    for copy in copies:
+        copy.start()
     tiles, vox, channels = out_ref.shape
     lowest = lax.axis_index("region") * tiles
-    fill_shifts(shift_ref, dense_ref, low_ref, high_ref)
-
-    def step(x, carry):
-        grid_ref[x] = conv_slab(shift_ref, weights_ref, x).reshape(NY, NZ, channels)
-        return carry
-
-    lax.fori_loop(0, NX, step, 0)
+    before, after = upright(low_ref[...]), upright(high_ref[...])
+    for copy in copies:
+        copy.wait()
+    own = [upright(turned_ref[i, :, j * SLAB : (j + 1) * SLAB]) for i in range(2) for j in range(2)]
+    first, last = conv_edges(shift_ref, weights_ref, [before] + own + [after])
+    grid_ref[0] = first.reshape(NY, NZ, channels)
+    grid_ref[NX - 1] = last.reshape(NY, NZ, channels)
+    for x in range(INNER):
+        grid_ref[x + 1] = inner_ref[x].astype(F32).reshape(NY, NZ, channels)
     for t in range(tiles):
         x, y, z = corner(adj_ref, t, lowest)
         brick = grid_ref[pl.ds(x, VX), pl.ds(y, VY), pl.ds(pl.multiple_of(z, VZ), VZ), :]
         out_ref[t] = brick.reshape(vox, channels).astype(BF)
 
 
-def forward(adjacency, dense, low, high, weights, tiles):
-    channels = dense.shape[2]
-    return call(
-        forward_body,
+def edge_forward(adjacency, turned, low, high, weights, inner, tiles):
+    channels = turned.shape[0]
+    return call(
+        edge_forward_body,
         [jax.ShapeDtypeStruct((tiles, VX * VY * VZ, channels), BF)],
-        [adjacency, dense, low, high, weights],
+        [adjacency, turned, low, high, weights, inner],
         smem=(0,),
+        far=(1, 4, 5),
         scratch=[
-            pltpu.VMEM(SHIFTS + (channels,), BF),
+            pltpu.VMEM((3, 6, SHIFTED, channels), BF),
             pltpu.VMEM((NX, NY, NZ, channels), F32),
-        ],
-        flops=2 * DENSE * KOFF * channels * channels,
+            pltpu.VMEM((2, channels, 2 * SLAB), BF),
+            pltpu.VMEM(weights.shape, BF),
+            pltpu.VMEM(inner.shape, BF),
+            pltpu.SemaphoreType.DMA((4,)),
+        ],
+        flops=4 * SLAB * KOFF * channels * channels,
+        limit=58,
     )[0]
 
 
-def voxel_body(
-    cap_rows, adj_ref, msg_ref, grad_ref, turned_ref, dense_ref, low_ref, high_ref, back_ref,
-    table_ref, feats_ref, pick_ref,
-):
-    regions, rows, channels = msg_ref.shape
+def read_slots(cap_rows, adj_ref, msg_ref, table_ref):
+    regions = msg_ref.shape[0]
     tiles = adj_ref.shape[0]
     segs = up_to(cap_rows, LANES) // LANES
     lowest = lax.axis_index("region") * tiles
     for r in range(regions):
-        feats_ref[r * cap_rows : (r + 1) * cap_rows, :] = msg_ref[r, 0:cap_rows, :]
         tile = msg_ref[r, cap_rows : cap_rows + 16, :].astype(F32)
         for s in range(segs):
             lanes = slice(s * LANES, (s + 1) * LANES)
@@ -269,77 +382,76 @@
     spot = jnp.where(start < 0, -LANES, start + inside)
     blocks = (spot >> 7).astype(F32)
     withins = (spot & (LANES - 1)).astype(F32)
-    turned = jnp.transpose(jnp.concatenate([blocks, withins], axis=0))
-    lane = iota((cap_rows, LANES), 1, F32).astype(BF)
+    return jnp.transpose(jnp.concatenate([blocks, withins], axis=0))
+
+
+def fill_picks(pick_ref, columns, r, regions, cap_rows, row):
+    shape = (cap_rows, LANES)
+    lane = iota(shape, 1, F32).astype(BF)
+    block = jnp.broadcast_to(columns[0:cap_rows, r : r + 1], shape).astype(BF)
+    place = regions + r
+    within = jnp.broadcast_to(columns[0:cap_rows, place : place + 1], shape).astype(BF)
+    one = jnp.where(lane == within, jnp.ones_like(lane), jnp.zeros_like(lane))
+    for q in range(DENSE // LANES):
+        pick_ref[row : row + cap_rows, q * LANES : (q + 1) * LANES] = jnp.where(
+            block == jnp.asarray(q, BF), one, jnp.zeros_like(one)
+        )
+
+
+def voxel_body(
+    cap_rows, scaling, adj_ref, msg_ref, shift_far, grad_far, edge_shift_far, edge_grad_far,
+    turned_far, low_ref, high_ref, back_far, keep_ref, send_ref,
+    table_ref, feats_ref, pick_ref, all_ref, shift_ref, grad_ref, turned_ref, back_ref, sems,
+):
+    grad_pairs = (
+        (grad_far, grad_ref.at[1 : NX - 1]),
+        (edge_grad_far.at[0], grad_ref.at[0]),
+        (edge_grad_far.at[1], grad_ref.at[NX - 1]),
+    )
+    shift_pairs = (
+        (shift_far, shift_ref.at[:, 1 : NX + 1]),
+        (edge_shift_far.at[0], shift_ref.at[:, 0]),
+        (edge_shift_far.at[1], shift_ref.at[:, NX + 1]),
+    )
+    copies = [
+        pltpu.make_async_copy(a, b, sems.at[2 + i]) for i, (a, b) in enumerate(grad_pairs + shift_pairs)
+    ]
+    for copy in copies:
+        copy.start()
+    regions, rows, channels = msg_ref.shape
+    total = regions * cap_rows
+    columns = read_slots(cap_rows, adj_ref, msg_ref, table_ref)
     for r in range(regions):
-        block = jnp.broadcast_to(turned[0:cap_rows, r : r + 1], (cap_rows, LANES)).astype(BF)
-        within = jnp.broadcast_to(
-            turned[0:cap_rows, regions + r : regions + r + 1], (cap_rows, LANES)
-        ).astype(BF)
-        one = jnp.where(lane == within, jnp.ones_like(lane), jnp.zeros_like(lane))
-        for q in range(DENSE // LANES):
-            pick_ref[r * cap_rows : (r + 1) * cap_rows, q * LANES : (q + 1) * LANES] = jnp.where(
-                block == jnp.asarray(q, BF), one, jnp.zeros_like(one)
-            )
-    total = regions * cap_rows
+        feats_ref[r * cap_rows : (r + 1) * cap_rows, :] = msg_ref[r, 0:cap_rows, :]
+        fill_picks(pick_ref, columns, r, regions, cap_rows, r * cap_rows)
     flipped = jnp.transpose(feats_ref[...].astype(F32)).astype(BF)
     left = jnp.concatenate([flipped, jnp.ones((16, total), BF)], axis=0)
     width = 2 * LANES
+    for copy in copies[:3]:
+        copy.wait()
     for q in range(0, DENSE, width):
         part = jnp.dot(left, pick_ref[:, q : q + width], preferred_element_type=F32)
         denom = jnp.maximum(part[channels : channels + 8], 1.0)
-        mean = part[0:channels] / denom[0:1]
-        turned_ref[:, q : q + width] = mean.astype(BF)
-        upright = jnp.transpose(mean).astype(BF)
-        dense_ref[q // SLAB, q % SLAB : q % SLAB + width, :] = upright
-        if q == 0:
-            low_ref[...] = upright
-        if q == DENSE - width:
-            high_ref[...] = upright
-        column = jnp.transpose(denom)[:, 0:1]
-        grad_ref[q // SLAB, q % SLAB : q % SLAB + width, :] = (
-            grad_ref[q // SLAB, q % SLAB : q % SLAB + width, :] / column
-        )
+        turned_ref[:, q : q + width] = (part[0:channels] / denom[0:1]).astype(BF)
+        x = q // SLAB
+        grad_ref[x] = grad_ref[x] / jnp.transpose(denom)[:, 0:1]
+    turned_out = pltpu.make_async_copy(turned_ref, turned_far, sems.at[0])
+    turned_out.start()
+    low_ref[...] = turned_ref[:, 0:SLAB]
+    high_ref[...] = turned_ref[:, DENSE - SLAB : DENSE]
     voxel_grad = grad_ref[...].reshape(DENSE, channels).astype(BF)
-    chunk = total // 4
-    for start in range(0, total, chunk):
+    group = regions // 4
+    for r in range(0, regions, group):
         picked = jnp.dot(
-            pick_ref[start : start + chunk, :], voxel_grad, preferred_element_type=F32
-        )
-        for r in range(start // cap_rows, (start + chunk) // cap_rows):
-            back_ref[r] = picked[r * cap_rows - start : (r + 1) * cap_rows - start].astype(BF)
-
-
-def voxels(adjacency, msg, grad, cap_rows):
-    regions, rows, channels = msg.shape
-    segs = up_to(cap_rows, LANES) // LANES
-    face = jax.ShapeDtypeStruct((SLAB, channels), BF)
-    total = regions * cap_rows
-    return call(
-        functools.partial(voxel_body, cap_rows),
-        [
-            jax.ShapeDtypeStruct((channels, DENSE), BF),
-            jax.ShapeDtypeStruct((NX, SLAB, channels), BF),
-            face,
-            face,
-            jax.ShapeDtypeStruct((regions, cap_rows, channels), BF),
-        ],
-        [adjacency, msg, grad],
-        smem=(0,),
-        scratch=[
-            pltpu.VMEM((2 * regions, segs * LANES), F32),
-            pltpu.VMEM((total, channels), BF),
-            pltpu.VMEM((total, DENSE), BF),
-        ],
-        flops=4 * total * DENSE * channels,
-    )
-
-
-def weight_body(scaling, turned_ref, shift_ref, keep_ref, send_ref, all_ref):
-    channels = turned_ref.shape[0]
-    half = keep_ref.shape[0]
-    core = lax.rem(lax.axis_index("region"), 2)
+            pick_ref[r * cap_rows : (r + group) * cap_rows, :], voxel_grad, preferred_element_type=F32
+        ).astype(BF)
+        for i in range(group):
+            back_ref[r + i] = picked[i * cap_rows : (i + 1) * cap_rows]
+    back_out = pltpu.make_async_copy(back_ref, back_far, sems.at[1])
+    back_out.start()
     left = turned_ref[...]
+    for copy in copies[3:]:
+        copy.wait()
     for k in range(0, KOFF, 2):
         pieces = []
         for j in range(k, min(k + 2, KOFF)):
@@ -351,19 +463,70 @@
         for i in range(len(pieces)):
             at = (KOFF - 1 - k - i) * channels
             all_ref[at : at + channels, :] = term[:, i * channels : (i + 1) * channels]
-    keep_ref[...] = all_ref[pl.ds(pl.multiple_of(core * half, 8), half), :]
-    send_ref[...] = all_ref[pl.ds(pl.multiple_of((1 - core) * half, 8), half), :]
-
-
-def weight_terms(turned, shifts, scaling):
-    channels = turned.shape[0]
-    half = jax.ShapeDtypeStruct((KOFF * channels // 2, channels), F32)
-    return call(
-        functools.partial(weight_body, scaling),
-        [half, half],
-        [turned, shifts],
-        scratch=[pltpu.VMEM((KOFF * channels, channels), F32)],
-        flops=2 * DENSE * KOFF * channels * channels,
+    core = lax.rem(lax.axis_index("region"), 2)
+    half = keep_ref.shape[0]
+    keep_ref[...] = all_ref[pl.ds(pl.multiple_of(core * half, 16), half), :]
+    send_ref[...] = all_ref[pl.ds(pl.multiple_of((1 - core) * half, 16), half), :].astype(BF)
+    turned_out.wait()
+    back_out.wait()
+
+
+def voxels(adjacency, msg, shifts, grad, edge_shifts, edge_grad, cap_rows, scaling):
+    regions, rows, channels = msg.shape
+    segs = up_to(cap_rows, LANES) // LANES
+    total = regions * cap_rows
+    face = jax.ShapeDtypeStruct((channels, SLAB), BF)
+    half = (KOFF * channels // 2, channels)
+    return call(
+        functools.partial(voxel_body, cap_rows, scaling),
+        [
+            jax.ShapeDtypeStruct((channels, DENSE), BF),
+            face,
+            face,
+            jax.ShapeDtypeStruct((regions, cap_rows, channels), BF),
+            jax.ShapeDtypeStruct(half, F32),
+            jax.ShapeDtypeStruct(half, BF),
+        ],
+        [adjacency, msg, shifts, grad, edge_shifts, edge_grad],
+        smem=(0,),
+        far=(2, 3, 4, 5),
+        far_outs=(0, 3),
+        scratch=[
+            pltpu.VMEM((2 * regions, segs * LANES), F32),
+            pltpu.VMEM((total, channels), BF),
+            pltpu.VMEM((total, DENSE), BF),
+            pltpu.VMEM((KOFF * channels, channels), F32),
+            pltpu.VMEM((3, NX + 2, SHIFTED, channels), BF),
+            pltpu.VMEM((NX, SLAB, channels), F32),
+            pltpu.VMEM((channels, DENSE), BF),
+            pltpu.VMEM((regions, cap_rows, channels), BF),
+            pltpu.SemaphoreType.DMA((8,)),
+        ],
+        flops=2 * DENSE * (KOFF * channels + 2 * total) * channels,
+        limit=60,
+    )
+
+
+def split_body(keep_ref, got_ref, own_ref, *sent_refs):
+    rows = own_ref.shape[0]
+    size = 1 + len(sent_refs)
+    side = lax.rem(lax.axis_index("region") // 2, size)
+    for i in range(size):
+        part = pl.ds(pl.multiple_of((side ^ i) * rows, 16), rows)
+        total = keep_ref[part, :] + got_ref[part, :].astype(F32)
+        if i == 0:
+            own_ref[...] = total
+        else:
+            sent_refs[i - 1][...] = total.astype(BF)
+
+
+def split(keep, got, size):
+    rows, channels = keep.shape[0] // size, keep.shape[1]
+    return call(
+        split_body,
+        [jax.ShapeDtypeStruct((rows, channels), F32)]
+        + [jax.ShapeDtypeStruct((rows, channels), BF)] * (size - 1),
+        [keep, got],
     )
 
 
@@ -410,29 +573,56 @@
     return lax.ppermute(array, "region", [(i, i ^ bit) for i in range(count)])
 
 
-def total_over_region(keep, send):
-    count = lax.axis_size("region")
+def in_order(pieces, side):
+    return jnp.concatenate(
+        [lax.select_n(side ^ q, *pieces) for q in range(len(pieces))], axis=0
+    )
+
+
+def reduce_group(term, bit, size):
+    side = (lax.axis_index("region") // bit) % size
+    rows = term.shape[0] // size
+    parts = [lax.dynamic_slice_in_dim(term, (side ^ i) * rows, rows) for i in range(size)]
+    return sum_group(parts[0], [part.astype(BF) for part in parts[1:]], bit)
+
+
+def sum_group(total, sent, bit):
+    for i, part in enumerate(sent):
+        total = total + swapped(part, bit * (i + 1)).astype(F32)
+    return total
+
+
+def gather_group(term, bit, size):
+    return [term] + [swapped(term, bit * i) for i in range(1, size)]
+
+
+def groups_of(count):
+    found, bit = [], 2
+    while bit < count:
+        size = min(4, count // bit)
+        found.append((bit, size))
+        bit *= size
+    return found
+
+
+def last_body(own_ref, other_ref, out_ref):
+    size, rows, channels = own_ref.shape
     me = lax.axis_index("region")
-    term = keep + swapped(send, 1)
-    bit = 2
-    while bit < count:
-        half = term.shape[0] // 2
-        side = (me // bit) % 2
-        sent = lax.dynamic_slice_in_dim(term, (1 - side) * half, half).astype(BF)
-        kept = lax.dynamic_slice_in_dim(term, side * half, half)
-        term = kept + swapped(sent, bit).astype(F32)
-        bit *= 2
-    term = term.astype(BF)
-    while bit > 1:
-        bit //= 2
-        other = swapped(term, bit)
-        side = (me // bit) % 2
-        term = jnp.where(
-            side == 0,
-            jnp.concatenate([term, other], axis=0),
-            jnp.concatenate([other, term], axis=0),
-        )
-    return term.astype(F32)
+    core = lax.rem(me, 2)
+    side = lax.rem(me // 2, size)
+    for half, ref in ((core, own_ref), (1 - core, other_ref)):
+        for i in range(size):
+            at = pl.multiple_of((half * size + (side ^ i)) * rows, 16)
+            out_ref[pl.ds(at, rows), :] = ref[i].astype(F32)
+
+
+def last_step(own, other):
+    size, rows, channels = own.shape
+    return call(
+        last_body,
+        [jax.ShapeDtypeStruct((2 * size * rows, channels), F32)],
+        [own, other],
+    )[0]
 
 
 def exchange(array):
@@ -452,15 +642,33 @@
     cot, cot_low, cot_high = to_dense(adjacency, cotangent)
     below, above = from_sides(cot_low, cot_high)
     mirrored = jnp.transpose(kernel[::-1], (0, 2, 1)).reshape(KOFF * channels, channels)
-    grad, shifts = gradient(cot, below, above, mirrored)
-    turned, feats, low, high, back = voxels(adjacency, received, grad, cap_rows)
+    grad, shifts = inner_gradient(cot, mirrored)
+    edge_grad, edge_shifts = edge_gradient(cot, below, above, mirrored)
     scaling = 1.0 / math.sqrt(tiles * regions * vox)
-    keep, send = weight_terms(turned, shifts, scaling)
-    grad_weight = total_over_region(keep, send).reshape(KOFF, channels, channels)
+    turned, low, high, back, keep, send = voxels(
+        adjacency, received, shifts, grad, edge_shifts, edge_grad, cap_rows, scaling
+    )
+    returned = exchange(back)
+    groups = groups_of(regions)
+    bit, size = groups[0]
+    term, *sent = split(keep, swapped(send, 1), size)
+    weights = kernel.reshape(KOFF * channels, channels)
+    turned, *sent = lax.optimization_barrier((turned, *sent))
+    inner = inner_forward(turned, weights)
+    term = sum_group(term, sent, bit)
+    term, returned, inner = lax.optimization_barrier((term, returned, inner))
+    for bit, size in groups[1:]:
+        term = reduce_group(term, bit, size)
+    term, low, high = lax.optimization_barrier((term.astype(BF), low, high))
     feats_below, feats_above = from_sides(low, high)
-    weights = kernel.reshape(KOFF * channels, channels)
-    out_tiles = forward(adjacency, feats, feats_below, feats_above, weights, tiles)
-    grad_points = unpack(place, exchange(back), points)
+    grad_points = unpack(place, returned, points)
+    out_tiles = edge_forward(adjacency, turned, feats_below, feats_above, weights, inner, tiles)
+    for bit, size in groups[:0:-1]:
+        side = (lax.axis_index("region") // bit) % size
+        term = in_order(gather_group(term, bit, size), side)
+    own = jnp.stack(gather_group(term, *groups[0]))
+    own, out_tiles, grad_points = lax.optimization_barrier((own, out_tiles, grad_points))
+    grad_weight = last_step(own, swapped(own, 1)).reshape(KOFF, channels, channels)
     return out_tiles, grad_points, grad_weight
 
 

time: 124 us -> 100 us (0.81)
  the two profiles are of different devices: /device:TPU:11 before, /device:TPU:0 now
where the time goes in v1:
time: 100 us; the launch traced here: 98.5 us
  Pallas kernels  37.9 us (38%)
  starting transfers between devices  37 us (37%)
  waiting for transfers between devices  17.4 us (17%)
  local copies, waits for them, and re-layouts  5.06 us (5%)
    pallas_call x10, Pallas kernels, call(): pl.pallas_call(body, out_shape=outs, in_specs=[SMEM if i in smem else FAR...  37.9 us
    ppermute x10, waiting for transfers between devices, swapped(): return lax.ppermute(array, 'region', [(i, i ^ bit) for i in range(count)])  15.6 us
    all_to_all x2, starting transfers between devices, exchange(): lax.all_to_all(array, 'region', split_axis=0, concat_axis=0, tiled=True)  15.5 us
    ppermute x10, starting transfers between devices, swapped(): return lax.ppermute(array, 'region', [(i, i ^ bit) for i in range(count)])  15.4 us
    ppermute x4, starting transfers between devices, from_sides(): return (lax.ppermute(high, 'region', up), lax.ppermute(low, 'region', down))  6.12 us
    unnamed x28, local copies, waits for them, and re-layouts  3.31 us
  transfers between devices with their start and end apart: 16, of which 8 were waited for; matrix products, arithmetic and copies ran while one was open for 2% of the time, Pallas kernels for 22%

profile of v1, /device:TPU:0, one launch (start us, length us, event | category | flops | bytes accessed | tf_op | source)
XLA Modules:
  0.0 98.5 jit_solution(17387982434218932220)
XLA Ops:
  0.7 3.6 %shard_map.85 = (bf16[16,176,128]{2,1,0:T(8,128)(2,1)}, f32[8,1024]{1,0:T(8,128)}) custom-call(s32[1,1024]{1,0:T(1,128)} %bitcast.20, s32[1,1024]{1,0:T(1,128)} %bitcast.21, bf16[1024,128]{1,0:T(8,128)(2,1)} %feats_far.1), custom_call_target="tpu_custom_call" | custom-call | flops 671088640 | bytes 1024000 | tf_op jit(solution)/shard_map/pallas_call | solution.py:43
  4.3 7.4 %all-to-all-start = ((bf16[16,176,128]{2,1,0:T(8,128)(2,1)}), bf16[16,176,128]{2,1,0:T(8,128)(2,1)}, u32[]{:S(2)}, u32[]{:S(2)}) async-start(bf16[16,176,128]{2,1,0:T(8,128)(2,1)} %get-tuple-element.35), calls=%async_computation | async-start | bytes 1441792 | tf_op jit(solution)/shard_map/all_to_all | solution.py:629
  11.7 0.9 shard_map.86
  12.6 0.8 copy-done.4
  13.4 2.3 %collective-permute-start = (bf16[256,128]{1,0:T(8,128)(2,1)S(1)}, bf16[256,128]{1,0:T(8,128)(2,1)S(1)}, u32[]{:S(2)}, u32[]{:S(2)}) collective-permute-start(bf16[256,128]{1,0:T(8,128)(2,1)S(1)} %get-tuple-element.39), channel_id=1, source_target_pairs={{0,1},{1,2},{2,3},{3,4},{4,5},{5,6},{6,7},{7,8},{8,9},{9,10},{10,1... | collective-permute-start | bytes 196616 | tf_op jit(solution)/shard_map/ppermute | solution.py:568
  15.7 1.3 %collective-permute-start.1 = (bf16[256,128]{1,0:T(8,128)(2,1)S(1)}, bf16[256,128]{1,0:T(8,128)(2,1)S(1)}, u32[]{:S(2)}, u32[]{:S(2)}) collective-permute-start(bf16[256,128]{1,0:T(8,128)(2,1)S(1)} %get-tuple-element.40), channel_id=1, source_target_pairs={{1,0},{2,1},{3,2},{4,3},{5,4},{6,5},{7,6},{8,7},{9,8},{10,9},{11,1... | collective-permute-start | bytes 196616 | tf_op jit(solution)/shard_map/ppermute | solution.py:568
  17.1 1.7 %copy.9 = bf16[27,128,128]{2,1,0:T(8,128)(2,1)} copy(bf16[27,128,128]{1,2,0:T(8,128)(2,1)S(1)} %reverse_bitcast_fusion) | data formatting | bytes 1769472 | tf_op jit(solution)/shard_map/transpose | solution.py:644
  18.7 6.4 %shard_map.87 = (f32[6,256,128]{2,1,0:T(8,128)}, bf16[3,8,288,128]{3,2,1,0:T(8,128)(2,1)}) custom-call(bf16[8,256,128]{2,1,0:T(8,128)(2,1)} %copy-done.4, bf16[3456,128]{1,0:T(8,128)(2,1)} %bitcast.12), custom_call_target="tpu_custom_call" | custom-call | flops 1358954496 | bytes 3964928 | tf_op jit(solution)/shard_map/pallas_call | solution.py:43
  25.2 1.1 %shard_map.88 = (f32[2,256,128]{2,1,0:T(8,128)S(1)}, bf16[2,3,288,128]{3,2,1,0:T(8,128)(2,1)S(1)}) custom-call(bf16[8,256,128]{2,1,0:T(8,128)(2,1)S(1)} %copy-done.5, bf16[256,128]{1,0:T(8,128)(2,1)S(1)} %collective-permute-done.low_ref, bf16[256,128]{1,0:T(8,128)(2,1)S(1)} %collective-permute-done.1.high_ref, bf16[3456,128]{1,0:T(8,128)(2,1)S(1)} %bitcast.13), custom_call_target="tpu_custom_call" | custom-call | flops 452984832 | bytes 2244608 | tf_op jit(solution)/shard_map/pallas_call | solution.py:43
  26.4 0.8 copy-done.6
  27.8 1.6 %all-to-all-done.msg_ref = bf16[16,176,128]{2,1,0:T(8,128)(2,1)} async-done(((bf16[16,176,128]{2,1,0:T(8,128)(2,1)}), bf16[16,176,128]{2,1,0:T(8,128)(2,1)}, u32[]{:S(2)}, u32[]{:S(2)}) %all-to-all-start) | async-done | bytes 720928 | tf_op jit(solution)/shard_map/all_to_all | solution.py:629
  29.4 11.7 %shard_map.89 = (bf16[128,2048]{1,0:T(8,128)(2,1)}, bf16[128,256]{1,0:T(8,128)(2,1)}, bf16[128,256]{1,0:T(8,128)(2,1)}, bf16[16,160,128]{2,1,0:T(8,128)(2,1)}, f...) custom-call(s32[16,27]{1,0:T(8,128)} %adj_ref.5, bf16[16,176,128]{2,1,0:T(8,128)(2,1)} %all-to-all-done.msg_ref, ...), custom_call_target="tpu_custom_call" | custom-call | flops 4496293888 | bytes 6620864 | tf_op jit(solution)/shard_map/pallas_call | solution.py:43
  41.2 8.1 %all-to-all-start.1 = ((bf16[16,160,128]{2,1,0:T(8,128)(2,1)}), bf16[16,160,128]{2,1,0:T(8,128)(2,1)S(1)}, u32[]{:S(2)}, u32[]{:S(2)}) async-start(bf16[16,160,128]{2,1,0:T(8,128)(2,1)} %get-tuple-element.53), calls=%async_computation.1 | async-start | bytes 1310720 | tf_op jit(solution)/shard_map/all_to_all | solution.py:629
  49.7 1.6 %collective-permute-done.2.got_ref = bf16[1728,128]{1,0:T(8,128)(2,1)S(1)} collective-permute-done((bf16[1728,128]{1,0:T(8,128)(2,1)}, bf16[1728,128]{1,0:T(8,128)(2,1)S(1)}, u32[]{:S(2)}, u32[]{:S(2)}) %collective-permute-start.2) | collective-permute-done | bytes 442400 | tf_op jit(solution)/shard_map/ppermute | solution.py:573
  51.4 2.0 %collective-permute-start.3 = (bf16[432,128]{1,0:T(8,128)(2,1)S(1)}, bf16[432,128]{1,0:T(8,128)(2,1)S(1)}, u32[]{:S(2)}, u32[]{:S(2)}) collective-permute-start(bf16[432,128]{1,0:T(8,128)(2,1)S(1)} %get-tuple-element.50), channel_id=1, source_target_pairs={{0,2},{1,3},{2,0},{3,1},{4,6},{5,7},{6,4},{7,5},{8,10},{9,11},{10,... | collective-permute-start | bytes 331784 | tf_op jit(solution)/shard_map/ppermute | solution.py:573
  53.4 1.5 %collective-permute-start.4 = (bf16[432,128]{1,0:T(8,128)(2,1)S(1)}, bf16[432,128]{1,0:T(8,128)(2,1)S(1)}, u32[]{:S(2)}, u32[]{:S(2)}) collective-permute-start(bf16[432,128]{1,0:T(8,128)(2,1)S(1)} %get-tuple-element.51), channel_id=1, source_target_pairs={{0,4},{1,5},{2,6},{3,7},{4,0},{5,1},{6,2},{7,3},{8,12},{9,13},{10,... | collective-permute-start | bytes 331784 | tf_op jit(solution)/shard_map/ppermute | solution.py:573
  55.0 6.0 %shard_map.91.inner_far = bf16[6,256,128]{2,1,0:T(8,128)(2,1)} custom-call(bf16[128,2048]{1,0:T(8,128)(2,1)} %get-tuple-element.54.turned_far, bf16[3456,128]{1,0:T(8,128)(2,1)} %bitcast.14), custom_call_target="tpu_custom_call" | custom-call | flops 1358954496 | bytes 1802240 | tf_op jit(solution)/shard_map/pallas_call | solution.py:43
  61.0 4.4 %collective-permute-done.4 = bf16[432,128]{1,0:T(8,128)(2,1)S(1)} collective-permute-done((bf16[432,128]{1,0:T(8,128)(2,1)S(1)}, bf16[432,128]{1,0:T(8,128)(2,1)S(1)}, u32[]{:S(2)}, u32[]{:S(2)}) %collective-permute-start.4) | collective-permute-done | bytes 110624 | tf_op jit(solution)/shard_map/ppermute | solution.py:573
  65.4 3.1 %collective-permute-done.5 = bf16[432,128]{1,0:T(8,128)(2,1)S(1)} collective-permute-done((bf16[432,128]{1,0:T(8,128)(2,1)S(1)}, bf16[432,128]{1,0:T(8,128)(2,1)S(1)}, u32[]{:S(2)}, u32[]{:S(2)}) %collective-permute-start.5) | collective-permute-done | bytes 110624 | tf_op jit(solution)/shard_map/ppermute | solution.py:573
  68.6 2.6 %collective-permute-start.6 = (bf16[216,128]{1,0:T(8,128)(2,1)S(1)}, bf16[216,128]{1,0:T(8,128)(2,1)S(1)}, u32[]{:S(2)}, u32[]{:S(2)}) collective-permute-start(bf16[216,128]{1,0:T(8,128)(2,1)S(1)} %dynamic-slice_convert_fusion), channel_id=1, source_target_pairs={{0,8},{1,9},{2,10},{3,11},{4,12},{5,13},{6,14},{7,15},{8,0},{9,1},... | collective-permute-start | bytes 165896 | tf_op jit(solution)/shard_map/ppermute | solution.py:573
  71.2 2.5 %collective-permute-done.6 = bf16[216,128]{1,0:T(8,128)(2,1)S(1)} collective-permute-done((bf16[216,128]{1,0:T(8,128)(2,1)S(1)}, bf16[216,128]{1,0:T(8,128)(2,1)S(1)}, u32[]{:S(2)}, u32[]{:S(2)}) %collective-permute-start.6) | collective-permute-done | bytes 55328 | tf_op jit(solution)/shard_map/ppermute | solution.py:573
  73.8 2.6 %collective-permute-start.7 = (bf16[216,128]{1,0:T(8,128)(2,1)S(1)}, bf16[216,128]{1,0:T(8,128)(2,1)S(1)}, u32[]{:S(2)}, u32[]{:S(2)}) collective-permute-start(bf16[216,128]{1,0:T(8,128)(2,1)S(1)} %add_convert_fusion), channel_id=1, source_target_pairs={{0,8},{1,9},{2,10},{3,11},{4,12},{5,13},{6,14},{7,15},{8,0},{9,1},... | collective-permute-start | bytes 165896 | tf_op jit(solution)/shard_map/ppermute | solution.py:573
  76.4 2.5 %collective-permute-done.7 = bf16[216,128]{1,0:T(8,128)(2,1)S(1)} collective-permute-done((bf16[216,128]{1,0:T(8,128)(2,1)S(1)}, bf16[216,128]{1,0:T(8,128)(2,1)S(1)}, u32[]{:S(2)}, u32[]{:S(2)}) %collective-permute-start.7) | collective-permute-done | bytes 55328 | tf_op jit(solution)/shard_map/ppermute | solution.py:573
  79.6 1.3 %collective-permute-start.9 = (bf16[432,128]{1,0:T(8,128)(2,1)S(1)}, bf16[432,128]{1,0:T(8,128)(2,1)S(1)}, u32[]{:S(2)}, u32[]{:S(2)}) collective-permute-start(bf16[432,128]{1,0:T(8,128)(2,1)S(1)} %get-tuple-element.68), channel_id=1, source_target_pairs={{0,4},{1,5},{2,6},{3,7},{4,0},{5,1},{6,2},{7,3},{8,12},{9,13},{10,... | collective-permute-start | bytes 331784 | tf_op jit(solution)/shard_map/ppermute | solution.py:573
  80.9 1.6 %collective-permute-start.10 = (bf16[432,128]{1,0:T(8,128)(2,1)S(1)}, bf16[432,128]{1,0:T(8,128)(2,1)S(1)}, u32[]{:S(2)}, u32[]{:S(2)}) collective-permute-start(bf16[432,128]{1,0:T(8,128)(2,1)S(1)} %get-tuple-element.68), channel_id=1, source_target_pairs={{0,6},{1,7},{2,4},{3,5},{4,2},{5,3},{6,0},{7,1},{8,14},{9,15},{10,... | collective-permute-start | bytes 331784 | tf_op jit(solution)/shard_map/ppermute | solution.py:573
  82.5 1.3 %collective-permute-start.11 = (bf16[128,256]{1,0:T(8,128)(2,1)S(1)}, bf16[128,256]{1,0:T(8,128)(2,1)S(1)}, u32[]{:S(2)}, u32[]{:S(2)}) collective-permute-start(bf16[128,256]{1,0:T(8,128)(2,1)S(1)} %copy-done.13), channel_id=1, source_target_pairs={{0,1},{1,2},{2,3},{3,4},{4,5},{5,6},{6,7},{7,8},{8,9},{9,10},{10,1... | collective-permute-start | bytes 196616 | tf_op jit(solution)/shard_map/ppermute | solution.py:568
  83.8 1.3 %collective-permute-start.12 = (bf16[128,256]{1,0:T(8,128)(2,1)S(1)}, bf16[128,256]{1,0:T(8,128)(2,1)S(1)}, u32[]{:S(2)}, u32[]{:S(2)}) collective-permute-start(bf16[128,256]{1,0:T(8,128)(2,1)S(1)} %copy-done.12), channel_id=1, source_target_pairs={{1,0},{2,1},{3,2},{4,3},{5,4},{6,5},{7,6},{8,7},{9,8},{10,9},{11,1... | collective-permute-start | bytes 196616 | tf_op jit(solution)/shard_map/ppermute | solution.py:568
  85.1 2.4 %shard_map.93 = bf16[1024,128]{1,0:T(8,128)(2,1)} custom-call(f32[8,1024]{1,0:T(8,128)S(1)} %copy-done.8, bf16[16,160,128]{2,1,0:T(8,128)(2,1)S(1)} %all-to-all-done.1.rows_ref), custom_call_target="tpu_custom_call" | custom-call | flops 671088640 | bytes 950272 | tf_op jit(solution)/shard_map/pallas_call | solution.py:43
  88.8 4.3 %shard_map.92 = bf16[16,128,128]{2,1,0:T(8,128)(2,1)} custom-call(s32[16,27]{1,0:T(8,128)} %adj_ref.5, bf16[128,2048]{1,0:T(8,128)(2,1)} %get-tuple-element.54.turned_far, bf16[128,256]{1,0:T(8,128)(2,1)} %copy-done.10, bf16[128,256]{1,0:T(8,128)(2,1)} %copy-done.11, bf16[3456,128]{1,0:T(8,128)(2,1)} %bitcast.15, bf16[6,256,128]{2,1,0:T(8,128)(2,1)} %shard_map.91.inner_far), custom_call_target="tpu_custom_call" | custom-call | flops 452984832 | bytes 2459328 | tf_op jit(solution)/shard_map/pallas_call | solution.py:43
  93.2 2.6 %collective-permute-start.13 = (bf16[4,432,128]{2,1,0:T(8,128)(2,1)S(1)}, bf16[4,432,128]{2,1,0:T(8,128)(2,1)S(1)}, u32[]{:S(2)}, u32[]{:S(2)}) collective-permute-start(bf16[4,432,128]{2,1,0:T(8,128)(2,1)S(1)} %pad_maximum_fusion.own_ref), channel_id=1, source_target_pairs={{0,1},{1,0},{2,3},{3,2},{4,5},{5,4},{6,7},{7,6},{8,9},{9,8},{10,11... | collective-permute-start | bytes 1327112 | tf_op jit(solution)/shard_map/ppermute | solution.py:573
  95.8 1.4 %collective-permute-done.13.other_ref = bf16[4,432,128]{2,1,0:T(8,128)(2,1)S(1)} collective-permute-done((bf16[4,432,128]{2,1,0:T(8,128)(2,1)S(1)}, bf16[4,432,128]{2,1,0:T(8,128)(2,1)S(1)}, u32[]{:S(2)}, u32[]{:S(2)}) %collective-permute-start.13) | collective-permute-done | bytes 442400 | tf_op jit(solution)/shard_map/ppermute | solution.py:573
  97.2 1.3 %shard_map.94 = f32[3456,128]{1,0:T(8,128)} custom-call(bf16[4,432,128]{2,1,0:T(8,128)(2,1)S(1)} %pad_maximum_fusion.own_ref, bf16[4,432,128]{2,1,0:T(8,128)(2,1)S(1)} %collective-permute-done.13.other_ref), custom_call_target="tpu_custom_call" | custom-call | bytes 2654208 | tf_op jit(solution)/shard_map/pallas_call | solution.py:43
  (46 shorter events, 3.6 us)
Async XLA Ops:
  0.6 11.1 %copy-start.2 = (bf16[16,128,128]{2,1,0:T(8,128)(2,1)S(1)}, bf16[16,128,128]{2,1,0:T(8,128)(2,1)}, u32[]{:S(2)}) copy-start(bf16[16,128,128]{2,1,0:T(8,128)(2,1)} %bricks_ref.1) | copy-start | bytes 1572868
  0.6 11.1 %copy-start.3 = (s32[16,27]{1,0:T(8,128)S(1)}, s32[16,27]{1,0:T(8,128)}, u32[]{:S(2)}) copy-start(s32[16,27]{1,0:T(8,128)} %adj_ref.5) | copy-start | bytes 5188
  0.7 16.3 %copy-start.9 = (bf16[27,128,128]{2,1,0:T(8,128)(2,1)S(1)}, bf16[27,128,128]{2,1,0:T(8,128)(2,1)}, u32[]{:S(2)}) copy-start(bf16[27,128,128]{2,1,0:T(8,128)(2,1)} %param.10) | copy-start | bytes 2654212
  4.3 25.1 %all-to-all-start = ((bf16[16,176,128]{2,1,0:T(8,128)(2,1)}), bf16[16,176,128]{2,1,0:T(8,128)(2,1)}, u32[]{:S(2)}, u32[]{:S(2)}) async-start(bf16[16,176,128]{2,1,0:T(8,128)(2,1)} %get-tuple-element.35), calls=%async_computation | async-start | bytes 1441792 | tf_op jit(solution)/shard_map/all_to_all | solution.py:629
  12.6 0.8 copy-start.4
  13.4 11.8 %collective-permute-start = (bf16[256,128]{1,0:T(8,128)(2,1)S(1)}, bf16[256,128]{1,0:T(8,128)(2,1)S(1)}, u32[]{:S(2)}, u32[]{:S(2)}) collective-permute-start(bf16[256,128]{1,0:T(8,128)(2,1)S(1)} %get-tuple-element.39), channel_id=1, source_target_pairs={{0,1},{1,2},{2,3},{3,4},{4,5},{5,6},{6,7},{7,8},{8,9},{9,10},{10,1... | collective-permute-start | bytes 196616 | tf_op jit(solution)/shard_map/ppermute | solution.py:568
  15.7 9.5 %collective-permute-start.1 = (bf16[256,128]{1,0:T(8,128)(2,1)S(1)}, bf16[256,128]{1,0:T(8,128)(2,1)S(1)}, u32[]{:S(2)}, u32[]{:S(2)}) collective-permute-start(bf16[256,128]{1,0:T(8,128)(2,1)S(1)} %get-tuple-element.40), channel_id=1, source_target_pairs={{1,0},{2,1},{3,2},{4,3},{5,4},{6,5},{7,6},{8,7},{9,8},{10,9},{11,1... | collective-permute-start | bytes 196616 | tf_op jit(solution)/shard_map/ppermute | solution.py:568
  18.7 6.5 %copy-start = (bf16[27,128,128]{2,1,0:T(8,128)(2,1)S(1)}, bf16[27,128,128]{2,1,0:T(8,128)(2,1)}, u32[]{:S(2)}) copy-start(bf16[27,128,128]{2,1,0:T(8,128)(2,1)} %copy.9) | copy-start | bytes 2654212
  18.7 6.5 %copy-start.5 = (bf16[8,256,128]{2,1,0:T(8,128)(2,1)S(1)}, bf16[8,256,128]{2,1,0:T(8,128)(2,1)}, u32[]{:S(2)}) copy-start(bf16[8,256,128]{2,1,0:T(8,128)(2,1)} %copy-done.4) | copy-start | bytes 1572868
  26.4 0.8 copy-start.6
  27.1 0.7 copy-start.7
  41.2 10.2 %copy-start.1 = (f32[1728,128]{1,0:T(8,128)S(1)}, f32[1728,128]{1,0:T(8,128)}, u32[]{:S(2)}) copy-start(f32[1728,128]{1,0:T(8,128)} %get-tuple-element.43.keep_ref) | copy-start | bytes 2654212
  41.2 27.4 %all-to-all-start.1 = ((bf16[16,160,128]{2,1,0:T(8,128)(2,1)}), bf16[16,160,128]{2,1,0:T(8,128)(2,1)S(1)}, u32[]{:S(2)}, u32[]{:S(2)}) async-start(bf16[16,160,128]{2,1,0:T(8,128)(2,1)} %get-tuple-element.53), calls=%async_computation.1 | async-start | bytes 1310720 | tf_op jit(solution)/shard_map/all_to_all | solution.py:629
  49.2 2.1 %collective-permute-start.2 = (bf16[1728,128]{1,0:T(8,128)(2,1)}, bf16[1728,128]{1,0:T(8,128)(2,1)S(1)}, u32[]{:S(2)}, u32[]{:S(2)}) collective-permute-start(bf16[1728,128]{1,0:T(8,128)(2,1)} %get-tuple-element.44), channel_id=1, source_target_pairs={{0,1},{1,0},{2,3},{3,2},{4,5},{5,4},{6,7},{7,6},{8,9},{9,8},{10,11... | collective-permute-start | bytes 1327112 | tf_op jit(solution)/shard_map/ppermute | solution.py:573
  51.4 9.6 %collective-permute-start.3 = (bf16[432,128]{1,0:T(8,128)(2,1)S(1)}, bf16[432,128]{1,0:T(8,128)(2,1)S(1)}, u32[]{:S(2)}, u32[]{:S(2)}) collective-permute-start(bf16[432,128]{1,0:T(8,128)(2,1)S(1)} %get-tuple-element.50), channel_id=1, source_target_pairs={{0,2},{1,3},{2,0},{3,1},{4,6},{5,7},{6,4},{7,5},{8,10},{9,11},{10,... | collective-permute-start | bytes 331784 | tf_op jit(solution)/shard_map/ppermute | solution.py:573
  53.4 12.0 %collective-permute-start.4 = (bf16[432,128]{1,0:T(8,128)(2,1)S(1)}, bf16[432,128]{1,0:T(8,128)(2,1)S(1)}, u32[]{:S(2)}, u32[]{:S(2)}) collective-permute-start(bf16[432,128]{1,0:T(8,128)(2,1)S(1)} %get-tuple-element.51), channel_id=1, source_target_pairs={{0,4},{1,5},{2,6},{3,7},{4,0},{5,1},{6,2},{7,3},{8,12},{9,13},{10,... | collective-permute-start | bytes 331784 | tf_op jit(solution)/shard_map/ppermute | solution.py:573
  54.9 13.7 %collective-permute-start.5 = (bf16[432,128]{1,0:T(8,128)(2,1)S(1)}, bf16[432,128]{1,0:T(8,128)(2,1)S(1)}, u32[]{:S(2)}, u32[]{:S(2)}) collective-permute-start(bf16[432,128]{1,0:T(8,128)(2,1)S(1)} %get-tuple-element.52), channel_id=1, source_target_pairs={{0,6},{1,7},{2,4},{3,5},{4,2},{5,3},{6,0},{7,1},{8,14},{9,15},{10,... | collective-permute-start | bytes 331784 | tf_op jit(solution)/shard_map/ppermute | solution.py:573
  55.0 27.5 %copy-start.13 = (bf16[128,256]{1,0:T(8,128)(2,1)S(1)}, bf16[128,256]{1,0:T(8,128)(2,1)}, u32[]{:S(2)}) copy-start(bf16[128,256]{1,0:T(8,128)(2,1)} %get-tuple-element.59) | copy-start | bytes 196612
  55.0 28.8 %copy-start.12 = (bf16[128,256]{1,0:T(8,128)(2,1)S(1)}, bf16[128,256]{1,0:T(8,128)(2,1)}, u32[]{:S(2)}) copy-start(bf16[128,256]{1,0:T(8,128)(2,1)} %get-tuple-element.60) | copy-start | bytes 196612
  55.0 30.1 %copy-start.8 = (f32[8,1024]{1,0:T(8,128)S(1)}, f32[8,1024]{1,0:T(8,128)}, u32[]{:S(2)}) copy-start(f32[8,1024]{1,0:T(8,128)} %get-tuple-element.62.place_ref) | copy-start | bytes 98308
  68.6 5.1 %collective-permute-start.6 = (bf16[216,128]{1,0:T(8,128)(2,1)S(1)}, bf16[216,128]{1,0:T(8,128)(2,1)S(1)}, u32[]{:S(2)}, u32[]{:S(2)}) collective-permute-start(bf16[216,128]{1,0:T(8,128)(2,1)S(1)} %dynamic-slice_convert_fusion), channel_id=1, source_target_pairs={{0,8},{1,9},{2,10},{3,11},{4,12},{5,13},{6,14},{7,15},{8,0},{9,1},... | collective-permute-start | bytes 165896 | tf_op jit(solution)/shard_map/ppermute | solution.py:573
  73.8 5.1 %collective-permute-start.7 = (bf16[216,128]{1,0:T(8,128)(2,1)S(1)}, bf16[216,128]{1,0:T(8,128)(2,1)S(1)}, u32[]{:S(2)}, u32[]{:S(2)}) collective-permute-start(bf16[216,128]{1,0:T(8,128)(2,1)S(1)} %add_convert_fusion), channel_id=1, source_target_pairs={{0,8},{1,9},{2,10},{3,11},{4,12},{5,13},{6,14},{7,15},{8,0},{9,1},... | collective-permute-start | bytes 165896 | tf_op jit(solution)/shard_map/ppermute | solution.py:573
  78.9 14.1 %collective-permute-start.8 = (bf16[432,128]{1,0:T(8,128)(2,1)S(1)}, bf16[432,128]{1,0:T(8,128)(2,1)S(1)}, u32[]{:S(2)}, u32[]{:S(2)}) collective-permute-start(bf16[432,128]{1,0:T(8,128)(2,1)S(1)} %get-tuple-element.68), channel_id=1, source_target_pairs={{0,2},{1,3},{2,0},{3,1},{4,6},{5,7},{6,4},{7,5},{8,10},{9,11},{10,... | collective-permute-start | bytes 331784 | tf_op jit(solution)/shard_map/ppermute | solution.py:573
  79.6 13.5 %collective-permute-start.9 = (bf16[432,128]{1,0:T(8,128)(2,1)S(1)}, bf16[432,128]{1,0:T(8,128)(2,1)S(1)}, u32[]{:S(2)}, u32[]{:S(2)}) collective-permute-start(bf16[432,128]{1,0:T(8,128)(2,1)S(1)} %get-tuple-element.68), channel_id=1, source_target_pairs={{0,4},{1,5},{2,6},{3,7},{4,0},{5,1},{6,2},{7,3},{8,12},{9,13},{10,... | collective-permute-start | bytes 331784 | tf_op jit(solution)/shard_map/ppermute | solution.py:573
  80.9 12.2 %collective-permute-start.10 = (bf16[432,128]{1,0:T(8,128)(2,1)S(1)}, bf16[432,128]{1,0:T(8,128)(2,1)S(1)}, u32[]{:S(2)}, u32[]{:S(2)}) collective-permute-start(bf16[432,128]{1,0:T(8,128)(2,1)S(1)} %get-tuple-element.68), channel_id=1, source_target_pairs={{0,6},{1,7},{2,4},{3,5},{4,2},{5,3},{6,0},{7,1},{8,14},{9,15},{10,... | collective-permute-start | bytes 331784 | tf_op jit(solution)/shard_map/ppermute | solution.py:573
  82.5 5.0 %collective-permute-start.11 = (bf16[128,256]{1,0:T(8,128)(2,1)S(1)}, bf16[128,256]{1,0:T(8,128)(2,1)S(1)}, u32[]{:S(2)}, u32[]{:S(2)}) collective-permute-start(bf16[128,256]{1,0:T(8,128)(2,1)S(1)} %copy-done.13), channel_id=1, source_target_pairs={{0,1},{1,2},{2,3},{3,4},{4,5},{5,6},{6,7},{7,8},{8,9},{9,10},{10,1... | collective-permute-start | bytes 196616 | tf_op jit(solution)/shard_map/ppermute | solution.py:568
  83.8 4.0 %collective-permute-start.12 = (bf16[128,256]{1,0:T(8,128)(2,1)S(1)}, bf16[128,256]{1,0:T(8,128)(2,1)S(1)}, u32[]{:S(2)}, u32[]{:S(2)}) collective-permute-start(bf16[128,256]{1,0:T(8,128)(2,1)S(1)} %copy-done.12), channel_id=1, source_target_pairs={{1,0},{2,1},{3,2},{4,3},{5,4},{6,5},{7,6},{8,7},{9,8},{10,9},{11,1... | collective-permute-start | bytes 196616 | tf_op jit(solution)/shard_map/ppermute | solution.py:568
  87.5 0.6 copy-start.10
  88.2 0.6 copy-start.11
  93.2 4.0 %collective-permute-start.13 = (bf16[4,432,128]{2,1,0:T(8,128)(2,1)S(1)}, bf16[4,432,128]{2,1,0:T(8,128)(2,1)S(1)}, u32[]{:S(2)}, u32[]{:S(2)}) collective-permute-start(bf16[4,432,128]{2,1,0:T(8,128)(2,1)S(1)} %pad_maximum_fusion.own_ref), channel_id=1, source_target_pairs={{0,1},{1,0},{2,3},{3,2},{4,5},{5,4},{6,7},{7,6},{8,9},{9,8},{10,11... | collective-permute-start | bytes 1327112 | tf_op jit(solution)/shard_map/ppermute | solution.py:573

commit v2 on v1

--- a/solution.py
+++ b/solution.py
@@ -27,6 +27,7 @@
 SMEM = pl.BlockSpec(memory_space=pltpu.SMEM)
 FAR = pl.BlockSpec(memory_space=pltpu.HBM)
 MIB = 1024 * 1024
+VOXEL_LIMIT = 60
 
 
 def up_to(value, unit):
@@ -215,61 +216,25 @@
     return conv_slab(shift_ref, weights_ref, 0), conv_slab(shift_ref, weights_ref, 3)
 
 
-def inner_gradient_body(dense_ref, weights_ref, grad_far, shift_far, grad_ref, shift_ref, sems):
+def inner_gradient_body(dense_ref, weights_ref, grad_ref, shift_ref):
     for x in range(NX):
         put_shifts(shift_ref, x, dense_ref[x])
-    shift_out = pltpu.make_async_copy(shift_ref, shift_far, sems.at[0])
-    shift_out.start()
 
     def store(x, value):
         grad_ref[x] = value
 
     conv_inner(shift_ref, weights_ref, store)
-    grad_out = pltpu.make_async_copy(grad_ref, grad_far, sems.at[1])
-    grad_out.start()
-    shift_out.wait()
-    grad_out.wait()
 
 
 def inner_gradient(dense, weights):
     channels = dense.shape[2]
-    grads, shifts = (INNER, SLAB, channels), (3, NX, SHIFTED, channels)
     return call(
         inner_gradient_body,
-        [jax.ShapeDtypeStruct(grads, F32), jax.ShapeDtypeStruct(shifts, BF)],
+        [jax.ShapeDtypeStruct((INNER, SLAB, channels), F32)],
         [dense, weights],
-        far_outs=(0, 1),
-        scratch=[
-            pltpu.VMEM(grads, F32),
-            pltpu.VMEM(shifts, BF),
-            pltpu.SemaphoreType.DMA((2,)),
-        ],
+        scratch=[pltpu.VMEM((3, NX, SHIFTED, channels), BF)],
         flops=2 * INNER * SLAB * KOFF * channels * channels,
-        limit=60,
-    )
-
-
-def edge_gradient_body(dense_ref, low_ref, high_ref, weights_ref, grad_ref, edge_ref, shift_ref):
-    slabs = [low_ref[...]] + [dense_ref[x] for x in (0, 1, NX - 2, NX - 1)] + [high_ref[...]]
-    first, last = conv_edges(shift_ref, weights_ref, slabs)
-    grad_ref[0] = first
-    grad_ref[1] = last
-    edge_ref[0] = shift_ref[:, 0]
-    edge_ref[1] = shift_ref[:, 5]
-
-
-def edge_gradient(dense, low, high, weights):
-    channels = dense.shape[2]
-    return call(
-        edge_gradient_body,
-        [
-            jax.ShapeDtypeStruct((2, SLAB, channels), F32),
-            jax.ShapeDtypeStruct((2, 3, SHIFTED, channels), BF),
-        ],
-        [dense, low, high, weights],
-        scratch=[pltpu.VMEM((3, 6, SHIFTED, channels), BF)],
-        flops=4 * SLAB * KOFF * channels * channels,
-    )
+    )[0]
 
 
 def upright(turned):
@@ -306,7 +271,7 @@
             pltpu.SemaphoreType.DMA((2,)),
         ],
         flops=2 * INNER * SLAB * KOFF * channels * channels,
-        limit=58,
+        limit=20,
     )[0]
 
 
@@ -357,7 +322,7 @@
             pltpu.SemaphoreType.DMA((4,)),
         ],
         flops=4 * SLAB * KOFF * channels * channels,
-        limit=58,
+        limit=20,
     )[0]
 
 
@@ -399,27 +364,36 @@
 
 
 def voxel_body(
-    cap_rows, scaling, adj_ref, msg_ref, shift_far, grad_far, edge_shift_far, edge_grad_far,
-    turned_far, low_ref, high_ref, back_far, keep_ref, send_ref,
-    table_ref, feats_ref, pick_ref, all_ref, shift_ref, grad_ref, turned_ref, back_ref, sems,
+    cap_rows, scaling,
+    adj_far, msg_far, below_far, above_far, dense_far, weights_far, grad_far,
+    turned_far, low_far, high_far, back_far, keep_far, send_far,
+    adj_ref, msg_ref, below_ref, above_ref, dense_ref, weights_ref, grad_ref,
+    turned_ref, back_ref,
+    table_ref, feats_ref, pick_ref, all_ref, shift_ref, in_sems, out_sems,
 ):
-    grad_pairs = (
+    pairs = (
+        (adj_far, adj_ref),
+        (msg_far, msg_ref),
+        (below_far, below_ref),
+        (above_far, above_ref),
+        (dense_far, dense_ref),
+        (weights_far, weights_ref),
         (grad_far, grad_ref.at[1 : NX - 1]),
-        (edge_grad_far.at[0], grad_ref.at[0]),
-        (edge_grad_far.at[1], grad_ref.at[NX - 1]),
-    )
-    shift_pairs = (
-        (shift_far, shift_ref.at[:, 1 : NX + 1]),
-        (edge_shift_far.at[0], shift_ref.at[:, 0]),
-        (edge_shift_far.at[1], shift_ref.at[:, NX + 1]),
-    )
-    copies = [
-        pltpu.make_async_copy(a, b, sems.at[2 + i]) for i, (a, b) in enumerate(grad_pairs + shift_pairs)
-    ]
+    )
+    copies = [pltpu.make_async_copy(a, b, in_sems.at[i]) for i, (a, b) in enumerate(pairs)]
     for copy in copies:
         copy.start()
     regions, rows, channels = msg_ref.shape
     total = regions * cap_rows
+    for copy in copies[2:]:
+        copy.wait()
+    slabs = [below_ref[...]] + [dense_ref[x] for x in range(NX)] + [above_ref[...]]
+    for x, slab in enumerate(slabs):
+        put_shifts(shift_ref, x, slab)
+    for x in (0, NX - 1):
+        grad_ref[x] = conv_slab(shift_ref, weights_ref, x)
+    copies[0].wait()
+    copies[1].wait()
     columns = read_slots(cap_rows, adj_ref, msg_ref, table_ref)
     for r in range(regions):
         feats_ref[r * cap_rows : (r + 1) * cap_rows, :] = msg_ref[r, 0:cap_rows, :]
@@ -427,18 +401,25 @@
     flipped = jnp.transpose(feats_ref[...].astype(F32)).astype(BF)
     left = jnp.concatenate([flipped, jnp.ones((16, total), BF)], axis=0)
     width = 2 * LANES
-    for copy in copies[:3]:
-        copy.wait()
     for q in range(0, DENSE, width):
         part = jnp.dot(left, pick_ref[:, q : q + width], preferred_element_type=F32)
         denom = jnp.maximum(part[channels : channels + 8], 1.0)
         turned_ref[:, q : q + width] = (part[0:channels] / denom[0:1]).astype(BF)
         x = q // SLAB
         grad_ref[x] = grad_ref[x] / jnp.transpose(denom)[:, 0:1]
-    turned_out = pltpu.make_async_copy(turned_ref, turned_far, sems.at[0])
-    turned_out.start()
-    low_ref[...] = turned_ref[:, 0:SLAB]
-    high_ref[...] = turned_ref[:, DENSE - SLAB : DENSE]
+    core = lax.rem(lax.axis_index("region"), 2)
+    half = keep_far.shape[0]
+    outs = (
+        (turned_ref, turned_far),
+        (turned_ref.at[:, 0:SLAB], low_far),
+        (turned_ref.at[:, DENSE - SLAB : DENSE], high_far),
+        (back_ref, back_far),
+        (all_ref.at[pl.ds(pl.multiple_of(core * half, 16), half)], keep_far),
+        (all_ref.at[pl.ds(pl.multiple_of((1 - core) * half, 16), half)], send_far),
+    )
+    results = [pltpu.make_async_copy(a, b, out_sems.at[i]) for i, (a, b) in enumerate(outs)]
+    for copy in results[:3]:
+        copy.start()
     voxel_grad = grad_ref[...].reshape(DENSE, channels).astype(BF)
     group = regions // 4
     for r in range(0, regions, group):
@@ -447,11 +428,8 @@
         ).astype(BF)
         for i in range(group):
             back_ref[r + i] = picked[i * cap_rows : (i + 1) * cap_rows]
-    back_out = pltpu.make_async_copy(back_ref, back_far, sems.at[1])
-    back_out.start()
+    results[3].start()
     left = turned_ref[...]
-    for copy in copies[3:]:
-        copy.wait()
     for k in range(0, KOFF, 2):
         pieces = []
         for j in range(k, min(k + 2, KOFF)):
@@ -463,47 +441,52 @@
         for i in range(len(pieces)):
             at = (KOFF - 1 - k - i) * channels
             all_ref[at : at + channels, :] = term[:, i * channels : (i + 1) * channels]
-    core = lax.rem(lax.axis_index("region"), 2)
-    half = keep_ref.shape[0]
-    keep_ref[...] = all_ref[pl.ds(pl.multiple_of(core * half, 16), half), :]
-    send_ref[...] = all_ref[pl.ds(pl.multiple_of((1 - core) * half, 16), half), :].astype(BF)
-    turned_out.wait()
-    back_out.wait()
-
-
-def voxels(adjacency, msg, shifts, grad, edge_shifts, edge_grad, cap_rows, scaling):
+    results[4].start()
+    results[5].start()
+    for copy in results:
+        copy.wait()
+
+
+def voxels(adjacency, msg, below, above, dense, weights, grad, cap_rows, scaling):
     regions, rows, channels = msg.shape
     segs = up_to(cap_rows, LANES) // LANES
     total = regions * cap_rows
+    half = (KOFF * channels // 2, channels)
+    turned, back = (channels, DENSE), (regions, cap_rows, channels)
     face = jax.ShapeDtypeStruct((channels, SLAB), BF)
-    half = (KOFF * channels // 2, channels)
     return call(
         functools.partial(voxel_body, cap_rows, scaling),
         [
-            jax.ShapeDtypeStruct((channels, DENSE), BF),
+            jax.ShapeDtypeStruct(turned, BF),
             face,
             face,
-            jax.ShapeDtypeStruct((regions, cap_rows, channels), BF),
+            jax.ShapeDtypeStruct(back, BF),
             jax.ShapeDtypeStruct(half, F32),
-            jax.ShapeDtypeStruct(half, BF),
+            jax.ShapeDtypeStruct(half, F32),
         ],
-        [adjacency, msg, shifts, grad, edge_shifts, edge_grad],
-        smem=(0,),
-        far=(2, 3, 4, 5),
-        far_outs=(0, 3),
+        [adjacency, msg, below, above, dense, weights, grad],
+        far=range(7),
+        far_outs=range(6),
         scratch=[
+            pltpu.SMEM(adjacency.shape, jnp.int32),
+            pltpu.VMEM(msg.shape, BF),
+            pltpu.VMEM(below.shape, BF),
+            pltpu.VMEM(above.shape, BF),
+            pltpu.VMEM(dense.shape, BF),
+            pltpu.VMEM(weights.shape, BF),
+            pltpu.VMEM((NX, SLAB, channels), F32),
+            pltpu.VMEM(turned, BF),
+            pltpu.VMEM(back, BF),
             pltpu.VMEM((2 * regions, segs * LANES), F32),
             pltpu.VMEM((total, channels), BF),
             pltpu.VMEM((total, DENSE), BF),
             pltpu.VMEM((KOFF * channels, channels), F32),
             pltpu.VMEM((3, NX + 2, SHIFTED, channels), BF),
-            pltpu.VMEM((NX, SLAB, channels), F32),
-            pltpu.VMEM((channels, DENSE), BF),
-            pltpu.VMEM((regions, cap_rows, channels), BF),
-            pltpu.SemaphoreType.DMA((8,)),
+            pltpu.SemaphoreType.DMA((7,)),
+            pltpu.SemaphoreType.DMA((6,)),
         ],
         flops=2 * DENSE * (KOFF * channels + 2 * total) * channels,
-        limit=60,
+        limit=VOXEL_LIMIT,
     )
 
 
@@ -513,7 +496,7 @@
     side = lax.rem(lax.axis_index("region") // 2, size)
     for i in range(size):
         part = pl.ds(pl.multiple_of((side ^ i) * rows, 16), rows)
-        total = keep_ref[part, :] + got_ref[part, :].astype(F32)
+        total = keep_ref[part, :] + got_ref[part, :]
         if i == 0:
             own_ref[...] = total
         else:
@@ -586,6 +569,16 @@
     return sum_group(parts[0], [part.astype(BF) for part in parts[1:]], bit)
 
 
+def exchange_group(term, bit, size, beside):
+    side = (lax.axis_index("region") // bit) % size
+    term, beside = lax.optimization_barrier((term.astype(BF), beside))
+    terms = gather_group(term, bit, size)
+    total = lax.select_n(side, *terms).astype(F32)
+    for q in range(1, size):
+        total = total + lax.select_n(side ^ q, *terms).astype(F32)
+    return total.astype(BF), beside
+
+
 def sum_group(total, sent, bit):
     for i, part in enumerate(sent):
         total = total + swapped(part, bit * (i + 1)).astype(F32)
@@ -642,32 +635,35 @@
     cot, cot_low, cot_high = to_dense(adjacency, cotangent)
     below, above = from_sides(cot_low, cot_high)
     mirrored = jnp.transpose(kernel[::-1], (0, 2, 1)).reshape(KOFF * channels, channels)
-    grad, shifts = inner_gradient(cot, mirrored)
-    edge_grad, edge_shifts = edge_gradient(cot, below, above, mirrored)
+    grad = inner_gradient(cot, mirrored)
     scaling = 1.0 / math.sqrt(tiles * regions * vox)
     turned, low, high, back, keep, send = voxels(
-        adjacency, received, shifts, grad, edge_shifts, edge_grad, cap_rows, scaling
+        adjacency, received, below, above, cot, mirrored, grad, cap_rows, scaling
     )
     returned = exchange(back)
     groups = groups_of(regions)
     bit, size = groups[0]
     term, *sent = split(keep, swapped(send, 1), size)
     weights = kernel.reshape(KOFF * channels, channels)
-    turned, *sent = lax.optimization_barrier((turned, *sent))
+    turned, low, high, *sent = lax.optimization_barrier((turned, low, high, *sent))
+    feats_below, feats_above = from_sides(low, high)
     inner = inner_forward(turned, weights)
     term = sum_group(term, sent, bit)
-    term, returned, inner = lax.optimization_barrier((term, returned, inner))
-    for bit, size in groups[1:]:
+    term, returned, inner, feats_below, feats_above = lax.optimization_barrier(
+        (term, returned, inner, feats_below, feats_above)
+    )
+    for bit, size in groups[1:-1]:
         term = reduce_group(term, bit, size)
-    term, low, high = lax.optimization_barrier((term.astype(BF), low, high))
-    feats_below, feats_above = from_sides(low, high)
+    bit, size = groups[-1]
+    term, returned = exchange_group(term, bit, size, returned)
     grad_points = unpack(place, returned, points)
-    out_tiles = edge_forward(adjacency, turned, feats_below, feats_above, weights, inner, tiles)
-    for bit, size in groups[:0:-1]:
+    for bit, size in groups[-2:0:-1]:
         side = (lax.axis_index("region") // bit) % size
         term = in_order(gather_group(term, bit, size), side)
+    term, grad_points = lax.optimization_barrier((term, grad_points))
+    out_tiles = edge_forward(adjacency, turned, feats_below, feats_above, weights, inner, tiles)
     own = jnp.stack(gather_group(term, *groups[0]))
-    own, out_tiles, grad_points = lax.optimization_barrier((own, out_tiles, grad_points))
+    own, out_tiles = lax.optimization_barrier((own, out_tiles))
     grad_weight = last_step(own, swapped(own, 1)).reshape(KOFF, channels, channels)
     return out_tiles, grad_points, grad_weight
 

time: 100 us -> 88.6 us (0.89)
  starting transfers between devices: 37 us -> 30.4 us
  Pallas kernels: 37.9 us -> 33 us
  waiting for transfers between devices: 17.4 us -> 21.2 us
  local copies, waits for them, and re-layouts: 5.06 us -> 2.35 us
    all_to_all x2, waiting for transfers between devices: 1.59 us -> 6.74 us  [exchange(): lax.all_to_all(array, 'region', split_axis=0, concat_axis=0, tiled=True)]
    pallas_call x10 -> x9, Pallas kernels: 37.9 us -> 33 us  [call(): pl.pallas_call(body, out_shape=outs, in_specs=[SMEM if i in smem else FAR...]
    ppermute x10 -> x9, starting transfers between devices: 15.4 us -> 10.7 us  [swapped(): return lax.ppermute(array, 'region', [(i, i ^ bit) for i in range(count)])]
    unnamed x28 -> x30, local copies, waits for them, and re-layouts: 3.31 us -> 0.95 us
    all_to_all x2, starting transfers between devices: 15.5 us -> 13.3 us  [exchange(): lax.all_to_all(array, 'region', split_axis=0, concat_axis=0, tiled=True)]
    ppermute x10 -> x9, waiting for transfers between devices: 15.6 us -> 14.5 us  [swapped(): return lax.ppermute(array, 'region', [(i, i ^ bit) for i in range(count)])]
  transfers between devices with their start and end apart: 16 -> 15, of which waited for: 8 -> 6; matrix products, arithmetic and copies ran while one was open for 2% -> 2% of each run, Pallas kernels for 22% -> 17%
where the time goes in v2:
time: 88.6 us; the launch traced here: 88.1 us
  Pallas kernels  33 us (37%)
  starting transfers between devices  30.4 us (34%)
  waiting for transfers between devices  21.2 us (24%)
  local copies, waits for them, and re-layouts  2.35 us (3%)
  between operations  1 us (1%)
    pallas_call x9, Pallas kernels, call(): pl.pallas_call(body, out_shape=outs, in_specs=[SMEM if i in smem else FAR...  33 us
    ppermute x9, waiting for transfers between devices, swapped(): return lax.ppermute(array, 'region', [(i, i ^ bit) for i in range(count)])  14.5 us
    all_to_all x2, starting transfers between devices, exchange(): lax.all_to_all(array, 'region', split_axis=0, concat_axis=0, tiled=True)  13.3 us
    ppermute x9, starting transfers between devices, swapped(): return lax.ppermute(array, 'region', [(i, i ^ bit) for i in range(count)])  10.7 us
    all_to_all x2, waiting for transfers between devices, exchange(): lax.all_to_all(array, 'region', split_axis=0, concat_axis=0, tiled=True)  6.74 us
    ppermute x4, starting transfers between devices, from_sides(): return (lax.ppermute(high, 'region', up), lax.ppermute(low, 'region', down))  6.34 us
  transfers between devices with their start and end apart: 15, of which 6 were waited for; matrix products, arithmetic and copies ran while one was open for 2% of the time, Pallas kernels for 17%

profile of v2, /device:TPU:0, one launch (start us, length us, event | category | flops | bytes accessed | tf_op | source)
XLA Modules:
  0.0 88.1 jit_solution(17196298284015950411)
XLA Ops:
  0.7 3.6 %shard_map.85 = (bf16[16,176,128]{2,1,0:T(8,128)(2,1)}, f32[8,1024]{1,0:T(8,128)}) custom-call(s32[1,1024]{1,0:T(1,128)} %bitcast.20, s32[1,1024]{1,0:T(1,128)} %bitcast.21, bf16[1024,128]{1,0:T(8,128)(2,1)} %feats_far.1), custom_call_target="tpu_custom_call" | custom-call | flops 671088640 | bytes 1024000 | tf_op jit(solution)/shard_map/pallas_call | solution.py:44
  4.3 7.4 %all-to-all-start = ((bf16[16,176,128]{2,1,0:T(8,128)(2,1)}), bf16[16,176,128]{2,1,0:T(8,128)(2,1)}, u32[]{:S(2)}, u32[]{:S(2)}) async-start(bf16[16,176,128]{2,1,0:T(8,128)(2,1)} %get-tuple-element.35), calls=%async_computation | async-start | bytes 1441792 | tf_op jit(solution)/shard_map/all_to_all | solution.py:622
  11.7 0.9 shard_map.86
  12.6 2.3 %collective-permute-start = (bf16[256,128]{1,0:T(8,128)(2,1)S(1)}, bf16[256,128]{1,0:T(8,128)(2,1)S(1)}, u32[]{:S(2)}, u32[]{:S(2)}) collective-permute-start(bf16[256,128]{1,0:T(8,128)(2,1)S(1)} %get-tuple-element.36), channel_id=1, source_target_pairs={{0,1},{1,2},{2,3},{3,4},{4,5},{5,6},{6,7},{7,8},{8,9},{9,10},{10,1... | collective-permute-start | bytes 196616 | tf_op jit(solution)/shard_map/ppermute | solution.py:551
  14.9 1.3 %collective-permute-start.1 = (bf16[256,128]{1,0:T(8,128)(2,1)S(1)}, bf16[256,128]{1,0:T(8,128)(2,1)S(1)}, u32[]{:S(2)}, u32[]{:S(2)}) collective-permute-start(bf16[256,128]{1,0:T(8,128)(2,1)S(1)} %get-tuple-element.37), channel_id=1, source_target_pairs={{1,0},{2,1},{3,2},{4,3},{5,4},{6,5},{7,6},{8,7},{9,8},{10,9},{11,1... | collective-permute-start | bytes 196616 | tf_op jit(solution)/shard_map/ppermute | solution.py:551
  16.2 0.1 reverse_bitcast_fusion
  16.3 1.3 %copy.9 = bf16[27,128,128]{2,1,0:T(8,128)(2,1)S(1)} copy(bf16[27,128,128]{1,2,0:T(8,128)(2,1)S(1)} %reverse_bitcast_fusion) | data formatting | bytes 1769472 | tf_op jit(solution)/shard_map/transpose | solution.py:637
  17.7 4.1 %shard_map.87.grad_far = f32[6,256,128]{2,1,0:T(8,128)S(1)} custom-call(bf16[8,256,128]{2,1,0:T(8,128)(2,1)S(1)} %get-tuple-element.38.dense_ref.dense_far, bf16[3456,128]{1,0:T(8,128)(2,1)S(1)} %bitcast.13), custom_call_target="tpu_custom_call" | custom-call | flops 1358954496 | bytes 2195456 | tf_op jit(solution)/shard_map/pallas_call | solution.py:44
  21.8 0.9 %copy-done.9 = f32[6,256,128]{2,1,0:T(8,128)} copy-done((f32[6,256,128]{2,1,0:T(8,128)}, f32[6,256,128]{2,1,0:T(8,128)S(1)}, u32[]{:S(2)}) %copy-start.9) | copy-done | bytes 786456
  22.7 6.7 %all-to-all-done.msg_far = bf16[16,176,128]{2,1,0:T(8,128)(2,1)} async-done(((bf16[16,176,128]{2,1,0:T(8,128)(2,1)}), bf16[16,176,128]{2,1,0:T(8,128)(2,1)}, u32[]{:S(2)}, u32[]{:S(2)}) %all-to-all-start) | async-done | bytes 720928 | tf_op jit(solution)/shard_map/all_to_all | solution.py:622
  29.4 12.9 %shard_map.88 = (bf16[128,2048]{1,0:T(8,128)(2,1)}, bf16[128,256]{1,0:T(8,128)(2,1)}, bf16[128,256]{1,0:T(8,128)(2,1)}, bf16[16,160,128]{2,1,0:T(8,128)(2,1)}, f32[1728,128]{1,0:T(8,128)}, /*index=5*/f32[1728,128]{1,0:T(8,128)}) custom-call(s32[16,27]{1,0:T(8,128)} %adj_ref.3, bf16[16,176,128]{2,1,0:T(8,128)(2,1)} %all-to-all-done.msg_far, ...), custom_call_target="tpu_custom_call" | custom-call | flops 4496293888 | bytes 6129344 | tf_op jit(solution)/shard_map/pallas_call | solution.py:44
  42.4 0.2 collective-permute-start.2
  42.7 5.9 %all-to-all-start.1 = ((bf16[16,160,128]{2,1,0:T(8,128)(2,1)}), bf16[16,160,128]{2,1,0:T(8,128)(2,1)S(1)}, u32[]{:S(2)}, u32[]{:S(2)}) async-start(bf16[16,160,128]{2,1,0:T(8,128)(2,1)} %get-tuple-element.51), calls=%async_computation.1 | async-start | bytes 1310720 | tf_op jit(solution)/shard_map/all_to_all | solution.py:622
  48.6 0.1 shard_map.89
  48.7 2.0 %collective-permute-start.3 = (bf16[432,128]{1,0:T(8,128)(2,1)S(1)}, bf16[432,128]{1,0:T(8,128)(2,1)S(1)}, u32[]{:S(2)}, u32[]{:S(2)}) collective-permute-start(bf16[432,128]{1,0:T(8,128)(2,1)S(1)} %get-tuple-element.48), channel_id=1, source_target_pairs={{0,2},{1,3},{2,0},{3,1},{4,6},{5,7},{6,4},{7,5},{8,10},{9,11},{10,... | collective-permute-start | bytes 331784 | tf_op jit(solution)/shard_map/ppermute | solution.py:556
  50.7 1.5 %collective-permute-start.4 = (bf16[432,128]{1,0:T(8,128)(2,1)S(1)}, bf16[432,128]{1,0:T(8,128)(2,1)S(1)}, u32[]{:S(2)}, u32[]{:S(2)}) collective-permute-start(bf16[432,128]{1,0:T(8,128)(2,1)S(1)} %get-tuple-element.49), channel_id=1, source_target_pairs={{0,4},{1,5},{2,6},{3,7},{4,0},{5,1},{6,2},{7,3},{8,12},{9,13},{10,... | collective-permute-start | bytes 331784 | tf_op jit(solution)/shard_map/ppermute | solution.py:556
  52.2 0.1 collective-permute-start.5
  52.3 1.5 %collective-permute-start.6 = (bf16[128,256]{1,0:T(8,128)(2,1)S(1)}, bf16[128,256]{1,0:T(8,128)(2,1)S(1)}, u32[]{:S(2)}, u32[]{:S(2)}) collective-permute-start(bf16[128,256]{1,0:T(8,128)(2,1)S(1)} %copy-done.12), channel_id=1, source_target_pairs={{0,1},{1,2},{2,3},{3,4},{4,5},{5,6},{6,7},{7,8},{8,9},{9,10},{10,1... | collective-permute-start | bytes 196616 | tf_op jit(solution)/shard_map/ppermute | solution.py:551
  53.8 1.3 %collective-permute-start.7 = (bf16[128,256]{1,0:T(8,128)(2,1)S(1)}, bf16[128,256]{1,0:T(8,128)(2,1)S(1)}, u32[]{:S(2)}, u32[]{:S(2)}) collective-permute-start(bf16[128,256]{1,0:T(8,128)(2,1)S(1)} %copy-done.11), channel_id=1, source_target_pairs={{1,0},{2,1},{3,2},{4,3},{5,4},{6,5},{7,6},{8,7},{9,8},{10,9},{11,1... | collective-permute-start | bytes 196616 | tf_op jit(solution)/shard_map/ppermute | solution.py:551
  55.1 4.4 %shard_map.90.inner_far = bf16[6,256,128]{2,1,0:T(8,128)(2,1)S(1)} custom-call(bf16[128,2048]{1,0:T(8,128)(2,1)S(1)} %copy-done.3, bf16[3456,128]{1,0:T(8,128)(2,1)S(1)} %bitcast.11), custom_call_target="tpu_custom_call" | custom-call | flops 1358954496 | bytes 1802240 | tf_op jit(solution)/shard_map/pallas_call | solution.py:44
  59.5 5.3 %collective-permute-done.4 = bf16[432,128]{1,0:T(8,128)(2,1)S(1)} collective-permute-done((bf16[432,128]{1,0:T(8,128)(2,1)S(1)}, bf16[432,128]{1,0:T(8,128)(2,1)S(1)}, u32[]{:S(2)}, u32[]{:S(2)}) %collective-permute-start.4) | collective-permute-done | bytes 110624 | tf_op jit(solution)/shard_map/ppermute | solution.py:556
  64.8 3.1 %collective-permute-done.5 = bf16[432,128]{1,0:T(8,128)(2,1)S(1)} collective-permute-done((bf16[432,128]{1,0:T(8,128)(2,1)S(1)}, bf16[432,128]{1,0:T(8,128)(2,1)S(1)}, u32[]{:S(2)}, u32[]{:S(2)}) %collective-permute-start.5) | collective-permute-done | bytes 110624 | tf_op jit(solution)/shard_map/ppermute | solution.py:556
  68.0 3.3 %collective-permute-start.8 = (bf16[432,128]{1,0:T(8,128)(2,1)S(1)}, bf16[432,128]{1,0:T(8,128)(2,1)S(1)}, u32[]{:S(2)}, u32[]{:S(2)}) collective-permute-start(bf16[432,128]{1,0:T(8,128)(2,1)S(1)} %convert_add_fusion), channel_id=1, source_target_pairs={{0,8},{1,9},{2,10},{3,11},{4,12},{5,13},{6,14},{7,15},{8,0},{9,1},... | collective-permute-start | bytes 331784 | tf_op jit(solution)/shard_map/ppermute | solution.py:556
  71.3 2.4 %shard_map.91 = bf16[1024,128]{1,0:T(8,128)(2,1)} custom-call(f32[8,1024]{1,0:T(8,128)S(1)} %copy-done.10, bf16[16,160,128]{2,1,0:T(8,128)(2,1)S(1)} %all-to-all-done.1.rows_ref), custom_call_target="tpu_custom_call" | custom-call | flops 671088640 | bytes 950272 | tf_op jit(solution)/shard_map/pallas_call | solution.py:44
  73.7 2.5 %collective-permute-done.8 = bf16[432,128]{1,0:T(8,128)(2,1)S(1)} collective-permute-done((bf16[432,128]{1,0:T(8,128)(2,1)S(1)}, bf16[432,128]{1,0:T(8,128)(2,1)S(1)}, u32[]{:S(2)}, u32[]{:S(2)}) %collective-permute-start.8) | collective-permute-done | bytes 110624 | tf_op jit(solution)/shard_map/ppermute | solution.py:556
  76.3 1.0 %collective-permute-start.9 = (bf16[432,128]{1,0:T(8,128)(2,1)S(1)}, bf16[432,128]{1,0:T(8,128)(2,1)S(1)}, u32[]{:S(2)}, u32[]{:S(2)}) collective-permute-start(bf16[432,128]{1,0:T(8,128)(2,1)S(1)} %add_convert_fusion), channel_id=1, source_target_pairs={{0,2},{1,3},{2,0},{3,1},{4,6},{5,7},{6,4},{7,5},{8,10},{9,11},{10,... | collective-permute-start | bytes 331784 | tf_op jit(solution)/shard_map/ppermute | solution.py:556
  77.3 2.5 %collective-permute-start.11 = (bf16[432,128]{1,0:T(8,128)(2,1)S(1)}, bf16[432,128]{1,0:T(8,128)(2,1)S(1)}, u32[]{:S(2)}, u32[]{:S(2)}) collective-permute-start(bf16[432,128]{1,0:T(8,128)(2,1)S(1)} %add_convert_fusion), channel_id=1, source_target_pairs={{0,6},{1,7},{2,4},{3,5},{4,2},{5,3},{6,0},{7,1},{8,14},{9,15},{10,... | collective-permute-start | bytes 331784 | tf_op jit(solution)/shard_map/ppermute | solution.py:556
  79.9 3.2 %shard_map.92 = bf16[16,128,128]{2,1,0:T(8,128)(2,1)} custom-call(s32[16,27]{1,0:T(8,128)S(1)} %copy-done.7, bf16[128,2048]{1,0:T(8,128)(2,1)S(1)} %copy-done.4, bf16[128,256]{1,0:T(8,128)(2,1)S(1)} %collective-permute-done.6.low_ref, bf16[128,256]{1,0:T(8,128)(2,1)S(1)} %collective-permute-done.7.high_ref, bf16[3456,128]{1,0:T(8,128)(2,1)S(1)} %bitcast.12, ...), custom_call_target="tpu_custom_call" | custom-call | flops 452984832 | bytes 2459328 | tf_op jit(solution)/shard_map/pallas_call | solution.py:44
  83.1 1.8 %collective-permute-done.11 = bf16[432,128]{1,0:T(8,128)(2,1)S(1)} collective-permute-done((bf16[432,128]{1,0:T(8,128)(2,1)S(1)}, bf16[432,128]{1,0:T(8,128)(2,1)S(1)}, u32[]{:S(2)}, u32[]{:S(2)}) %collective-permute-start.11) | collective-permute-done | bytes 110624 | tf_op jit(solution)/shard_map/ppermute | solution.py:556
  84.9 0.1 collective-permute-start.12
  85.0 1.8 %collective-permute-done.12.other_ref = bf16[4,432,128]{2,1,0:T(8,128)(2,1)S(1)} collective-permute-done((bf16[4,432,128]{2,1,0:T(8,128)(2,1)S(1)}, bf16[4,432,128]{2,1,0:T(8,128)(2,1)S(1)}, u32[]{:S(2)}, u32[]{:S(2)}) %collective-permute-start.12) | collective-permute-done | bytes 442400 | tf_op jit(solution)/shard_map/ppermute | solution.py:556
  86.8 1.3 %shard_map.93 = f32[3456,128]{1,0:T(8,128)} custom-call(bf16[4,432,128]{2,1,0:T(8,128)(2,1)S(1)} %pad_maximum_fusion.own_ref, bf16[4,432,128]{2,1,0:T(8,128)(2,1)S(1)} %collective-permute-done.12.other_ref), custom_call_target="tpu_custom_call" | custom-call | bytes 2654208 | tf_op jit(solution)/shard_map/pallas_call | solution.py:44
  (42 shorter events, 0.3 us)
Async XLA Ops:
  0.6 11.1 %copy-start.5 = (bf16[16,128,128]{2,1,0:T(8,128)(2,1)S(1)}, bf16[16,128,128]{2,1,0:T(8,128)(2,1)}, u32[]{:S(2)}) copy-start(bf16[16,128,128]{2,1,0:T(8,128)(2,1)} %bricks_ref.1) | copy-start | bytes 1572868
  0.6 11.1 %copy-start.6 = (s32[16,27]{1,0:T(8,128)S(1)}, s32[16,27]{1,0:T(8,128)}, u32[]{:S(2)}) copy-start(s32[16,27]{1,0:T(8,128)} %adj_ref.3) | copy-start | bytes 5188
  0.7 15.6 %copy-start = (bf16[27,128,128]{2,1,0:T(8,128)(2,1)S(1)}, bf16[27,128,128]{2,1,0:T(8,128)(2,1)}, u32[]{:S(2)}) copy-start(bf16[27,128,128]{2,1,0:T(8,128)(2,1)} %param.10) | copy-start | bytes 2654212
  4.3 25.1 %all-to-all-start = ((bf16[16,176,128]{2,1,0:T(8,128)(2,1)}), bf16[16,176,128]{2,1,0:T(8,128)(2,1)}, u32[]{:S(2)}, u32[]{:S(2)}) async-start(bf16[16,176,128]{2,1,0:T(8,128)(2,1)} %get-tuple-element.35), calls=%async_computation | async-start | bytes 1441792 | tf_op jit(solution)/shard_map/all_to_all | solution.py:622
  12.6 5.0 %copy-start.8 = (bf16[8,256,128]{2,1,0:T(8,128)(2,1)}, bf16[8,256,128]{2,1,0:T(8,128)(2,1)S(1)}, u32[]{:S(2)}) copy-start(bf16[8,256,128]{2,1,0:T(8,128)(2,1)S(1)} %get-tuple-element.38.dense_ref.dense_far) | copy-start | bytes 1572868
  12.6 10.0 %collective-permute-start = (bf16[256,128]{1,0:T(8,128)(2,1)S(1)}, bf16[256,128]{1,0:T(8,128)(2,1)S(1)}, u32[]{:S(2)}, u32[]{:S(2)}) collective-permute-start(bf16[256,128]{1,0:T(8,128)(2,1)S(1)} %get-tuple-element.36), channel_id=1, source_target_pairs={{0,1},{1,2},{2,3},{3,4},{4,5},{5,6},{6,7},{7,8},{8,9},{9,10},{10,1... | collective-permute-start | bytes 196616 | tf_op jit(solution)/shard_map/ppermute | solution.py:551
  14.9 7.8 %collective-permute-start.1 = (bf16[256,128]{1,0:T(8,128)(2,1)S(1)}, bf16[256,128]{1,0:T(8,128)(2,1)S(1)}, u32[]{:S(2)}, u32[]{:S(2)}) collective-permute-start(bf16[256,128]{1,0:T(8,128)(2,1)S(1)} %get-tuple-element.37), channel_id=1, source_target_pairs={{1,0},{2,1},{3,2},{4,3},{5,4},{6,5},{7,6},{8,7},{9,8},{10,9},{11,1... | collective-permute-start | bytes 196616 | tf_op jit(solution)/shard_map/ppermute | solution.py:551
  17.6 4.1 %copy-start.2 = (bf16[27,128,128]{2,1,0:T(8,128)(2,1)}, bf16[27,128,128]{2,1,0:T(8,128)(2,1)S(1)}, u32[]{:S(2)}) copy-start(bf16[27,128,128]{2,1,0:T(8,128)(2,1)S(1)} %copy.9) | copy-start | bytes 2654212
  21.8 0.9 %copy-start.9 = (f32[6,256,128]{2,1,0:T(8,128)}, f32[6,256,128]{2,1,0:T(8,128)S(1)}, u32[]{:S(2)}) copy-start(f32[6,256,128]{2,1,0:T(8,128)S(1)} %shard_map.87.grad_far) | copy-start | bytes 2359300
  22.7 6.8 %copy-start.13 = (bf16[256,128]{1,0:T(8,128)(2,1)}, bf16[256,128]{1,0:T(8,128)(2,1)S(1)}, u32[]{:S(2)}) copy-start(bf16[256,128]{1,0:T(8,128)(2,1)S(1)} %collective-permute-done.below_far) | copy-start | bytes 196612
  22.7 6.8 %copy-start.14 = (bf16[256,128]{1,0:T(8,128)(2,1)}, bf16[256,128]{1,0:T(8,128)(2,1)S(1)}, u32[]{:S(2)}) copy-start(bf16[256,128]{1,0:T(8,128)(2,1)S(1)} %collective-permute-done.1.above_far) | copy-start | bytes 196612
  42.4 6.2 %copy-start.1 = (f32[1728,128]{1,0:T(8,128)S(1)}, f32[1728,128]{1,0:T(8,128)}, u32[]{:S(2)}) copy-start(f32[1728,128]{1,0:T(8,128)} %get-tuple-element.39.keep_ref) | copy-start | bytes 2654212
  42.4 9.9 %copy-start.12 = (bf16[128,256]{1,0:T(8,128)(2,1)S(1)}, bf16[128,256]{1,0:T(8,128)(2,1)}, u32[]{:S(2)}) copy-start(bf16[128,256]{1,0:T(8,128)(2,1)} %get-tuple-element.53) | copy-start | bytes 196612
  42.4 11.4 %copy-start.11 = (bf16[128,256]{1,0:T(8,128)(2,1)S(1)}, bf16[128,256]{1,0:T(8,128)(2,1)}, u32[]{:S(2)}) copy-start(bf16[128,256]{1,0:T(8,128)(2,1)} %get-tuple-element.54) | copy-start | bytes 196612
  42.4 6.2 %collective-permute-start.2 = (f32[1728,128]{1,0:T(8,128)}, f32[1728,128]{1,0:T(8,128)S(1)}, u32[]{:S(2)}, u32[]{:S(2)}) collective-permute-start(f32[1728,128]{1,0:T(8,128)} %get-tuple-element.40), channel_id=1, source_target_pairs={{0,1},{1,0},{2,3},{3,2},{4,5},{5,4},{6,7},{7,6},{8,9},{9,8},{10,11... | collective-permute-start | bytes 2654216 | tf_op jit(solution)/shard_map/ppermute | solution.py:556
  42.7 25.3 %all-to-all-start.1 = ((bf16[16,160,128]{2,1,0:T(8,128)(2,1)}), bf16[16,160,128]{2,1,0:T(8,128)(2,1)S(1)}, u32[]{:S(2)}, u32[]{:S(2)}) async-start(bf16[16,160,128]{2,1,0:T(8,128)(2,1)} %get-tuple-element.51), calls=%async_computation.1 | async-start | bytes 1310720 | tf_op jit(solution)/shard_map/all_to_all | solution.py:622
  48.6 6.5 %copy-start.3 = (bf16[128,2048]{1,0:T(8,128)(2,1)S(1)}, bf16[128,2048]{1,0:T(8,128)(2,1)}, u32[]{:S(2)}) copy-start(bf16[128,2048]{1,0:T(8,128)(2,1)} %get-tuple-element.52.turned_far) | copy-start | bytes 1572868
  48.7 10.8 %collective-permute-start.3 = (bf16[432,128]{1,0:T(8,128)(2,1)S(1)}, bf16[432,128]{1,0:T(8,128)(2,1)S(1)}, u32[]{:S(2)}, u32[]{:S(2)}) collective-permute-start(bf16[432,128]{1,0:T(8,128)(2,1)S(1)} %get-tuple-element.48), channel_id=1, source_target_pairs={{0,2},{1,3},{2,0},{3,1},{4,6},{5,7},{6,4},{7,5},{8,10},{9,11},{10,... | collective-permute-start | bytes 331784 | tf_op jit(solution)/shard_map/ppermute | solution.py:556
  50.7 14.0 %collective-permute-start.4 = (bf16[432,128]{1,0:T(8,128)(2,1)S(1)}, bf16[432,128]{1,0:T(8,128)(2,1)S(1)}, u32[]{:S(2)}, u32[]{:S(2)}) collective-permute-start(bf16[432,128]{1,0:T(8,128)(2,1)S(1)} %get-tuple-element.49), channel_id=1, source_target_pairs={{0,4},{1,5},{2,6},{3,7},{4,0},{5,1},{6,2},{7,3},{8,12},{9,13},{10,... | collective-permute-start | bytes 331784 | tf_op jit(solution)/shard_map/ppermute | solution.py:556
  52.2 15.7 %collective-permute-start.5 = (bf16[432,128]{1,0:T(8,128)(2,1)S(1)}, bf16[432,128]{1,0:T(8,128)(2,1)S(1)}, u32[]{:S(2)}, u32[]{:S(2)}) collective-permute-start(bf16[432,128]{1,0:T(8,128)(2,1)S(1)} %get-tuple-element.50), channel_id=1, source_target_pairs={{0,6},{1,7},{2,4},{3,5},{4,2},{5,3},{6,0},{7,1},{8,14},{9,15},{10,... | collective-permute-start | bytes 331784 | tf_op jit(solution)/shard_map/ppermute | solution.py:556
  52.3 15.7 %collective-permute-start.6 = (bf16[128,256]{1,0:T(8,128)(2,1)S(1)}, bf16[128,256]{1,0:T(8,128)(2,1)S(1)}, u32[]{:S(2)}, u32[]{:S(2)}) collective-permute-start(bf16[128,256]{1,0:T(8,128)(2,1)S(1)} %copy-done.12), channel_id=1, source_target_pairs={{0,1},{1,2},{2,3},{3,4},{4,5},{5,6},{6,7},{7,8},{8,9},{9,10},{10,1... | collective-permute-start | bytes 196616 | tf_op jit(solution)/shard_map/ppermute | solution.py:551
  53.8 14.2 %collective-permute-start.7 = (bf16[128,256]{1,0:T(8,128)(2,1)S(1)}, bf16[128,256]{1,0:T(8,128)(2,1)S(1)}, u32[]{:S(2)}, u32[]{:S(2)}) collective-permute-start(bf16[128,256]{1,0:T(8,128)(2,1)S(1)} %copy-done.11), channel_id=1, source_target_pairs={{1,0},{2,1},{3,2},{4,3},{5,4},{6,5},{7,6},{8,7},{9,8},{10,9},{11,1... | collective-permute-start | bytes 196616 | tf_op jit(solution)/shard_map/ppermute | solution.py:551
  55.1 16.2 %copy-start.10 = (f32[8,1024]{1,0:T(8,128)S(1)}, f32[8,1024]{1,0:T(8,128)}, u32[]{:S(2)}) copy-start(f32[8,1024]{1,0:T(8,128)} %get-tuple-element.58.place_ref) | copy-start | bytes 98308
  67.9 12.0 %copy-start.4 = (bf16[128,2048]{1,0:T(8,128)(2,1)S(1)}, bf16[128,2048]{1,0:T(8,128)(2,1)}, u32[]{:S(2)}) copy-start(bf16[128,2048]{1,0:T(8,128)(2,1)} %get-tuple-element.52.turned_far) | copy-start | bytes 1572868
  67.9 12.0 %copy-start.7 = (s32[16,27]{1,0:T(8,128)S(1)}, s32[16,27]{1,0:T(8,128)}, u32[]{:S(2)}) copy-start(s32[16,27]{1,0:T(8,128)} %adj_ref.3) | copy-start | bytes 5188
  68.0 8.3 %collective-permute-start.8 = (bf16[432,128]{1,0:T(8,128)(2,1)S(1)}, bf16[432,128]{1,0:T(8,128)(2,1)S(1)}, u32[]{:S(2)}, u32[]{:S(2)}) collective-permute-start(bf16[432,128]{1,0:T(8,128)(2,1)S(1)} %convert_add_fusion), channel_id=1, source_target_pairs={{0,8},{1,9},{2,10},{3,11},{4,12},{5,13},{6,14},{7,15},{8,0},{9,1},... | collective-permute-start | bytes 331784 | tf_op jit(solution)/shard_map/ppermute | solution.py:556
  76.3 6.8 %collective-permute-start.9 = (bf16[432,128]{1,0:T(8,128)(2,1)S(1)}, bf16[432,128]{1,0:T(8,128)(2,1)S(1)}, u32[]{:S(2)}, u32[]{:S(2)}) collective-permute-start(bf16[432,128]{1,0:T(8,128)(2,1)S(1)} %add_convert_fusion), channel_id=1, source_target_pairs={{0,2},{1,3},{2,0},{3,1},{4,6},{5,7},{6,4},{7,5},{8,10},{9,11},{10,... | collective-permute-start | bytes 331784 | tf_op jit(solution)/shard_map/ppermute | solution.py:556
  77.3 5.7 %collective-permute-start.10 = (bf16[432,128]{1,0:T(8,128)(2,1)S(1)}, bf16[432,128]{1,0:T(8,128)(2,1)S(1)}, u32[]{:S(2)}, u32[]{:S(2)}) collective-permute-start(bf16[432,128]{1,0:T(8,128)(2,1)S(1)} %add_convert_fusion), channel_id=1, source_target_pairs={{0,4},{1,5},{2,6},{3,7},{4,0},{5,1},{6,2},{7,3},{8,12},{9,13},{10,... | collective-permute-start | bytes 331784 | tf_op jit(solution)/shard_map/ppermute | solution.py:556
  77.3 7.5 %collective-permute-start.11 = (bf16[432,128]{1,0:T(8,128)(2,1)S(1)}, bf16[432,128]{1,0:T(8,128)(2,1)S(1)}, u32[]{:S(2)}, u32[]{:S(2)}) collective-permute-start(bf16[432,128]{1,0:T(8,128)(2,1)S(1)} %add_convert_fusion), channel_id=1, source_target_pairs={{0,6},{1,7},{2,4},{3,5},{4,2},{5,3},{6,0},{7,1},{8,14},{9,15},{10,... | collective-permute-start | bytes 331784 | tf_op jit(solution)/shard_map/ppermute | solution.py:556
  84.9 1.9 %collective-permute-start.12 = (bf16[4,432,128]{2,1,0:T(8,128)(2,1)S(1)}, bf16[4,432,128]{2,1,0:T(8,128)(2,1)S(1)}, u32[]{:S(2)}, u32[]{:S(2)}) collective-permute-start(bf16[4,432,128]{2,1,0:T(8,128)(2,1)S(1)} %pad_maximum_fusion.own_ref), channel_id=1, source_target_pairs={{0,1},{1,0},{2,3},{3,2},{4,5},{5,4},{6,7},{7,6},{8,9},{9,8},{10,11... | collective-permute-start | bytes 1327112 | tf_op jit(solution)/shard_map/ppermute | solution.py:556

commit v3 on v2

--- a/solution.py
+++ b/solution.py
@@ -20,6 +20,7 @@
 NX = SX * VX
 SLAB = NY * NZ
 DENSE = NX * SLAB
+HALF = DENSE // 2
 LANES = 128
 BF = jnp.bfloat16
 F32 = jnp.float32
@@ -27,7 +28,6 @@
 SMEM = pl.BlockSpec(memory_space=pltpu.SMEM)
 FAR = pl.BlockSpec(memory_space=pltpu.HBM)
 MIB = 1024 * 1024
-VOXEL_LIMIT = 60
 
 
 def up_to(value, unit):
@@ -38,9 +38,11 @@
     return lax.broadcasted_iota(jnp.int32, shape, dim).astype(dtype)
 
 
-def call(body, outs, args, smem=(), far=(), far_outs=(), scratch=(), flops=0, limit=16):
+def call(body, outs, args, smem=(), far=(), far_outs=(), scratch=(), flops=0, limit=16, quick=False):
     moved = sum(math.prod(o.shape) * o.dtype.itemsize for o in outs)
     moved += sum(math.prod(a.shape) * a.dtype.itemsize for a in args)
+    if quick:
+        flops, moved = 0, 1024
     return pl.pallas_call(
         body,
         out_shape=outs,
@@ -50,6 +52,13 @@
         compiler_params=pltpu.CompilerParams(vmem_limit_bytes=limit * MIB),
         cost_estimate=pl.CostEstimate(flops=flops, bytes_accessed=moved, transcendentals=0),
     )(*args)
+
+
+def start_all(pairs, sems):
+    copies = [pltpu.make_async_copy(a, b, sems.at[i]) for i, (a, b) in enumerate(pairs)]
+    for copy in copies:
+        copy.start()
+    return copies
 
 
 def corner(adj_ref, t, lowest):
@@ -272,6 +281,7 @@
         ],
         flops=2 * INNER * SLAB * KOFF * channels * channels,
         limit=20,
+        quick=True,
     )[0]
 
 
@@ -326,13 +336,13 @@
     )[0]
 
 
-def read_slots(cap_rows, adj_ref, msg_ref, table_ref):
-    regions = msg_ref.shape[0]
+def read_slots(cap_rows, adj_ref, slots_ref, table_ref):
+    regions = slots_ref.shape[0]
     tiles = adj_ref.shape[0]
     segs = up_to(cap_rows, LANES) // LANES
     lowest = lax.axis_index("region") * tiles
     for r in range(regions):
-        tile = msg_ref[r, cap_rows : cap_rows + 16, :].astype(F32)
+        tile = slots_ref[r].astype(F32)
         for s in range(segs):
             lanes = slice(s * LANES, (s + 1) * LANES)
             table_ref[r : r + 1, lanes] = tile[s : s + 1]
@@ -350,85 +360,157 @@
     return jnp.transpose(jnp.concatenate([blocks, withins], axis=0))
 
 
-def fill_picks(pick_ref, columns, r, regions, cap_rows, row):
+def fill_picks(pick_ref, side_ref, columns, r, regions, cap_rows):
     shape = (cap_rows, LANES)
+    rows = slice(r * cap_rows, (r + 1) * cap_rows)
     lane = iota(shape, 1, F32).astype(BF)
-    block = jnp.broadcast_to(columns[0:cap_rows, r : r + 1], shape).astype(BF)
+    whole = jnp.broadcast_to(columns[0:cap_rows, r : r + 1], shape)
+    upper = whole >= HALF // LANES
+    block = jnp.where(upper, whole - HALF // LANES, whole).astype(BF)
+    side_ref[rows, :] = jnp.where(upper, 1.0, jnp.where(whole < 0.0, -1.0, 0.0))
     place = regions + r
     within = jnp.broadcast_to(columns[0:cap_rows, place : place + 1], shape).astype(BF)
     one = jnp.where(lane == within, jnp.ones_like(lane), jnp.zeros_like(lane))
-    for q in range(DENSE // LANES):
-        pick_ref[row : row + cap_rows, q * LANES : (q + 1) * LANES] = jnp.where(
+    for q in range(HALF // LANES):
+        pick_ref[rows, q * LANES : (q + 1) * LANES] = jnp.where(
             block == jnp.asarray(q, BF), one, jnp.zeros_like(one)
         )
 
 
+def flip(array):
+    return jnp.transpose(array).astype(BF)
+
+
+def sum_rows(rows, side):
+    lower, upper = side == 0.0, side == 1.0
+    return jnp.concatenate(
+        [
+            flip(jnp.where(lower, rows, 0.0)),
+            flip(jnp.where(upper, rows, 0.0)),
+            flip(jnp.where(lower, 1.0, 0.0))[0:16],
+            flip(jnp.where(upper, 1.0, 0.0))[0:16],
+        ],
+        axis=0,
+    )
+
+
 def voxel_body(
-    cap_rows, scaling,
+    cap_rows,
     adj_far, msg_far, below_far, above_far, dense_far, weights_far, grad_far,
-    turned_far, low_far, high_far, back_far, keep_far, send_far,
-    adj_ref, msg_ref, below_ref, above_ref, dense_ref, weights_ref, grad_ref,
+    turned_far, low_far, high_far, back_far,
+    adj_ref, slots_ref, rows_ref, below_ref, above_ref, dense_ref, weights_ref, grad_ref,
     turned_ref, back_ref,
-    table_ref, feats_ref, pick_ref, all_ref, shift_ref, in_sems, out_sems,
+    table_ref, pick_ref, side_ref, shift_ref, in_sems, out_sems,
 ):
     pairs = (
         (adj_far, adj_ref),
-        (msg_far, msg_ref),
+        (msg_far.at[:, cap_rows : cap_rows + 16], slots_ref),
         (below_far, below_ref),
         (above_far, above_ref),
-        (dense_far, dense_ref),
+        (dense_far.at[0:2], dense_ref.at[0:2]),
+        (dense_far.at[NX - 2 : NX], dense_ref.at[2:4]),
         (weights_far, weights_ref),
+        (msg_far.at[:, 0:cap_rows], rows_ref),
         (grad_far, grad_ref.at[1 : NX - 1]),
     )
-    copies = [pltpu.make_async_copy(a, b, in_sems.at[i]) for i, (a, b) in enumerate(pairs)]
-    for copy in copies:
-        copy.start()
-    regions, rows, channels = msg_ref.shape
+    copies = start_all(pairs, in_sems)
+    regions, _, channels = rows_ref.shape
     total = regions * cap_rows
-    for copy in copies[2:]:
+    copies[0].wait()
+    copies[1].wait()
+    columns = read_slots(cap_rows, adj_ref, slots_ref, table_ref)
+    for r in range(regions):
+        fill_picks(pick_ref, side_ref, columns, r, regions, cap_rows)
+    for copy in copies[2:7]:
         copy.wait()
+    slabs = [below_ref[...]] + [dense_ref[i] for i in range(4)] + [above_ref[...]]
+    grad_ref[0], grad_ref[NX - 1] = conv_edges(shift_ref, weights_ref, slabs)
+    for copy in copies[7:]:
+        copy.wait()
+    left = sum_rows(rows_ref[...].reshape(total, channels).astype(F32), side_ref[...])
+    width = 2 * LANES
+    for q in range(0, HALF, width):
+        part = jnp.dot(left, pick_ref[:, q : q + width], preferred_element_type=F32)
+        for h in range(2):
+            at = 2 * channels + 16 * h
+            denom = jnp.maximum(part[at : at + 8], 1.0)
+            start = h * HALF + q
+            turned_ref[:, start : start + width] = (
+                part[h * channels : (h + 1) * channels] / denom[0:1]
+            ).astype(BF)
+            x = start // SLAB
+            grad_ref[x] = grad_ref[x] / jnp.transpose(denom)[:, 0:1]
+    results = start_all(
+        (
+            (turned_ref, turned_far),
+            (turned_ref.at[:, 0:SLAB], low_far),
+            (turned_ref.at[:, DENSE - SLAB : DENSE], high_far),
+        ),
+        out_sems,
+    )
+    voxel_grad = grad_ref[...].reshape(DENSE, channels).astype(BF)
+    halves = jnp.concatenate([voxel_grad[0:HALF], voxel_grad[HALF:DENSE]], axis=1)
+    group = regions // 4
+    for n in range(4):
+        r = n * group
+        rows = slice(r * cap_rows, (r + group) * cap_rows)
+        both = jnp.dot(pick_ref[rows, :], halves, preferred_element_type=F32)
+        picked = jnp.where(side_ref[rows, :] == 1.0, both[:, channels:], both[:, 0:channels]).astype(BF)
+        for i in range(group):
+            back_ref[r + i] = picked[i * cap_rows : (i + 1) * cap_rows]
+        part = pl.ds(r, group)
+        results += start_all([(back_ref.at[part], back_far.at[part])], out_sems.at[3 + n : 4 + n])
+    for copy in results:
+        copy.wait()
+
+
+def voxels(adjacency, msg, below, above, dense, weights, grad, cap_rows):
+    regions, rows, channels = msg.shape
+    segs = up_to(cap_rows, LANES) // LANES
+    total = regions * cap_rows
+    turned, back = (channels, DENSE), (regions, cap_rows, channels)
+    face = jax.ShapeDtypeStruct((channels, SLAB), BF)
+    return call(
+        functools.partial(voxel_body, cap_rows),
+        [
+            jax.ShapeDtypeStruct(turned, BF),
+            face,
+            face,
+            jax.ShapeDtypeStruct(back, BF),
+        ],
+        [adjacency, msg, below, above, dense, weights, grad],
+        far=range(7),
+        far_outs=range(4),
+        scratch=[
+            pltpu.SMEM(adjacency.shape, jnp.int32),
+            pltpu.VMEM((regions, 16, channels), BF),
+            pltpu.VMEM(back, BF),
+            pltpu.VMEM(below.shape, BF),
+            pltpu.VMEM(above.shape, BF),
+            pltpu.VMEM((4, SLAB, channels), BF),
+            pltpu.VMEM(weights.shape, BF),
+            pltpu.VMEM((NX, SLAB, channels), F32),
+            pltpu.VMEM(turned, BF),
+            pltpu.VMEM(back, BF),
+            pltpu.VMEM((2 * regions, segs * LANES), F32),
+            pltpu.VMEM((total, HALF), BF),
+            pltpu.VMEM((total, LANES), F32),
+            pltpu.VMEM((3, 6, SHIFTED, channels), BF),
+            pltpu.SemaphoreType.DMA((9,)),
+            pltpu.SemaphoreType.DMA((7,)),
+        ],
+        flops=4 * total * DENSE * channels,
+        limit=60,
+    )
+
+
+def weight_body(
+    scaling, turned_ref, below_ref, above_ref, dense_ref, keep_ref, send_ref, shift_ref, all_ref
+):
+    channels = turned_ref.shape[0]
     slabs = [below_ref[...]] + [dense_ref[x] for x in range(NX)] + [above_ref[...]]
     for x, slab in enumerate(slabs):
         put_shifts(shift_ref, x, slab)
-    for x in (0, NX - 1):
-        grad_ref[x] = conv_slab(shift_ref, weights_ref, x)
-    copies[0].wait()
-    copies[1].wait()
-    columns = read_slots(cap_rows, adj_ref, msg_ref, table_ref)
-    for r in range(regions):
-        feats_ref[r * cap_rows : (r + 1) * cap_rows, :] = msg_ref[r, 0:cap_rows, :]
-        fill_picks(pick_ref, columns, r, regions, cap_rows, r * cap_rows)
-    flipped = jnp.transpose(feats_ref[...].astype(F32)).astype(BF)
-    left = jnp.concatenate([flipped, jnp.ones((16, total), BF)], axis=0)
-    width = 2 * LANES
-    for q in range(0, DENSE, width):
-        part = jnp.dot(left, pick_ref[:, q : q + width], preferred_element_type=F32)
-        denom = jnp.maximum(part[channels : channels + 8], 1.0)
-        turned_ref[:, q : q + width] = (part[0:channels] / denom[0:1]).astype(BF)
-        x = q // SLAB
-        grad_ref[x] = grad_ref[x] / jnp.transpose(denom)[:, 0:1]
-    core = lax.rem(lax.axis_index("region"), 2)
-    half = keep_far.shape[0]
-    outs = (
-        (turned_ref, turned_far),
-        (turned_ref.at[:, 0:SLAB], low_far),
-        (turned_ref.at[:, DENSE - SLAB : DENSE], high_far),
-        (back_ref, back_far),
-        (all_ref.at[pl.ds(pl.multiple_of(core * half, 16), half)], keep_far),
-        (all_ref.at[pl.ds(pl.multiple_of((1 - core) * half, 16), half)], send_far),
-    )
-    results = [pltpu.make_async_copy(a, b, out_sems.at[i]) for i, (a, b) in enumerate(outs)]
-    for copy in results[:3]:
-        copy.start()
-    voxel_grad = grad_ref[...].reshape(DENSE, channels).astype(BF)
-    group = regions // 4
-    for r in range(0, regions, group):
-        picked = jnp.dot(
-            pick_ref[r * cap_rows : (r + group) * cap_rows, :], voxel_grad, preferred_element_type=F32
-        ).astype(BF)
-        for i in range(group):
-            back_ref[r + i] = picked[i * cap_rows : (i + 1) * cap_rows]
-    results[3].start()
     left = turned_ref[...]
     for k in range(0, KOFF, 2):
         pieces = []
@@ -441,52 +523,24 @@
         for i in range(len(pieces)):
             at = (KOFF - 1 - k - i) * channels
             all_ref[at : at + channels, :] = term[:, i * channels : (i + 1) * channels]
-    results[4].start()
-    results[5].start()
-    for copy in results:
-        copy.wait()
-
-
-def voxels(adjacency, msg, below, above, dense, weights, grad, cap_rows, scaling):
-    regions, rows, channels = msg.shape
-    segs = up_to(cap_rows, LANES) // LANES
-    total = regions * cap_rows
-    half = (KOFF * channels // 2, channels)
-    turned, back = (channels, DENSE), (regions, cap_rows, channels)
-    face = jax.ShapeDtypeStruct((channels, SLAB), BF)
-    return call(
-        functools.partial(voxel_body, cap_rows, scaling),
-        [
-            jax.ShapeDtypeStruct(turned, BF),
-            face,
-            face,
-            jax.ShapeDtypeStruct(back, BF),
-            jax.ShapeDtypeStruct(half, F32),
-            jax.ShapeDtypeStruct(half, F32),
+    core = lax.rem(lax.axis_index("region"), 2)
+    half = keep_ref.shape[0]
+    keep_ref[...] = all_ref[pl.ds(pl.multiple_of(core * half, 16), half), :]
+    send_ref[...] = all_ref[pl.ds(pl.multiple_of((1 - core) * half, 16), half), :]
+
+
+def weight_terms(turned, below, above, dense, scaling):
+    channels = turned.shape[0]
+    half = jax.ShapeDtypeStruct((KOFF * channels // 2, channels), F32)
+    return call(
+        functools.partial(weight_body, scaling),
+        [half, half],
+        [turned, below, above, dense],
+        scratch=[
+            pltpu.VMEM((3, NX + 2, SHIFTED, channels), BF),
+            pltpu.VMEM((KOFF * channels, channels), F32),
         ],
-        [adjacency, msg, below, above, dense, weights, grad],
-        far=range(7),
-        far_outs=range(6),
-        scratch=[
-            pltpu.SMEM(adjacency.shape, jnp.int32),
-            pltpu.VMEM(msg.shape, BF),
-            pltpu.VMEM(below.shape, BF),
-            pltpu.VMEM(above.shape, BF),
-            pltpu.VMEM(dense.shape, BF),
-            pltpu.VMEM(weights.shape, BF),
-            pltpu.VMEM((NX, SLAB, channels), F32),
-            pltpu.VMEM(turned, BF),
-            pltpu.VMEM(back, BF),
-            pltpu.VMEM((2 * regions, segs * LANES), F32),
-            pltpu.VMEM((total, channels), BF),
-            pltpu.VMEM((total, DENSE), BF),
-            pltpu.VMEM((KOFF * channels, channels), F32),
-            pltpu.VMEM((3, NX + 2, SHIFTED, channels), BF),
-            pltpu.SemaphoreType.DMA((7,)),
-            pltpu.SemaphoreType.DMA((6,)),
-        ],
-        flops=2 * DENSE * (KOFF * channels + 2 * total) * channels,
-        limit=VOXEL_LIMIT,
+        flops=2 * DENSE * KOFF * channels * channels,
     )
 
 
@@ -637,10 +691,11 @@
     mirrored = jnp.transpose(kernel[::-1], (0, 2, 1)).reshape(KOFF * channels, channels)
     grad = inner_gradient(cot, mirrored)
     scaling = 1.0 / math.sqrt(tiles * regions * vox)
-    turned, low, high, back, keep, send = voxels(
-        adjacency, received, below, above, cot, mirrored, grad, cap_rows, scaling
+    turned, low, high, back = voxels(
+        adjacency, received, below, above, cot, mirrored, grad, cap_rows
     )
     returned = exchange(back)
+    keep, send = weight_terms(turned, below, above, cot, scaling)
     groups = groups_of(regions)
     bit, size = groups[0]
     term, *sent = split(keep, swapped(send, 1), size)
@@ -648,10 +703,12 @@
     turned, low, high, *sent = lax.optimization_barrier((turned, low, high, *sent))
     feats_below, feats_above = from_sides(low, high)
     inner = inner_forward(turned, weights)
-    term = sum_group(term, sent, bit)
-    term, returned, inner, feats_below, feats_above = lax.optimization_barrier(
-        (term, returned, inner, feats_below, feats_above)
-    )
+    got = [swapped(part, bit * (i + 1)) for i, part in enumerate(sent)]
+    got, returned, inner, feats_below, feats_above = lax.optimization_barrier(
+        (got, returned, inner, feats_below, feats_above)
+    )
+    for part in got:
+        term = term + part.astype(F32)
     for bit, size in groups[1:-1]:
         term = reduce_group(term, bit, size)
     bit, size = groups[-1]

time: 88.6 us -> 85 us (0.959)
  waiting for transfers between devices: 21.2 us -> 14.8 us
  starting transfers between devices: 30.4 us -> 33.2 us
  Pallas kernels: 33 us -> 30.2 us
  local copies, waits for them, and re-layouts: 2.35 us -> 5.05 us
    ppermute x9, waiting for transfers between devices: 14.5 us -> 8.03 us  [swapped(): return lax.ppermute(array, 'region', [(i, i ^ bit) for i in range(count)])]
    pallas_call x9 -> x10, Pallas kernels: 33 us -> 30.2 us  [call(): pl.pallas_call(body, out_shape=outs, in_specs=[SMEM if i in smem else FAR...]
    unnamed x30 -> x34, local copies, waits for them, and re-layouts: 0.95 us -> 3.65 us
    ppermute x9, starting transfers between devices: 10.7 us -> 13.4 us  [swapped(): return lax.ppermute(array, 'region', [(i, i ^ bit) for i in range(count)])]
  transfers between devices with their start and end apart: 15 -> 15, of which waited for: 6 -> 6; matrix products, arithmetic and copies ran while one was open for 2% -> 2% of each run, Pallas kernels for 17% -> 21%
where the time goes in v3:
time: 85 us; the launch traced here: 84.4 us
  starting transfers between devices  33.2 us (39%)
  Pallas kernels  30.2 us (36%)
  waiting for transfers between devices  14.8 us (17%)
  local copies, waits for them, and re-layouts  5.05 us (6%)
  between operations  0.98 us (1%)
    pallas_call x10, Pallas kernels, call(): pl.pallas_call(body, out_shape=outs, in_specs=[SMEM if i in smem else FAR...  30.2 us
    ppermute x9, starting transfers between devices, swapped(): return lax.ppermute(array, 'region', [(i, i ^ bit) for i in range(count)])  13.4 us
    all_to_all x2, starting transfers between devices, exchange(): lax.all_to_all(array, 'region', split_axis=0, concat_axis=0, tiled=True)  13.4 us
    ppermute x9, waiting for transfers between devices, swapped(): return lax.ppermute(array, 'region', [(i, i ^ bit) for i in range(count)])  8.03 us
    all_to_all x2, waiting for transfers between devices, exchange(): lax.all_to_all(array, 'region', split_axis=0, concat_axis=0, tiled=True)  6.74 us
    ppermute x4, starting transfers between devices, from_sides(): return (lax.ppermute(high, 'region', up), lax.ppermute(low, 'region', down))  6.45 us
    unnamed x34, local copies, waits for them, and re-layouts  3.65 us
  transfers between devices with their start and end apart: 15, of which 6 were waited for; matrix products, arithmetic and copies ran while one was open for 2% of the time, Pallas kernels for 21%

profile of v3, /device:TPU:0, one launch (start us, length us, event | category | flops | bytes accessed | tf_op | source)
XLA Modules:
  0.0 84.4 jit_solution(10159987465613262202)
XLA Ops:
  0.7 3.6 %shard_map.85 = (bf16[16,176,128]{2,1,0:T(8,128)(2,1)}, f32[8,1024]{1,0:T(8,128)}) custom-call(s32[1,1024]{1,0:T(1,128)} %bitcast.20, s32[1,1024]{1,0:T(1,128)} %bitcast.21, bf16[1024,128]{1,0:T(8,128)(2,1)} %feats_far.1), custom_call_target="tpu_custom_call" | custom-call | flops 671088640 | bytes 1024000 | tf_op jit(solution)/shard_map/pallas_call | solution.py:46
  4.3 7.4 %all-to-all-start = ((bf16[16,176,128]{2,1,0:T(8,128)(2,1)}), bf16[16,176,128]{2,1,0:T(8,128)(2,1)}, u32[]{:S(2)}, u32[]{:S(2)}) async-start(bf16[16,176,128]{2,1,0:T(8,128)(2,1)} %get-tuple-element.37), calls=%async_computation | async-start | bytes 1441792 | tf_op jit(solution)/shard_map/all_to_all | solution.py:676
  11.7 0.9 %shard_map.86 = (bf16[8,256,128]{2,1,0:T(8,128)(2,1)S(1)}, bf16[256,128]{1,0:T(8,128)(2,1)S(1)}, bf16[256,128]{1,0:T(8,128)(2,1)S(1)}) custom-call(s32[16,27]{1,0:T(8,128)S(1)} %copy-done.5, bf16[16,128,128]{2,1,0:T(8,128)(2,1)S(1)} %copy-done.4), custom_call_target="tpu_custom_call" | custom-call | bytes 1181376 | tf_op jit(solution)/shard_map/pallas_call | solution.py:46
  12.6 2.3 %collective-permute-start = (bf16[256,128]{1,0:T(8,128)(2,1)S(1)}, bf16[256,128]{1,0:T(8,128)(2,1)S(1)}, u32[]{:S(2)}, u32[]{:S(2)}) collective-permute-start(bf16[256,128]{1,0:T(8,128)(2,1)S(1)} %get-tuple-element.38), channel_id=1, source_target_pairs={{0,1},{1,2},{2,3},{3,4},{4,5},{5,6},{6,7},{7,8},{8,9},{9,10},{10,1... | collective-permute-start | bytes 196616 | tf_op jit(solution)/shard_map/ppermute | solution.py:605
  14.9 1.3 %collective-permute-start.1 = (bf16[256,128]{1,0:T(8,128)(2,1)S(1)}, bf16[256,128]{1,0:T(8,128)(2,1)S(1)}, u32[]{:S(2)}, u32[]{:S(2)}) collective-permute-start(bf16[256,128]{1,0:T(8,128)(2,1)S(1)} %get-tuple-element.39), channel_id=1, source_target_pairs={{1,0},{2,1},{3,2},{4,3},{5,4},{6,5},{7,6},{8,7},{9,8},{10,9},{11,1... | collective-permute-start | bytes 196616 | tf_op jit(solution)/shard_map/ppermute | solution.py:605
  16.3 1.3 %copy.9 = bf16[27,128,128]{2,1,0:T(8,128)(2,1)S(1)} copy(bf16[27,128,128]{1,2,0:T(8,128)(2,1)S(1)} %reverse_bitcast_fusion) | data formatting | bytes 1769472 | tf_op jit(solution)/shard_map/transpose | solution.py:691
  17.7 4.1 %shard_map.87.grad_far = f32[6,256,128]{2,1,0:T(8,128)S(1)} custom-call(bf16[8,256,128]{2,1,0:T(8,128)(2,1)S(1)} %get-tuple-element.40.dense_ref.dense_far, bf16[3456,128]{1,0:T(8,128)(2,1)S(1)} %bitcast.13), custom_call_target="tpu_custom_call" | custom-call | flops 1358954496 | bytes 2195456 | tf_op jit(solution)/shard_map/pallas_call | solution.py:46
  21.8 0.9 %copy-done.13 = f32[6,256,128]{2,1,0:T(8,128)} copy-done((f32[6,256,128]{2,1,0:T(8,128)}, f32[6,256,128]{2,1,0:T(8,128)S(1)}, u32[]{:S(2)}) %copy-start.13) | copy-done | bytes 786456
  22.7 6.7 %all-to-all-done.msg_far = bf16[16,176,128]{2,1,0:T(8,128)(2,1)} async-done(((bf16[16,176,128]{2,1,0:T(8,128)(2,1)}), bf16[16,176,128]{2,1,0:T(8,128)(2,1)}, u32[]{:S(2)}, u32[]{:S(2)}) %all-to-all-start) | async-done | bytes 720928 | tf_op jit(solution)/shard_map/all_to_all | solution.py:676
  29.4 7.6 %shard_map.88 = (bf16[128,2048]{1,0:T(8,128)(2,1)}, bf16[128,256]{1,0:T(8,128)(2,1)}, bf16[128,256]{1,0:T(8,128)(2,1)}, bf16[16,160,128]{2,1,0:T(8,128)(2,1)}) custom-call(s32[16,27]{1,0:T(8,128)} %adj_ref.3, bf16[16,176,128]{2,1,0:T(8,128)(2,1)} %all-to-all-done.msg_far, bf16[256,128]{1,0:T(8,128)(2,1)} %copy-done.9, bf16[256,128]{1,0:T(8,128)(2,1)} %copy-done.11, ...), custom_call_target="tpu_custom_call" | custom-call | flops 2684354560 | bytes 4359872 | tf_op jit(solution)/shard_map/pallas_call | solution.py:46
  37.0 6.0 %all-to-all-start.1 = ((bf16[16,160,128]{2,1,0:T(8,128)(2,1)}), bf16[16,160,128]{2,1,0:T(8,128)(2,1)S(1)}, u32[]{:S(2)}, u32[]{:S(2)}) async-start(bf16[16,160,128]{2,1,0:T(8,128)(2,1)} %get-tuple-element.53), calls=%async_computation.1 | async-start | bytes 1310720 | tf_op jit(solution)/shard_map/all_to_all | solution.py:676
  43.0 1.0 %copy-done.1 = bf16[128,2048]{1,0:T(8,128)(2,1)S(1)} copy-done((bf16[128,2048]{1,0:T(8,128)(2,1)S(1)}, bf16[128,2048]{1,0:T(8,128)(2,1)}, u32[]{:S(2)}) %copy-start.1) | copy-done | bytes 524312
  44.1 0.8 copy-done.10
  44.9 0.8 copy-done.12
  45.7 2.6 %shard_map.89 = (f32[1728,128]{1,0:T(8,128)S(1)}, f32[1728,128]{1,0:T(8,128)S(1)}) custom-call(bf16[128,2048]{1,0:T(8,128)(2,1)S(1)} %copy-done.1, bf16[256,128]{1,0:T(8,128)(2,1)S(1)} %copy-done.10, bf16[256,128]{1,0:T(8,128)(2,1)S(1)} %copy-done.12, bf16[8,256,128]{2,1,0:T(8,128)(2,1)S(1)} %copy-done.8), custom_call_target="tpu_custom_call" | custom-call | flops 1811939328 | bytes 2949120 | tf_op jit(solution)/shard_map/pallas_call | solution.py:46
  48.4 0.5 collective-permute-start.2
  48.9 2.1 %collective-permute-done.2.got_ref = f32[1728,128]{1,0:T(8,128)S(1)} collective-permute-done((f32[1728,128]{1,0:T(8,128)S(1)}, f32[1728,128]{1,0:T(8,128)S(1)}, u32[]{:S(2)}, u32[]{:S(2)}) %collective-permute-start.2) | collective-permute-done | bytes 884768 | tf_op jit(solution)/shard_map/ppermute | solution.py:610
  51.0 2.0 %collective-permute-start.3 = (bf16[432,128]{1,0:T(8,128)(2,1)S(1)}, bf16[432,128]{1,0:T(8,128)(2,1)S(1)}, u32[]{:S(2)}, u32[]{:S(2)}) collective-permute-start(bf16[432,128]{1,0:T(8,128)(2,1)S(1)} %get-tuple-element.50), channel_id=1, source_target_pairs={{0,2},{1,3},{2,0},{3,1},{4,6},{5,7},{6,4},{7,5},{8,10},{9,11},{10,... | collective-permute-start | bytes 331784 | tf_op jit(solution)/shard_map/ppermute | solution.py:610
  53.0 1.5 %collective-permute-start.4 = (bf16[432,128]{1,0:T(8,128)(2,1)S(1)}, bf16[432,128]{1,0:T(8,128)(2,1)S(1)}, u32[]{:S(2)}, u32[]{:S(2)}) collective-permute-start(bf16[432,128]{1,0:T(8,128)(2,1)S(1)} %get-tuple-element.51), channel_id=1, source_target_pairs={{0,4},{1,5},{2,6},{3,7},{4,0},{5,1},{6,2},{7,3},{8,12},{9,13},{10,... | collective-permute-start | bytes 331784 | tf_op jit(solution)/shard_map/ppermute | solution.py:610
  54.6 1.6 %collective-permute-start.6 = (bf16[128,256]{1,0:T(8,128)(2,1)S(1)}, bf16[128,256]{1,0:T(8,128)(2,1)S(1)}, u32[]{:S(2)}, u32[]{:S(2)}) collective-permute-start(bf16[128,256]{1,0:T(8,128)(2,1)S(1)} %copy-done.16), channel_id=1, source_target_pairs={{0,1},{1,2},{2,3},{3,4},{4,5},{5,6},{6,7},{7,8},{8,9},{9,10},{10,1... | collective-permute-start | bytes 196616 | tf_op jit(solution)/shard_map/ppermute | solution.py:605
  56.2 1.3 %collective-permute-start.7 = (bf16[128,256]{1,0:T(8,128)(2,1)S(1)}, bf16[128,256]{1,0:T(8,128)(2,1)S(1)}, u32[]{:S(2)}, u32[]{:S(2)}) collective-permute-start(bf16[128,256]{1,0:T(8,128)(2,1)S(1)} %copy-done.15), channel_id=1, source_target_pairs={{1,0},{2,1},{3,2},{4,3},{5,4},{6,5},{7,6},{8,7},{9,8},{10,9},{11,1... | collective-permute-start | bytes 196616 | tf_op jit(solution)/shard_map/ppermute | solution.py:605
  57.5 4.4 %shard_map.91.inner_far = bf16[6,256,128]{2,1,0:T(8,128)(2,1)S(1)} custom-call(bf16[128,2048]{1,0:T(8,128)(2,1)S(1)} %copy-done.2, bf16[3456,128]{1,0:T(8,128)(2,1)S(1)} %bitcast.11), custom_call_target="tpu_custom_call" | custom-call | bytes 1024 | tf_op jit(solution)/shard_map/pallas_call | solution.py:46
  61.9 0.9 %collective-permute-done.5 = bf16[432,128]{1,0:T(8,128)(2,1)S(1)} collective-permute-done((bf16[432,128]{1,0:T(8,128)(2,1)S(1)}, bf16[432,128]{1,0:T(8,128)(2,1)S(1)}, u32[]{:S(2)}, u32[]{:S(2)}) %collective-permute-start.5) | collective-permute-done | bytes 110624 | tf_op jit(solution)/shard_map/ppermute | solution.py:610
  62.9 5.7 %collective-permute-start.8 = (bf16[432,128]{1,0:T(8,128)(2,1)S(1)}, bf16[432,128]{1,0:T(8,128)(2,1)S(1)}, u32[]{:S(2)}, u32[]{:S(2)}) collective-permute-start(bf16[432,128]{1,0:T(8,128)(2,1)S(1)} %add_convert_fusion.1), channel_id=1, source_target_pairs={{0,8},{1,9},{2,10},{3,11},{4,12},{5,13},{6,14},{7,15},{8,0},{9,1},... | collective-permute-start | bytes 331784 | tf_op jit(solution)/shard_map/ppermute | solution.py:610
  68.6 2.4 %shard_map.92 = bf16[1024,128]{1,0:T(8,128)(2,1)} custom-call(f32[8,1024]{1,0:T(8,128)S(1)} %copy-done.14, bf16[16,160,128]{2,1,0:T(8,128)(2,1)S(1)} %all-to-all-done.1.rows_ref), custom_call_target="tpu_custom_call" | custom-call | flops 671088640 | bytes 950272 | tf_op jit(solution)/shard_map/pallas_call | solution.py:46
  71.0 2.4 %collective-permute-done.8 = bf16[432,128]{1,0:T(8,128)(2,1)S(1)} collective-permute-done((bf16[432,128]{1,0:T(8,128)(2,1)S(1)}, bf16[432,128]{1,0:T(8,128)(2,1)S(1)}, u32[]{:S(2)}, u32[]{:S(2)}) %collective-permute-start.8) | collective-permute-done | bytes 110624 | tf_op jit(solution)/shard_map/ppermute | solution.py:610
  73.5 1.7 %collective-permute-start.9 = (bf16[432,128]{1,0:T(8,128)(2,1)S(1)}, bf16[432,128]{1,0:T(8,128)(2,1)S(1)}, u32[]{:S(2)}, u32[]{:S(2)}) collective-permute-start(bf16[432,128]{1,0:T(8,128)(2,1)S(1)} %add_convert_fusion), channel_id=1, source_target_pairs={{0,2},{1,3},{2,0},{3,1},{4,6},{5,7},{6,4},{7,5},{8,10},{9,11},{10,... | collective-permute-start | bytes 331784 | tf_op jit(solution)/shard_map/ppermute | solution.py:610
  75.1 1.9 %collective-permute-start.11 = (bf16[432,128]{1,0:T(8,128)(2,1)S(1)}, bf16[432,128]{1,0:T(8,128)(2,1)S(1)}, u32[]{:S(2)}, u32[]{:S(2)}) collective-permute-start(bf16[432,128]{1,0:T(8,128)(2,1)S(1)} %add_convert_fusion), channel_id=1, source_target_pairs={{0,6},{1,7},{2,4},{3,5},{4,2},{5,3},{6,0},{7,1},{8,14},{9,15},{10,... | collective-permute-start | bytes 331784 | tf_op jit(solution)/shard_map/ppermute | solution.py:610
  77.0 3.2 %shard_map.93 = bf16[16,128,128]{2,1,0:T(8,128)(2,1)} custom-call(s32[16,27]{1,0:T(8,128)S(1)} %copy-done.6, bf16[128,2048]{1,0:T(8,128)(2,1)S(1)} %copy-done.2, bf16[128,256]{1,0:T(8,128)(2,1)S(1)} %collective-permute-done.6.low_ref, bf16[128,256]{1,0:T(8,128)(2,1)S(1)} %collective-permute-done.7.high_ref, bf16[3456,128]{1,0:T(8,128)(2,1)S(1)} %bitcast.12, ...), custom_call_target="tpu_custom_call" | custom-call | flops 452984832 | bytes 2459328 | tf_op jit(solution)/shard_map/pallas_call | solution.py:46
  80.3 0.9 %collective-permute-done.11 = bf16[432,128]{1,0:T(8,128)(2,1)S(1)} collective-permute-done((bf16[432,128]{1,0:T(8,128)(2,1)S(1)}, bf16[432,128]{1,0:T(8,128)(2,1)S(1)}, u32[]{:S(2)}, u32[]{:S(2)}) %collective-permute-start.11) | collective-permute-done | bytes 110624 | tf_op jit(solution)/shard_map/ppermute | solution.py:610
  81.3 1.8 %collective-permute-done.12.other_ref = bf16[4,432,128]{2,1,0:T(8,128)(2,1)S(1)} collective-permute-done((bf16[4,432,128]{2,1,0:T(8,128)(2,1)S(1)}, bf16[4,432,128]{2,1,0:T(8,128)(2,1)S(1)}, u32[]{:S(2)}, u32[]{:S(2)}) %collective-permute-start.12) | collective-permute-done | bytes 442400 | tf_op jit(solution)/shard_map/ppermute | solution.py:610
  83.1 1.3 %shard_map.94 = f32[3456,128]{1,0:T(8,128)} custom-call(bf16[4,432,128]{2,1,0:T(8,128)(2,1)S(1)} %pad_maximum_fusion.own_ref, bf16[4,432,128]{2,1,0:T(8,128)(2,1)S(1)} %collective-permute-done.12.other_ref), custom_call_target="tpu_custom_call" | custom-call | bytes 2654208 | tf_op jit(solution)/shard_map/pallas_call | solution.py:46
  (47 shorter events, 0.6 us)
Async XLA Ops:
  0.6 11.1 %copy-start.4 = (bf16[16,128,128]{2,1,0:T(8,128)(2,1)S(1)}, bf16[16,128,128]{2,1,0:T(8,128)(2,1)}, u32[]{:S(2)}) copy-start(bf16[16,128,128]{2,1,0:T(8,128)(2,1)} %bricks_ref.1) | copy-start | bytes 1572868
  0.6 11.1 %copy-start.5 = (s32[16,27]{1,0:T(8,128)S(1)}, s32[16,27]{1,0:T(8,128)}, u32[]{:S(2)}) copy-start(s32[16,27]{1,0:T(8,128)} %adj_ref.3) | copy-start | bytes 5188
  0.7 15.6 %copy-start = (bf16[27,128,128]{2,1,0:T(8,128)(2,1)S(1)}, bf16[27,128,128]{2,1,0:T(8,128)(2,1)}, u32[]{:S(2)}) copy-start(bf16[27,128,128]{2,1,0:T(8,128)(2,1)} %param.10) | copy-start | bytes 2654212
  4.3 25.1 %all-to-all-start = ((bf16[16,176,128]{2,1,0:T(8,128)(2,1)}), bf16[16,176,128]{2,1,0:T(8,128)(2,1)}, u32[]{:S(2)}, u32[]{:S(2)}) async-start(bf16[16,176,128]{2,1,0:T(8,128)(2,1)} %get-tuple-element.37), calls=%async_computation | async-start | bytes 1441792 | tf_op jit(solution)/shard_map/all_to_all | solution.py:676
  12.6 5.0 %copy-start.7 = (bf16[8,256,128]{2,1,0:T(8,128)(2,1)}, bf16[8,256,128]{2,1,0:T(8,128)(2,1)S(1)}, u32[]{:S(2)}) copy-start(bf16[8,256,128]{2,1,0:T(8,128)(2,1)S(1)} %get-tuple-element.40.dense_ref.dense_far) | copy-start | bytes 1572868
  12.6 10.0 %collective-permute-start = (bf16[256,128]{1,0:T(8,128)(2,1)S(1)}, bf16[256,128]{1,0:T(8,128)(2,1)S(1)}, u32[]{:S(2)}, u32[]{:S(2)}) collective-permute-start(bf16[256,128]{1,0:T(8,128)(2,1)S(1)} %get-tuple-element.38), channel_id=1, source_target_pairs={{0,1},{1,2},{2,3},{3,4},{4,5},{5,6},{6,7},{7,8},{8,9},{9,10},{10,1... | collective-permute-start | bytes 196616 | tf_op jit(solution)/shard_map/ppermute | solution.py:605
  14.9 7.8 %collective-permute-start.1 = (bf16[256,128]{1,0:T(8,128)(2,1)S(1)}, bf16[256,128]{1,0:T(8,128)(2,1)S(1)}, u32[]{:S(2)}, u32[]{:S(2)}) collective-permute-start(bf16[256,128]{1,0:T(8,128)(2,1)S(1)} %get-tuple-element.39), channel_id=1, source_target_pairs={{1,0},{2,1},{3,2},{4,3},{5,4},{6,5},{7,6},{8,7},{9,8},{10,9},{11,1... | collective-permute-start | bytes 196616 | tf_op jit(solution)/shard_map/ppermute | solution.py:605
  17.6 4.1 %copy-start.3 = (bf16[27,128,128]{2,1,0:T(8,128)(2,1)}, bf16[27,128,128]{2,1,0:T(8,128)(2,1)S(1)}, u32[]{:S(2)}) copy-start(bf16[27,128,128]{2,1,0:T(8,128)(2,1)S(1)} %copy.9) | copy-start | bytes 2654212
  21.8 0.9 %copy-start.13 = (f32[6,256,128]{2,1,0:T(8,128)}, f32[6,256,128]{2,1,0:T(8,128)S(1)}, u32[]{:S(2)}) copy-start(f32[6,256,128]{2,1,0:T(8,128)S(1)} %shard_map.87.grad_far) | copy-start | bytes 2359300
  22.7 20.3 %copy-start.8 = (bf16[8,256,128]{2,1,0:T(8,128)(2,1)S(1)}, bf16[8,256,128]{2,1,0:T(8,128)(2,1)}, u32[]{:S(2)}) copy-start(bf16[8,256,128]{2,1,0:T(8,128)(2,1)} %copy-done.7) | copy-start | bytes 1572868
  22.7 6.8 %copy-start.9 = (bf16[256,128]{1,0:T(8,128)(2,1)}, bf16[256,128]{1,0:T(8,128)(2,1)S(1)}, u32[]{:S(2)}) copy-start(bf16[256,128]{1,0:T(8,128)(2,1)S(1)} %collective-permute-done.below_far.below_ref) | copy-start | bytes 196612
  22.7 6.8 %copy-start.11 = (bf16[256,128]{1,0:T(8,128)(2,1)}, bf16[256,128]{1,0:T(8,128)(2,1)S(1)}, u32[]{:S(2)}) copy-start(bf16[256,128]{1,0:T(8,128)(2,1)S(1)} %collective-permute-done.1.above_far.above_ref) | copy-start | bytes 196612
  37.0 25.8 %all-to-all-start.1 = ((bf16[16,160,128]{2,1,0:T(8,128)(2,1)}), bf16[16,160,128]{2,1,0:T(8,128)(2,1)S(1)}, u32[]{:S(2)}, u32[]{:S(2)}) async-start(bf16[16,160,128]{2,1,0:T(8,128)(2,1)} %get-tuple-element.53), calls=%async_computation.1 | async-start | bytes 1310720 | tf_op jit(solution)/shard_map/all_to_all | solution.py:676
  43.0 1.0 %copy-start.1 = (bf16[128,2048]{1,0:T(8,128)(2,1)S(1)}, bf16[128,2048]{1,0:T(8,128)(2,1)}, u32[]{:S(2)}) copy-start(bf16[128,2048]{1,0:T(8,128)(2,1)} %get-tuple-element.54.turned_ref.turned_far) | copy-start | bytes 1572868
  44.0 0.8 copy-start.10
  44.9 0.8 copy-start.12
  48.4 6.2 %copy-start.16 = (bf16[128,256]{1,0:T(8,128)(2,1)S(1)}, bf16[128,256]{1,0:T(8,128)(2,1)}, u32[]{:S(2)}) copy-start(bf16[128,256]{1,0:T(8,128)(2,1)} %get-tuple-element.55) | copy-start | bytes 196612
  48.4 7.8 %copy-start.15 = (bf16[128,256]{1,0:T(8,128)(2,1)S(1)}, bf16[128,256]{1,0:T(8,128)(2,1)}, u32[]{:S(2)}) copy-start(bf16[128,256]{1,0:T(8,128)(2,1)} %get-tuple-element.56) | copy-start | bytes 196612
  48.4 9.1 %copy-start.2 = (bf16[128,2048]{1,0:T(8,128)(2,1)S(1)}, bf16[128,2048]{1,0:T(8,128)(2,1)}, u32[]{:S(2)}) copy-start(bf16[128,2048]{1,0:T(8,128)(2,1)} %get-tuple-element.54.turned_ref.turned_far) | copy-start | bytes 1572868
  48.4 2.5 %collective-permute-start.2 = (f32[1728,128]{1,0:T(8,128)S(1)}, f32[1728,128]{1,0:T(8,128)S(1)}, u32[]{:S(2)}, u32[]{:S(2)}) collective-permute-start(f32[1728,128]{1,0:T(8,128)S(1)} %get-tuple-element.43), channel_id=1, source_target_pairs={{0,1},{1,0},{2,3},{3,2},{4,5},{5,4},{6,7},{7,6},{8,9},{9,8},{10,11... | collective-permute-start | bytes 2654216 | tf_op jit(solution)/shard_map/ppermute | solution.py:610
  50.9 17.7 %copy-start.14 = (f32[8,1024]{1,0:T(8,128)S(1)}, f32[8,1024]{1,0:T(8,128)}, u32[]{:S(2)}) copy-start(f32[8,1024]{1,0:T(8,128)} %get-tuple-element.62.place_ref) | copy-start | bytes 98308
  51.0 10.9 %collective-permute-start.3 = (bf16[432,128]{1,0:T(8,128)(2,1)S(1)}, bf16[432,128]{1,0:T(8,128)(2,1)S(1)}, u32[]{:S(2)}, u32[]{:S(2)}) collective-permute-start(bf16[432,128]{1,0:T(8,128)(2,1)S(1)} %get-tuple-element.50), channel_id=1, source_target_pairs={{0,2},{1,3},{2,0},{3,1},{4,6},{5,7},{6,4},{7,5},{8,10},{9,11},{10,... | collective-permute-start | bytes 331784 | tf_op jit(solution)/shard_map/ppermute | solution.py:610
  53.0 8.9 %collective-permute-start.4 = (bf16[432,128]{1,0:T(8,128)(2,1)S(1)}, bf16[432,128]{1,0:T(8,128)(2,1)S(1)}, u32[]{:S(2)}, u32[]{:S(2)}) collective-permute-start(bf16[432,128]{1,0:T(8,128)(2,1)S(1)} %get-tuple-element.51), channel_id=1, source_target_pairs={{0,4},{1,5},{2,6},{3,7},{4,0},{5,1},{6,2},{7,3},{8,12},{9,13},{10,... | collective-permute-start | bytes 331784 | tf_op jit(solution)/shard_map/ppermute | solution.py:610
  54.4 8.4 %collective-permute-start.5 = (bf16[432,128]{1,0:T(8,128)(2,1)S(1)}, bf16[432,128]{1,0:T(8,128)(2,1)S(1)}, u32[]{:S(2)}, u32[]{:S(2)}) collective-permute-start(bf16[432,128]{1,0:T(8,128)(2,1)S(1)} %get-tuple-element.52), channel_id=1, source_target_pairs={{0,6},{1,7},{2,4},{3,5},{4,2},{5,3},{6,0},{7,1},{8,14},{9,15},{10,... | collective-permute-start | bytes 331784 | tf_op jit(solution)/shard_map/ppermute | solution.py:610
  54.6 7.3 %collective-permute-start.6 = (bf16[128,256]{1,0:T(8,128)(2,1)S(1)}, bf16[128,256]{1,0:T(8,128)(2,1)S(1)}, u32[]{:S(2)}, u32[]{:S(2)}) collective-permute-start(bf16[128,256]{1,0:T(8,128)(2,1)S(1)} %copy-done.16), channel_id=1, source_target_pairs={{0,1},{1,2},{2,3},{3,4},{4,5},{5,6},{6,7},{7,8},{8,9},{9,10},{10,1... | collective-permute-start | bytes 196616 | tf_op jit(solution)/shard_map/ppermute | solution.py:605
  56.2 5.7 %collective-permute-start.7 = (bf16[128,256]{1,0:T(8,128)(2,1)S(1)}, bf16[128,256]{1,0:T(8,128)(2,1)S(1)}, u32[]{:S(2)}, u32[]{:S(2)}) collective-permute-start(bf16[128,256]{1,0:T(8,128)(2,1)S(1)} %copy-done.15), channel_id=1, source_target_pairs={{1,0},{2,1},{3,2},{4,3},{5,4},{6,5},{7,6},{8,7},{9,8},{10,9},{11,1... | collective-permute-start | bytes 196616 | tf_op jit(solution)/shard_map/ppermute | solution.py:605
  62.8 14.2 %copy-start.6 = (s32[16,27]{1,0:T(8,128)S(1)}, s32[16,27]{1,0:T(8,128)}, u32[]{:S(2)}) copy-start(s32[16,27]{1,0:T(8,128)} %adj_ref.3) | copy-start | bytes 5188
  62.9 10.5 %collective-permute-start.8 = (bf16[432,128]{1,0:T(8,128)(2,1)S(1)}, bf16[432,128]{1,0:T(8,128)(2,1)S(1)}, u32[]{:S(2)}, u32[]{:S(2)}) collective-permute-start(bf16[432,128]{1,0:T(8,128)(2,1)S(1)} %add_convert_fusion.1), channel_id=1, source_target_pairs={{0,8},{1,9},{2,10},{3,11},{4,12},{5,13},{6,14},{7,15},{8,0},{9,1},... | collective-permute-start | bytes 331784 | tf_op jit(solution)/shard_map/ppermute | solution.py:610
  73.5 6.8 %collective-permute-start.9 = (bf16[432,128]{1,0:T(8,128)(2,1)S(1)}, bf16[432,128]{1,0:T(8,128)(2,1)S(1)}, u32[]{:S(2)}, u32[]{:S(2)}) collective-permute-start(bf16[432,128]{1,0:T(8,128)(2,1)S(1)} %add_convert_fusion), channel_id=1, source_target_pairs={{0,2},{1,3},{2,0},{3,1},{4,6},{5,7},{6,4},{7,5},{8,10},{9,11},{10,... | collective-permute-start | bytes 331784 | tf_op jit(solution)/shard_map/ppermute | solution.py:610
  75.1 5.1 %collective-permute-start.10 = (bf16[432,128]{1,0:T(8,128)(2,1)S(1)}, bf16[432,128]{1,0:T(8,128)(2,1)S(1)}, u32[]{:S(2)}, u32[]{:S(2)}) collective-permute-start(bf16[432,128]{1,0:T(8,128)(2,1)S(1)} %add_convert_fusion), channel_id=1, source_target_pairs={{0,4},{1,5},{2,6},{3,7},{4,0},{5,1},{6,2},{7,3},{8,12},{9,13},{10,... | collective-permute-start | bytes 331784 | tf_op jit(solution)/shard_map/ppermute | solution.py:610
  75.1 6.0 %collective-permute-start.11 = (bf16[432,128]{1,0:T(8,128)(2,1)S(1)}, bf16[432,128]{1,0:T(8,128)(2,1)S(1)}, u32[]{:S(2)}, u32[]{:S(2)}) collective-permute-start(bf16[432,128]{1,0:T(8,128)(2,1)S(1)} %add_convert_fusion), channel_id=1, source_target_pairs={{0,6},{1,7},{2,4},{3,5},{4,2},{5,3},{6,0},{7,1},{8,14},{9,15},{10,... | collective-permute-start | bytes 331784 | tf_op jit(solution)/shard_map/ppermute | solution.py:610
  81.2 1.9 %collective-permute-start.12 = (bf16[4,432,128]{2,1,0:T(8,128)(2,1)S(1)}, bf16[4,432,128]{2,1,0:T(8,128)(2,1)S(1)}, u32[]{:S(2)}, u32[]{:S(2)}) collective-permute-start(bf16[4,432,128]{2,1,0:T(8,128)(2,1)S(1)} %pad_maximum_fusion.own_ref), channel_id=1, source_target_pairs={{0,1},{1,0},{2,3},{3,2},{4,5},{5,4},{6,7},{7,6},{8,9},{9,8},{10,11... | collective-permute-start | bytes 1327112 | tf_op jit(solution)/shard_map/ppermute | solution.py:610

commit v4 on v3

--- a/solution.py
+++ b/solution.py
@@ -59,6 +59,17 @@
     for copy in copies:
         copy.start()
     return copies
+
+
+def this_core():
+    return lax.rem(lax.axis_index("region"), 2)
+
+
+def in_place(dense_ref, near_ref, away_ref):
+    first = this_core() == 0
+    near, away = near_ref[...], away_ref[...]
+    before, after = jnp.where(first, away, near), jnp.where(first, near, away)
+    return [before] + [dense_ref[x] for x in range(dense_ref.shape[0])] + [after]
 
 
 def corner(adj_ref, t, lowest):
@@ -157,9 +168,10 @@
     )
 
 
-def dense_body(adj_ref, bricks_ref, dense_ref, low_ref, high_ref, grid_ref):
+def dense_body(adj_ref, bricks_ref, dense_ref, near_ref, away_ref, grid_ref):
     tiles, vox, channels = bricks_ref.shape
     lowest = lax.axis_index("region") * tiles
+    core = this_core()
     for t in range(tiles):
         x, y, z = corner(adj_ref, t, lowest)
         brick = bricks_ref[t].astype(F32).reshape(VX, VY, VZ, channels)
@@ -167,10 +179,8 @@
     for x in range(NX):
         slab = grid_ref[x].reshape(SLAB, channels).astype(BF)
         dense_ref[x] = slab
-        if x == 0:
-            low_ref[...] = slab
-        if x == NX - 1:
-            high_ref[...] = slab
+    near_ref[...] = dense_ref[(1 - core) * (NX - 1)]
+    away_ref[...] = dense_ref[core * (NX - 1)]
 
 
 def to_dense(adjacency, bricks):
@@ -211,12 +221,12 @@
     )
 
 
-def conv_inner(shift_ref, weights_ref, store):
+def conv_slabs(count, shift_ref, weights_ref, store):
     def step(x, carry):
         store(x, conv_slab(shift_ref, weights_ref, x))
         return carry
 
-    lax.fori_loop(0, INNER, step, 0)
+    lax.fori_loop(0, count, step, 0)
 
 
 def conv_edges(shift_ref, weights_ref, slabs):
@@ -232,7 +242,7 @@
     def store(x, value):
         grad_ref[x] = value
 
-    conv_inner(shift_ref, weights_ref, store)
+    conv_slabs(INNER, shift_ref, weights_ref, store)
 
 
 def inner_gradient(dense, weights):
@@ -243,6 +253,24 @@
         [dense, weights],
         scratch=[pltpu.VMEM((3, NX, SHIFTED, channels), BF)],
         flops=2 * INNER * SLAB * KOFF * channels * channels,
+    )[0]
+
+
+def edge_gradient_body(dense_ref, near_ref, away_ref, weights_ref, grad_ref, shift_ref):
+    slabs = in_place(dense_ref, near_ref, away_ref)
+    first, last = conv_edges(shift_ref, weights_ref, slabs[:3] + slabs[-3:])
+    grad_ref[0] = first
+    grad_ref[1] = last
+
+
+def edge_gradient(dense, near, away, weights):
+    channels = dense.shape[2]
+    return call(
+        edge_gradient_body,
+        [jax.ShapeDtypeStruct((2, SLAB, channels), F32)],
+        [dense, near, away, weights],
+        scratch=[pltpu.VMEM((3, 6, SHIFTED, channels), BF)],
+        flops=4 * SLAB * KOFF * channels * channels,
     )[0]
 
 
@@ -263,7 +291,7 @@
     def store(x, value):
         out_ref[x] = value.astype(BF)
 
-    conv_inner(shift_ref, weights_ref, store)
+    conv_slabs(INNER, shift_ref, weights_ref, store)
 
 
 def inner_forward(turned, weights):
@@ -286,7 +314,7 @@
 
 
 def edge_forward_body(
-    adj_ref, turned_far, low_ref, high_ref, weights_far, inner_far, out_ref,
+    adj_ref, turned_far, near_ref, away_ref, weights_far, inner_far, out_ref,
     shift_ref, grid_ref, turned_ref, weights_ref, inner_ref, sems,
 ):
     ends = ((0, 2 * SLAB), (DENSE - 2 * SLAB, DENSE))
@@ -300,7 +328,10 @@
         copy.start()
     tiles, vox, channels = out_ref.shape
     lowest = lax.axis_index("region") * tiles
-    before, after = upright(low_ref[...]), upright(high_ref[...])
+    first = this_core() == 0
+    near, away = near_ref[...], away_ref[...]
+    before = upright(jnp.where(first, away, near))
+    after = upright(jnp.where(first, near, away))
     for copy in copies:
         copy.wait()
     own = [upright(turned_ref[i, :, j * SLAB : (j + 1) * SLAB]) for i in range(2) for j in range(2)]
@@ -315,12 +346,12 @@
         out_ref[t] = brick.reshape(vox, channels).astype(BF)
 
 
-def edge_forward(adjacency, turned, low, high, weights, inner, tiles):
+def edge_forward(adjacency, turned, near, away, weights, inner, tiles):
     channels = turned.shape[0]
     return call(
         edge_forward_body,
         [jax.ShapeDtypeStruct((tiles, VX * VY * VZ, channels), BF)],
-        [adjacency, turned, low, high, weights, inner],
+        [adjacency, turned, near, away, weights, inner],
         smem=(0,),
         far=(1, 4, 5),
         scratch=[
@@ -377,41 +408,29 @@
         )
 
 
-def flip(array):
-    return jnp.transpose(array).astype(BF)
-
-
 def sum_rows(rows, side):
-    lower, upper = side == 0.0, side == 1.0
-    return jnp.concatenate(
-        [
-            flip(jnp.where(lower, rows, 0.0)),
-            flip(jnp.where(upper, rows, 0.0)),
-            flip(jnp.where(lower, 1.0, 0.0))[0:16],
-            flip(jnp.where(upper, 1.0, 0.0))[0:16],
-        ],
-        axis=0,
-    )
+    across, half = jnp.transpose(rows), jnp.transpose(side)[0:1]
+    parts = [jnp.where(half == h, across, 0.0) for h in (0.0, 1.0)]
+    counts = [
+        jnp.broadcast_to(jnp.where(half == h, 1.0, 0.0), (16, half.shape[1])) for h in (0.0, 1.0)
+    ]
+    return jnp.concatenate([x.astype(BF) for x in parts + counts], axis=0)
 
 
 def voxel_body(
     cap_rows,
-    adj_far, msg_far, below_far, above_far, dense_far, weights_far, grad_far,
-    turned_far, low_far, high_far, back_far,
-    adj_ref, slots_ref, rows_ref, below_ref, above_ref, dense_ref, weights_ref, grad_ref,
-    turned_ref, back_ref,
-    table_ref, pick_ref, side_ref, shift_ref, in_sems, out_sems,
+    adj_far, msg_far, grad_far, edge_far,
+    turned_far, near_far, away_far, back_far,
+    adj_ref, slots_ref, rows_ref, grad_ref, turned_ref, back_ref,
+    table_ref, pick_ref, side_ref, in_sems, out_sems,
 ):
     pairs = (
         (adj_far, adj_ref),
         (msg_far.at[:, cap_rows : cap_rows + 16], slots_ref),
-        (below_far, below_ref),
-        (above_far, above_ref),
-        (dense_far.at[0:2], dense_ref.at[0:2]),
-        (dense_far.at[NX - 2 : NX], dense_ref.at[2:4]),
-        (weights_far, weights_ref),
         (msg_far.at[:, 0:cap_rows], rows_ref),
         (grad_far, grad_ref.at[1 : NX - 1]),
+        (edge_far.at[0], grad_ref.at[0]),
+        (edge_far.at[1], grad_ref.at[NX - 1]),
     )
     copies = start_all(pairs, in_sems)
     regions, _, channels = rows_ref.shape
@@ -421,11 +440,7 @@
     columns = read_slots(cap_rows, adj_ref, slots_ref, table_ref)
     for r in range(regions):
         fill_picks(pick_ref, side_ref, columns, r, regions, cap_rows)
-    for copy in copies[2:7]:
-        copy.wait()
-    slabs = [below_ref[...]] + [dense_ref[i] for i in range(4)] + [above_ref[...]]
-    grad_ref[0], grad_ref[NX - 1] = conv_edges(shift_ref, weights_ref, slabs)
-    for copy in copies[7:]:
+    for copy in copies[2:]:
         copy.wait()
     left = sum_rows(rows_ref[...].reshape(total, channels).astype(F32), side_ref[...])
     width = 2 * LANES
@@ -440,11 +455,12 @@
             ).astype(BF)
             x = start // SLAB
             grad_ref[x] = grad_ref[x] / jnp.transpose(denom)[:, 0:1]
+    core, last = this_core(), DENSE - SLAB
     results = start_all(
         (
             (turned_ref, turned_far),
-            (turned_ref.at[:, 0:SLAB], low_far),
-            (turned_ref.at[:, DENSE - SLAB : DENSE], high_far),
+            (turned_ref.at[:, pl.ds(pl.multiple_of((1 - core) * last, SLAB), SLAB)], near_far),
+            (turned_ref.at[:, pl.ds(pl.multiple_of(core * last, SLAB), SLAB)], away_far),
         ),
         out_sems,
     )
@@ -464,7 +480,7 @@
         copy.wait()
 
 
-def voxels(adjacency, msg, below, above, dense, weights, grad, cap_rows):
+def voxels(adjacency, msg, grad, edge_grad, cap_rows):
     regions, rows, channels = msg.shape
     segs = up_to(cap_rows, LANES) // LANES
     total = regions * cap_rows
@@ -478,25 +494,20 @@
             face,
             jax.ShapeDtypeStruct(back, BF),
         ],
-        [adjacency, msg, below, above, dense, weights, grad],
-        far=range(7),
+        [adjacency, msg, grad, edge_grad],
+        far=range(4),
         far_outs=range(4),
         scratch=[
             pltpu.SMEM(adjacency.shape, jnp.int32),
             pltpu.VMEM((regions, 16, channels), BF),
             pltpu.VMEM(back, BF),
-            pltpu.VMEM(below.shape, BF),
-            pltpu.VMEM(above.shape, BF),
-            pltpu.VMEM((4, SLAB, channels), BF),
-            pltpu.VMEM(weights.shape, BF),
             pltpu.VMEM((NX, SLAB, channels), F32),
             pltpu.VMEM(turned, BF),
             pltpu.VMEM(back, BF),
             pltpu.VMEM((2 * regions, segs * LANES), F32),
             pltpu.VMEM((total, HALF), BF),
             pltpu.VMEM((total, LANES), F32),
-            pltpu.VMEM((3, 6, SHIFTED, channels), BF),
-            pltpu.SemaphoreType.DMA((9,)),
+            pltpu.SemaphoreType.DMA((6,)),
             pltpu.SemaphoreType.DMA((7,)),
         ],
         flops=4 * total * DENSE * channels,
@@ -505,11 +516,10 @@
 
 
 def weight_body(
-    scaling, turned_ref, below_ref, above_ref, dense_ref, keep_ref, send_ref, shift_ref, all_ref
+    scaling, turned_ref, near_ref, away_ref, dense_ref, keep_ref, send_ref, shift_ref, all_ref
 ):
     channels = turned_ref.shape[0]
-    slabs = [below_ref[...]] + [dense_ref[x] for x in range(NX)] + [above_ref[...]]
-    for x, slab in enumerate(slabs):
+    for x, slab in enumerate(in_place(dense_ref, near_ref, away_ref)):
         put_shifts(shift_ref, x, slab)
     left = turned_ref[...]
     for k in range(0, KOFF, 2):
@@ -529,13 +539,13 @@
     send_ref[...] = all_ref[pl.ds(pl.multiple_of((1 - core) * half, 16), half), :]
 
 
-def weight_terms(turned, below, above, dense, scaling):
+def weight_terms(turned, near, away, dense, scaling):
     channels = turned.shape[0]
     half = jax.ShapeDtypeStruct((KOFF * channels // 2, channels), F32)
     return call(
         functools.partial(weight_body, scaling),
         [half, half],
-        [turned, below, above, dense],
+        [turned, near, away, dense],
         scratch=[
             pltpu.VMEM((3, NX + 2, SHIFTED, channels), BF),
             pltpu.VMEM((KOFF * channels, channels), F32),
@@ -598,11 +608,10 @@
     )[0]
 
 
-def from_sides(low, high):
+def from_sides(near, away):
     count = lax.axis_size("region")
-    up = [(i, i + 1) for i in range(count - 1)]
-    down = [(j, i) for i, j in up]
-    return lax.ppermute(high, "region", up), lax.ppermute(low, "region", down)
+    pairs = [(i, i + 1) for i in range(1, count - 1, 2)]
+    return swapped(near, 1), lax.ppermute(away, "region", pairs + [(j, i) for i, j in pairs])
 
 
 def swapped(array, bit):
@@ -652,24 +661,37 @@
     return found
 
 
-def last_body(own_ref, other_ref, out_ref):
-    size, rows, channels = own_ref.shape
-    me = lax.axis_index("region")
-    core = lax.rem(me, 2)
-    side = lax.rem(me // 2, size)
-    for half, ref in ((core, own_ref), (1 - core, other_ref)):
-        for i in range(size):
-            at = pl.multiple_of((half * size + (side ^ i)) * rows, 16)
-            out_ref[pl.ds(at, rows), :] = ref[i].astype(F32)
-
-
-def last_step(own, other):
-    size, rows, channels = own.shape
-    return call(
-        last_body,
-        [jax.ShapeDtypeStruct((2 * size * rows, channels), F32)],
-        [own, other],
-    )[0]
+def last_body(other, pieces_ref, *refs):
+    out_far, wide_ref, sems = refs[-3:]
+    size, rows, channels = pieces_ref.shape
+    core = this_core()
+    half = 1 - core if other else core
+    side = lax.rem(lax.axis_index("region") // 2, size)
+    copies = []
+    for i in range(size):
+        wide_ref[i] = pieces_ref[i].astype(F32)
+        at = pl.multiple_of((half * size + (side ^ i)) * rows, 16)
+        copies += start_all([(wide_ref.at[i], out_far.at[pl.ds(at, rows)])], sems.at[i : i + 1])
+    for copy in copies:
+        copy.wait()
+
+
+def last_step(pieces, out=None):
+    size, rows, channels = pieces.shape
+    other = out is not None
+    return pl.pallas_call(
+        functools.partial(last_body, other),
+        out_shape=jax.ShapeDtypeStruct((2 * size * rows, channels), F32),
+        in_specs=[VMEM] + [FAR] * other,
+        out_specs=FAR,
+        scratch_shapes=[
+            pltpu.VMEM((size, rows, channels), F32),
+            pltpu.SemaphoreType.DMA((size,)),
+        ],
+        input_output_aliases={1: 0} if other else {},
+        compiler_params=pltpu.CompilerParams(vmem_limit_bytes=16 * MIB),
+        cost_estimate=pl.CostEstimate(flops=0, bytes_accessed=6 * size * rows * channels, transcendentals=0),
+    )(pieces, *([out] if other else []))
 
 
 def exchange(array):
@@ -686,26 +708,27 @@
         point_owner.reshape(1, points), point_slot.reshape(1, points), point_feats, regions, cap_rows
     )
     received = exchange(msg)
-    cot, cot_low, cot_high = to_dense(adjacency, cotangent)
-    below, above = from_sides(cot_low, cot_high)
+    cot, cot_near, cot_away = to_dense(adjacency, cotangent)
+    near, away = from_sides(cot_near, cot_away)
     mirrored = jnp.transpose(kernel[::-1], (0, 2, 1)).reshape(KOFF * channels, channels)
     grad = inner_gradient(cot, mirrored)
+    edge_grad = edge_gradient(cot, near, away, mirrored)
     scaling = 1.0 / math.sqrt(tiles * regions * vox)
-    turned, low, high, back = voxels(
-        adjacency, received, below, above, cot, mirrored, grad, cap_rows
-    )
+    turned, feats_near, feats_away, back = voxels(adjacency, received, grad, edge_grad, cap_rows)
     returned = exchange(back)
-    keep, send = weight_terms(turned, below, above, cot, scaling)
+    keep, send = weight_terms(turned, near, away, cot, scaling)
     groups = groups_of(regions)
     bit, size = groups[0]
     term, *sent = split(keep, swapped(send, 1), size)
     weights = kernel.reshape(KOFF * channels, channels)
-    turned, low, high, *sent = lax.optimization_barrier((turned, low, high, *sent))
-    feats_below, feats_above = from_sides(low, high)
+    turned, feats_near, feats_away, *sent = lax.optimization_barrier(
+        (turned, feats_near, feats_away, *sent)
+    )
+    feats_near, feats_away = from_sides(feats_near, feats_away)
     inner = inner_forward(turned, weights)
     got = [swapped(part, bit * (i + 1)) for i, part in enumerate(sent)]
-    got, returned, inner, feats_below, feats_above = lax.optimization_barrier(
-        (got, returned, inner, feats_below, feats_above)
+    got, returned, inner, feats_near, feats_away = lax.optimization_barrier(
+        (got, returned, inner, feats_near, feats_away)
     )
     for part in got:
         term = term + part.astype(F32)
@@ -718,10 +741,10 @@
         side = (lax.axis_index("region") // bit) % size
         term = in_order(gather_group(term, bit, size), side)
     term, grad_points = lax.optimization_barrier((term, grad_points))
-    out_tiles = edge_forward(adjacency, turned, feats_below, feats_above, weights, inner, tiles)
+    out_tiles = edge_forward(adjacency, turned, feats_near, feats_away, weights, inner, tiles)
     own = jnp.stack(gather_group(term, *groups[0]))
     own, out_tiles = lax.optimization_barrier((own, out_tiles))
-    grad_weight = last_step(own, swapped(own, 1)).reshape(KOFF, channels, channels)
+    grad_weight = last_step(swapped(own, 1), last_step(own)).reshape(KOFF, channels, channels)
     return out_tiles, grad_points, grad_weight
 
 

time: 85 us -> 82.9 us (0.975)
  starting transfers between devices: 33.2 us -> 27.5 us
  waiting for transfers between devices: 14.8 us -> 17.3 us
    ppermute x4 -> x2, starting transfers between devices: 6.45 us -> 1.5 us  [from_sides(): lax.ppermute(away, 'region', pairs + [(j, i) for i, j in pairs])]
    ppermute x9 -> x11, waiting for transfers between devices: 8.03 us -> 11.3 us  [swapped(): return lax.ppermute(array, 'region', [(i, i ^ bit) for i in range(count)])]
    pallas_call x0 -> x2, Pallas kernels: none -> 1.91 us  [last_step(): pl.pallas_call(functools.partial(last_body, other), out_shape=jax.ShapeDt...]
    ppermute x9 -> x11, starting transfers between devices: 13.4 us -> 11.5 us  [swapped(): return lax.ppermute(array, 'region', [(i, i ^ bit) for i in range(count)])]
    transpose x2, local copies, waits for them, and re-layouts: 1.4 us -> 2.89 us  [local(): jnp.transpose(kernel[::-1], (0, 2, 1)).reshape(KOFF * channels, channels)]
    pallas_call x10, Pallas kernels: 30.2 us -> 28.9 us  [call(): pl.pallas_call(body, out_shape=outs, in_specs=[SMEM if i in smem else FAR...]
    all_to_all x2, starting transfers between devices: 13.4 us -> 14.5 us  [exchange(): lax.all_to_all(array, 'region', split_axis=0, concat_axis=0, tiled=True)]
    unnamed x34 -> x22, local copies, waits for them, and re-layouts: 3.65 us -> 2.64 us
  transfers between devices with their start and end apart: 15 -> 15, of which waited for: 6 -> 6; matrix products, arithmetic and copies ran while one was open for 2% -> 4% of each run, Pallas kernels for 21% -> 24%
where the time goes in v4:
time: 82.9 us; the launch traced here: 82.4 us
  Pallas kernels  30.8 us (37%)
  starting transfers between devices  27.5 us (33%)
  waiting for transfers between devices  17.3 us (21%)
  local copies, waits for them, and re-layouts  5.53 us (7%)
  between operations  1.08 us (1%)
    pallas_call x10, Pallas kernels, call(): pl.pallas_call(body, out_shape=outs, in_specs=[SMEM if i in smem else FAR...  28.9 us
    all_to_all x2, starting transfers between devices, exchange(): lax.all_to_all(array, 'region', split_axis=0, concat_axis=0, tiled=True)  14.5 us
    ppermute x11, starting transfers between devices, swapped(): return lax.ppermute(array, 'region', [(i, i ^ bit) for i in range(count)])  11.5 us
    ppermute x11, waiting for transfers between devices, swapped(): return lax.ppermute(array, 'region', [(i, i ^ bit) for i in range(count)])  11.3 us
    all_to_all x2, waiting for transfers between devices, exchange(): lax.all_to_all(array, 'region', split_axis=0, concat_axis=0, tiled=True)  6.02 us
    transpose x2, local copies, waits for them, and re-layouts, local(): jnp.transpose(kernel[::-1], (0, 2, 1)).reshape(KOFF * channels, channels)  2.89 us
    unnamed x22, local copies, waits for them, and re-layouts  2.64 us
    pallas_call x2, Pallas kernels, last_step(): pl.pallas_call(functools.partial(last_body, other), out_shape=jax.ShapeDt...  1.91 us
  transfers between devices with their start and end apart: 15, of which 6 were waited for; matrix products, arithmetic and copies ran while one was open for 4% of the time, Pallas kernels for 24%

profile of v4, /device:TPU:0, one launch (start us, length us, event | category | flops | bytes accessed | tf_op | source)
XLA Modules:
  0.0 82.4 jit_solution(7085137375787645675)
XLA Ops:
  0.7 3.6 %shard_map.85 = (bf16[16,176,128]{2,1,0:T(8,128)(2,1)}, f32[8,1024]{1,0:T(8,128)}) custom-call(s32[1,1024]{1,0:T(1,128)} %bitcast.20, s32[1,1024]{1,0:T(1,128)} %bitcast.21, bf16[1024,128]{1,0:T(8,128)(2,1)} %feats_far.1), custom_call_target="tpu_custom_call" | custom-call | flops 671088640 | bytes 1024000 | tf_op jit(solution)/shard_map/pallas_call | solution.py:46
  4.3 7.4 %all-to-all-start = ((bf16[16,176,128]{2,1,0:T(8,128)(2,1)}), bf16[16,176,128]{2,1,0:T(8,128)(2,1)}, u32[]{:S(2)}, u32[]{:S(2)}) async-start(bf16[16,176,128]{2,1,0:T(8,128)(2,1)} %get-tuple-element.37), calls=%async_computation | async-start | bytes 1441792 | tf_op jit(solution)/shard_map/all_to_all | solution.py:698
  11.8 0.9 %shard_map.86 = (bf16[8,256,128]{2,1,0:T(8,128)(2,1)S(1)}, bf16[256,128]{1,0:T(8,128)(2,1)S(1)}, bf16[256,128]{1,0:T(8,128)(2,1)S(1)}) custom-call(s32[16,27]{1,0:T(8,128)S(1)} %copy-done.5, bf16[16,128,128]{2,1,0:T(8,128)(2,1)S(1)} %copy-done.3), custom_call_target="tpu_custom_call" | custom-call | bytes 1181376 | tf_op jit(solution)/shard_map/pallas_call | solution.py:46
  13.1 0.7 collective-permute-start.1
  13.8 1.0 %reverse_bitcast_fusion = bf16[27,128,128]{1,2,0:T(8,128)(2,1)} fusion(bf16[27,128,128]{2,1,0:T(8,128)(2,1)S(1)} %copy-done), kind=kLoop, calls=%fused_computation | loop fusion | bytes 1769472 | tf_op jit(solution)/shard_map/transpose | solution.py:713
  14.8 1.9 %copy.10 = bf16[27,128,128]{2,1,0:T(8,128)(2,1)S(1)} copy(bf16[27,128,128]{1,2,0:T(8,128)(2,1)} %reverse_bitcast_fusion) | data formatting | bytes 1769472 | tf_op jit(solution)/shard_map/transpose | solution.py:713
  16.6 4.1 %shard_map.87.grad_far = f32[6,256,128]{2,1,0:T(8,128)S(1)} custom-call(bf16[8,256,128]{2,1,0:T(8,128)(2,1)S(1)} %get-tuple-element.38.dense_ref, bf16[3456,128]{1,0:T(8,128)(2,1)S(1)} %bitcast.13), custom_call_target="tpu_custom_call" | custom-call | flops 1358954496 | bytes 2195456 | tf_op jit(solution)/shard_map/pallas_call | solution.py:46
  20.8 0.9 %copy-done.7 = f32[6,256,128]{2,1,0:T(8,128)} copy-done((f32[6,256,128]{2,1,0:T(8,128)}, f32[6,256,128]{2,1,0:T(8,128)S(1)}, u32[]{:S(2)}) %copy-start.7) | copy-done | bytes 786456
  21.6 1.1 %shard_map.88.edge_far = f32[2,256,128]{2,1,0:T(8,128)S(1)} custom-call(bf16[8,256,128]{2,1,0:T(8,128)(2,1)S(1)} %get-tuple-element.38.dense_ref, bf16[256,128]{1,0:T(8,128)(2,1)S(1)} %collective-permute-done.near_ref, bf16[256,128]{1,0:T(8,128)(2,1)S(1)} %collective-permute-done.1.away_ref, bf16[3456,128]{1,0:T(8,128)(2,1)S(1)} %bitcast.14), custom_call_target="tpu_custom_call" | custom-call | flops 452984832 | bytes 1802240 | tf_op jit(solution)/shard_map/pallas_call | solution.py:46
  22.7 0.7 copy-done.4
  23.4 6.0 %all-to-all-done.msg_far = bf16[16,176,128]{2,1,0:T(8,128)(2,1)} async-done(((bf16[16,176,128]{2,1,0:T(8,128)(2,1)}), bf16[16,176,128]{2,1,0:T(8,128)(2,1)}, u32[]{:S(2)}, u32[]{:S(2)}) %all-to-all-start) | async-done | bytes 720928 | tf_op jit(solution)/shard_map/all_to_all | solution.py:698
  29.5 6.5 %shard_map.89 = (bf16[128,2048]{1,0:T(8,128)(2,1)}, bf16[128,256]{1,0:T(8,128)(2,1)}, bf16[128,256]{1,0:T(8,128)(2,1)}, bf16[16,160,128]{2,1,0:T(8,128)(2,1)}) custom-call(s32[16,27]{1,0:T(8,128)} %adj_ref.3, bf16[16,176,128]{2,1,0:T(8,128)(2,1)} %all-to-all-done.msg_far, f32[6,256,128]{2,1,0:T(8,128)} %copy-done.7, f32[2,256,128]{2,1,0:T(8,128)} %copy-done.4), custom_call_target="tpu_custom_call" | custom-call | flops 2684354560 | bytes 3081920 | tf_op jit(solution)/shard_map/pallas_call | solution.py:46
  35.9 7.1 %all-to-all-start.1 = ((bf16[16,160,128]{2,1,0:T(8,128)(2,1)}), bf16[16,160,128]{2,1,0:T(8,128)(2,1)S(1)}, u32[]{:S(2)}, u32[]{:S(2)}) async-start(bf16[16,160,128]{2,1,0:T(8,128)(2,1)} %get-tuple-element.53), calls=%async_computation.1 | async-start | bytes 1310720 | tf_op jit(solution)/shard_map/all_to_all | solution.py:698
  43.1 1.0 %copy-done.1 = bf16[128,2048]{1,0:T(8,128)(2,1)S(1)} copy-done((bf16[128,2048]{1,0:T(8,128)(2,1)S(1)}, bf16[128,2048]{1,0:T(8,128)(2,1)}, u32[]{:S(2)}) %copy-start.1) | copy-done | bytes 524312
  44.1 2.6 %shard_map.90 = (f32[1728,128]{1,0:T(8,128)S(1)}, f32[1728,128]{1,0:T(8,128)S(1)}) custom-call(bf16[128,2048]{1,0:T(8,128)(2,1)S(1)} %copy-done.1, bf16[256,128]{1,0:T(8,128)(2,1)S(1)} %collective-permute-done.near_ref, bf16[256,128]{1,0:T(8,128)(2,1)S(1)} %collective-permute-done.1.away_ref, bf16[8,256,128]{2,1,0:T(8,128)(2,1)S(1)} %get-tuple-element.38.dense_ref), custom_call_target="tpu_custom_call" | custom-call | flops 1811939328 | bytes 2949120 | tf_op jit(solution)/shard_map/pallas_call | solution.py:46
  46.7 0.5 collective-permute-start.2
  47.2 2.1 %collective-permute-done.2.got_ref = f32[1728,128]{1,0:T(8,128)S(1)} collective-permute-done((f32[1728,128]{1,0:T(8,128)S(1)}, f32[1728,128]{1,0:T(8,128)S(1)}, u32[]{:S(2)}, u32[]{:S(2)}) %collective-permute-start.2) | collective-permute-done | bytes 884768 | tf_op jit(solution)/shard_map/ppermute | solution.py:619
  49.4 2.0 %collective-permute-start.3 = (bf16[432,128]{1,0:T(8,128)(2,1)S(1)}, bf16[432,128]{1,0:T(8,128)(2,1)S(1)}, u32[]{:S(2)}, u32[]{:S(2)}) collective-permute-start(bf16[432,128]{1,0:T(8,128)(2,1)S(1)} %get-tuple-element.50), channel_id=1, source_target_pairs={{0,2},{1,3},{2,0},{3,1},{4,6},{5,7},{6,4},{7,5},{8,10},{9,11},{10,... | collective-permute-start | bytes 331784 | tf_op jit(solution)/shard_map/ppermute | solution.py:619
  51.3 1.5 %collective-permute-start.4 = (bf16[432,128]{1,0:T(8,128)(2,1)S(1)}, bf16[432,128]{1,0:T(8,128)(2,1)S(1)}, u32[]{:S(2)}, u32[]{:S(2)}) collective-permute-start(bf16[432,128]{1,0:T(8,128)(2,1)S(1)} %get-tuple-element.51), channel_id=1, source_target_pairs={{0,4},{1,5},{2,6},{3,7},{4,0},{5,1},{6,2},{7,3},{8,12},{9,13},{10,... | collective-permute-start | bytes 331784 | tf_op jit(solution)/shard_map/ppermute | solution.py:619
  52.9 0.8 %collective-permute-start.7 = (bf16[128,256]{1,0:T(8,128)(2,1)S(1)}, bf16[128,256]{1,0:T(8,128)(2,1)S(1)}, u32[]{:S(2)}, u32[]{:S(2)}) collective-permute-start(bf16[128,256]{1,0:T(8,128)(2,1)S(1)} %copy-done.9), channel_id=1, source_target_pairs={{1,2},{3,4},{5,6},{7,8},{9,10},{11,12},{13,14},{2,1},{4,3},{6,5},{... | collective-permute-start | bytes 196616 | tf_op jit(solution)/shard_map/ppermute | solution.py:614
  53.8 4.4 %shard_map.92.inner_far = bf16[6,256,128]{2,1,0:T(8,128)(2,1)S(1)} custom-call(bf16[128,2048]{1,0:T(8,128)(2,1)S(1)} %copy-done.2, bf16[3456,128]{1,0:T(8,128)(2,1)S(1)} %bitcast.11), custom_call_target="tpu_custom_call" | custom-call | bytes 1024 | tf_op jit(solution)/shard_map/pallas_call | solution.py:46
  58.2 4.1 %collective-permute-done.5 = bf16[432,128]{1,0:T(8,128)(2,1)S(1)} collective-permute-done((bf16[432,128]{1,0:T(8,128)(2,1)S(1)}, bf16[432,128]{1,0:T(8,128)(2,1)S(1)}, u32[]{:S(2)}, u32[]{:S(2)}) %collective-permute-start.5) | collective-permute-done | bytes 110624 | tf_op jit(solution)/shard_map/ppermute | solution.py:619
  62.4 3.4 %collective-permute-start.8 = (bf16[432,128]{1,0:T(8,128)(2,1)S(1)}, bf16[432,128]{1,0:T(8,128)(2,1)S(1)}, u32[]{:S(2)}, u32[]{:S(2)}) collective-permute-start(bf16[432,128]{1,0:T(8,128)(2,1)S(1)} %add_convert_fusion.1), channel_id=1, source_target_pairs={{0,8},{1,9},{2,10},{3,11},{4,12},{5,13},{6,14},{7,15},{8,0},{9,1},... | collective-permute-start | bytes 331784 | tf_op jit(solution)/shard_map/ppermute | solution.py:619
  65.8 2.4 %shard_map.93 = bf16[1024,128]{1,0:T(8,128)(2,1)} custom-call(f32[8,1024]{1,0:T(8,128)S(1)} %copy-done.8, bf16[16,160,128]{2,1,0:T(8,128)(2,1)S(1)} %all-to-all-done.1.rows_ref), custom_call_target="tpu_custom_call" | custom-call | flops 671088640 | bytes 950272 | tf_op jit(solution)/shard_map/pallas_call | solution.py:46
  68.2 3.3 %collective-permute-done.8 = bf16[432,128]{1,0:T(8,128)(2,1)S(1)} collective-permute-done((bf16[432,128]{1,0:T(8,128)(2,1)S(1)}, bf16[432,128]{1,0:T(8,128)(2,1)S(1)}, u32[]{:S(2)}, u32[]{:S(2)}) %collective-permute-start.8) | collective-permute-done | bytes 110624 | tf_op jit(solution)/shard_map/ppermute | solution.py:619
  72.0 1.7 %collective-permute-start.10 = (bf16[432,128]{1,0:T(8,128)(2,1)S(1)}, bf16[432,128]{1,0:T(8,128)(2,1)S(1)}, u32[]{:S(2)}, u32[]{:S(2)}) collective-permute-start(bf16[432,128]{1,0:T(8,128)(2,1)S(1)} %add_convert_fusion), channel_id=1, source_target_pairs={{0,4},{1,5},{2,6},{3,7},{4,0},{5,1},{6,2},{7,3},{8,12},{9,13},{10,... | collective-permute-start | bytes 331784 | tf_op jit(solution)/shard_map/ppermute | solution.py:619
  73.6 1.5 %collective-permute-start.9 = (bf16[432,128]{1,0:T(8,128)(2,1)S(1)}, bf16[432,128]{1,0:T(8,128)(2,1)S(1)}, u32[]{:S(2)}, u32[]{:S(2)}) collective-permute-start(bf16[432,128]{1,0:T(8,128)(2,1)S(1)} %add_convert_fusion), channel_id=1, source_target_pairs={{0,2},{1,3},{2,0},{3,1},{4,6},{5,7},{6,4},{7,5},{8,10},{9,11},{10,... | collective-permute-start | bytes 331784 | tf_op jit(solution)/shard_map/ppermute | solution.py:619
  75.1 3.2 %shard_map.94 = bf16[16,128,128]{2,1,0:T(8,128)(2,1)} custom-call(s32[16,27]{1,0:T(8,128)S(1)} %copy-done.6, bf16[128,2048]{1,0:T(8,128)(2,1)S(1)} %copy-done.2, bf16[128,256]{1,0:T(8,128)(2,1)S(1)} %collective-permute-done.6.near_ref, bf16[128,256]{1,0:T(8,128)(2,1)S(1)} %collective-permute-done.7.away_ref, bf16[3456,128]{1,0:T(8,128)(2,1)S(1)} %bitcast.12, ...), custom_call_target="tpu_custom_call" | custom-call | flops 452984832 | bytes 2459328 | tf_op jit(solution)/shard_map/pallas_call | solution.py:46
  78.4 1.0 %collective-permute-done.9 = bf16[432,128]{1,0:T(8,128)(2,1)S(1)} collective-permute-done((bf16[432,128]{1,0:T(8,128)(2,1)S(1)}, bf16[432,128]{1,0:T(8,128)(2,1)S(1)}, u32[]{:S(2)}, u32[]{:S(2)}) %collective-permute-start.9) | collective-permute-done | bytes 110624 | tf_op jit(solution)/shard_map/ppermute | solution.py:619
  79.6 1.0 %shard_map.95.refs_0_ = f32[3456,128]{1,0:T(8,128)} custom-call(bf16[4,432,128]{2,1,0:T(8,128)(2,1)S(1)} %pad_maximum_fusion.pieces_ref), custom_call_target="tpu_custom_call" | custom-call | bytes 1327104 | tf_op jit(solution)/shard_map/pallas_call | solution.py:682
  80.5 0.8 collective-permute-done.12.pieces_ref
  81.3 1.0 %shard_map.96 = f32[3456,128]{1,0:T(8,128)} custom-call(bf16[4,432,128]{2,1,0:T(8,128)(2,1)S(1)} %collective-permute-done.12.pieces_ref, f32[3456,128]{1,0:T(8,128)} %shard_map.95.refs_0_), custom_call_target="tpu_custom_call", output_to_operand_aliasing={{}: (1, {})} | custom-call | bytes 1327104 | tf_op jit(solution)/shard_map/pallas_call | solution.py:682
  (37 shorter events, 1.4 us)
Async XLA Ops:
  0.6 11.1 %copy-start.3 = (bf16[16,128,128]{2,1,0:T(8,128)(2,1)S(1)}, bf16[16,128,128]{2,1,0:T(8,128)(2,1)}, u32[]{:S(2)}) copy-start(bf16[16,128,128]{2,1,0:T(8,128)(2,1)} %bricks_ref.1) | copy-start | bytes 1572868
  0.6 11.1 %copy-start.5 = (s32[16,27]{1,0:T(8,128)S(1)}, s32[16,27]{1,0:T(8,128)}, u32[]{:S(2)}) copy-start(s32[16,27]{1,0:T(8,128)} %adj_ref.3) | copy-start | bytes 5188
  0.7 13.1 %copy-start = (bf16[27,128,128]{2,1,0:T(8,128)(2,1)S(1)}, bf16[27,128,128]{2,1,0:T(8,128)(2,1)}, u32[]{:S(2)}) copy-start(bf16[27,128,128]{2,1,0:T(8,128)(2,1)} %param.10) | copy-start | bytes 2654212
  4.3 25.1 %all-to-all-start = ((bf16[16,176,128]{2,1,0:T(8,128)(2,1)}), bf16[16,176,128]{2,1,0:T(8,128)(2,1)}, u32[]{:S(2)}, u32[]{:S(2)}) async-start(bf16[16,176,128]{2,1,0:T(8,128)(2,1)} %get-tuple-element.37), calls=%async_computation | async-start | bytes 1441792 | tf_op jit(solution)/shard_map/all_to_all | solution.py:698
  12.7 9.0 %collective-permute-start = (bf16[256,128]{1,0:T(8,128)(2,1)S(1)}, bf16[256,128]{1,0:T(8,128)(2,1)S(1)}, u32[]{:S(2)}, u32[]{:S(2)}) collective-permute-start(bf16[256,128]{1,0:T(8,128)(2,1)S(1)} %get-tuple-element.39), channel_id=1, source_target_pairs={{0,1},{1,0},{2,3},{3,2},{4,5},{5,4},{6,7},{7,6},{8,9},{9,8},{10,11... | collective-permute-start | bytes 196616 | tf_op jit(solution)/shard_map/ppermute | solution.py:619
  13.1 8.6 %collective-permute-start.1 = (bf16[256,128]{1,0:T(8,128)(2,1)S(1)}, bf16[256,128]{1,0:T(8,128)(2,1)S(1)}, u32[]{:S(2)}, u32[]{:S(2)}) collective-permute-start(bf16[256,128]{1,0:T(8,128)(2,1)S(1)} %get-tuple-element.40), channel_id=1, source_target_pairs={{1,2},{3,4},{5,6},{7,8},{9,10},{11,12},{13,14},{2,1},{4,3},{6,5},{... | collective-permute-start | bytes 196616 | tf_op jit(solution)/shard_map/ppermute | solution.py:614
  20.7 0.9 %copy-start.7 = (f32[6,256,128]{2,1,0:T(8,128)}, f32[6,256,128]{2,1,0:T(8,128)S(1)}, u32[]{:S(2)}) copy-start(f32[6,256,128]{2,1,0:T(8,128)S(1)} %shard_map.87.grad_far) | copy-start | bytes 2359300
  22.7 0.7 copy-start.4
  35.9 26.4 %all-to-all-start.1 = ((bf16[16,160,128]{2,1,0:T(8,128)(2,1)}), bf16[16,160,128]{2,1,0:T(8,128)(2,1)S(1)}, u32[]{:S(2)}, u32[]{:S(2)}) async-start(bf16[16,160,128]{2,1,0:T(8,128)(2,1)} %get-tuple-element.53), calls=%async_computation.1 | async-start | bytes 1310720 | tf_op jit(solution)/shard_map/all_to_all | solution.py:698
  43.0 1.0 %copy-start.1 = (bf16[128,2048]{1,0:T(8,128)(2,1)S(1)}, bf16[128,2048]{1,0:T(8,128)(2,1)}, u32[]{:S(2)}) copy-start(bf16[128,2048]{1,0:T(8,128)(2,1)} %get-tuple-element.54.turned_ref.turned_far) | copy-start | bytes 1572868
  46.7 6.2 %copy-start.10 = (bf16[128,256]{1,0:T(8,128)(2,1)S(1)}, bf16[128,256]{1,0:T(8,128)(2,1)}, u32[]{:S(2)}) copy-start(bf16[128,256]{1,0:T(8,128)(2,1)} %get-tuple-element.55) | copy-start | bytes 196612
  46.7 6.2 %copy-start.9 = (bf16[128,256]{1,0:T(8,128)(2,1)S(1)}, bf16[128,256]{1,0:T(8,128)(2,1)}, u32[]{:S(2)}) copy-start(bf16[128,256]{1,0:T(8,128)(2,1)} %get-tuple-element.56) | copy-start | bytes 196612
  46.7 7.1 %copy-start.2 = (bf16[128,2048]{1,0:T(8,128)(2,1)S(1)}, bf16[128,2048]{1,0:T(8,128)(2,1)}, u32[]{:S(2)}) copy-start(bf16[128,2048]{1,0:T(8,128)(2,1)} %get-tuple-element.54.turned_ref.turned_far) | copy-start | bytes 1572868
  46.7 2.5 %collective-permute-start.2 = (f32[1728,128]{1,0:T(8,128)S(1)}, f32[1728,128]{1,0:T(8,128)S(1)}, u32[]{:S(2)}, u32[]{:S(2)}) collective-permute-start(f32[1728,128]{1,0:T(8,128)S(1)} %get-tuple-element.43), channel_id=1, source_target_pairs={{0,1},{1,0},{2,3},{3,2},{4,5},{5,4},{6,7},{7,6},{8,9},{9,8},{10,11... | collective-permute-start | bytes 2654216 | tf_op jit(solution)/shard_map/ppermute | solution.py:619
  49.3 16.6 %copy-start.8 = (f32[8,1024]{1,0:T(8,128)S(1)}, f32[8,1024]{1,0:T(8,128)}, u32[]{:S(2)}) copy-start(f32[8,1024]{1,0:T(8,128)} %get-tuple-element.62.place_ref) | copy-start | bytes 98308
  49.4 8.8 %collective-permute-start.3 = (bf16[432,128]{1,0:T(8,128)(2,1)S(1)}, bf16[432,128]{1,0:T(8,128)(2,1)S(1)}, u32[]{:S(2)}, u32[]{:S(2)}) collective-permute-start(bf16[432,128]{1,0:T(8,128)(2,1)S(1)} %get-tuple-element.50), channel_id=1, source_target_pairs={{0,2},{1,3},{2,0},{3,1},{4,6},{5,7},{6,4},{7,5},{8,10},{9,11},{10,... | collective-permute-start | bytes 331784 | tf_op jit(solution)/shard_map/ppermute | solution.py:619
  51.3 6.9 %collective-permute-start.4 = (bf16[432,128]{1,0:T(8,128)(2,1)S(1)}, bf16[432,128]{1,0:T(8,128)(2,1)S(1)}, u32[]{:S(2)}, u32[]{:S(2)}) collective-permute-start(bf16[432,128]{1,0:T(8,128)(2,1)S(1)} %get-tuple-element.51), channel_id=1, source_target_pairs={{0,4},{1,5},{2,6},{3,7},{4,0},{5,1},{6,2},{7,3},{8,12},{9,13},{10,... | collective-permute-start | bytes 331784 | tf_op jit(solution)/shard_map/ppermute | solution.py:619
  52.8 9.6 %collective-permute-start.5 = (bf16[432,128]{1,0:T(8,128)(2,1)S(1)}, bf16[432,128]{1,0:T(8,128)(2,1)S(1)}, u32[]{:S(2)}, u32[]{:S(2)}) collective-permute-start(bf16[432,128]{1,0:T(8,128)(2,1)S(1)} %get-tuple-element.52), channel_id=1, source_target_pairs={{0,6},{1,7},{2,4},{3,5},{4,2},{5,3},{6,0},{7,1},{8,14},{9,15},{10,... | collective-permute-start | bytes 331784 | tf_op jit(solution)/shard_map/ppermute | solution.py:619
  52.9 5.2 %collective-permute-start.6 = (bf16[128,256]{1,0:T(8,128)(2,1)S(1)}, bf16[128,256]{1,0:T(8,128)(2,1)S(1)}, u32[]{:S(2)}, u32[]{:S(2)}) collective-permute-start(bf16[128,256]{1,0:T(8,128)(2,1)S(1)} %copy-done.10), channel_id=1, source_target_pairs={{0,1},{1,0},{2,3},{3,2},{4,5},{5,4},{6,7},{7,6},{8,9},{9,8},{10,11... | collective-permute-start | bytes 196616 | tf_op jit(solution)/shard_map/ppermute | solution.py:619
  52.9 5.3 %collective-permute-start.7 = (bf16[128,256]{1,0:T(8,128)(2,1)S(1)}, bf16[128,256]{1,0:T(8,128)(2,1)S(1)}, u32[]{:S(2)}, u32[]{:S(2)}) collective-permute-start(bf16[128,256]{1,0:T(8,128)(2,1)S(1)} %copy-done.9), channel_id=1, source_target_pairs={{1,2},{3,4},{5,6},{7,8},{9,10},{11,12},{13,14},{2,1},{4,3},{6,5},{... | collective-permute-start | bytes 196616 | tf_op jit(solution)/shard_map/ppermute | solution.py:614
  62.4 12.7 %copy-start.6 = (s32[16,27]{1,0:T(8,128)S(1)}, s32[16,27]{1,0:T(8,128)}, u32[]{:S(2)}) copy-start(s32[16,27]{1,0:T(8,128)} %adj_ref.3) | copy-start | bytes 5188
  62.4 9.1 %collective-permute-start.8 = (bf16[432,128]{1,0:T(8,128)(2,1)S(1)}, bf16[432,128]{1,0:T(8,128)(2,1)S(1)}, u32[]{:S(2)}, u32[]{:S(2)}) collective-permute-start(bf16[432,128]{1,0:T(8,128)(2,1)S(1)} %add_convert_fusion.1), channel_id=1, source_target_pairs={{0,8},{1,9},{2,10},{3,11},{4,12},{5,13},{6,14},{7,15},{8,0},{9,1},... | collective-permute-start | bytes 331784 | tf_op jit(solution)/shard_map/ppermute | solution.py:619
  71.6 6.8 %collective-permute-start.11 = (bf16[432,128]{1,0:T(8,128)(2,1)S(1)}, bf16[432,128]{1,0:T(8,128)(2,1)S(1)}, u32[]{:S(2)}, u32[]{:S(2)}) collective-permute-start(bf16[432,128]{1,0:T(8,128)(2,1)S(1)} %add_convert_fusion), channel_id=1, source_target_pairs={{0,6},{1,7},{2,4},{3,5},{4,2},{5,3},{6,0},{7,1},{8,14},{9,15},{10,... | collective-permute-start | bytes 331784 | tf_op jit(solution)/shard_map/ppermute | solution.py:619
  72.0 6.4 %collective-permute-start.10 = (bf16[432,128]{1,0:T(8,128)(2,1)S(1)}, bf16[432,128]{1,0:T(8,128)(2,1)S(1)}, u32[]{:S(2)}, u32[]{:S(2)}) collective-permute-start(bf16[432,128]{1,0:T(8,128)(2,1)S(1)} %add_convert_fusion), channel_id=1, source_target_pairs={{0,4},{1,5},{2,6},{3,7},{4,0},{5,1},{6,2},{7,3},{8,12},{9,13},{10,... | collective-permute-start | bytes 331784 | tf_op jit(solution)/shard_map/ppermute | solution.py:619
  73.6 5.8 %collective-permute-start.9 = (bf16[432,128]{1,0:T(8,128)(2,1)S(1)}, bf16[432,128]{1,0:T(8,128)(2,1)S(1)}, u32[]{:S(2)}, u32[]{:S(2)}) collective-permute-start(bf16[432,128]{1,0:T(8,128)(2,1)S(1)} %add_convert_fusion), channel_id=1, source_target_pairs={{0,2},{1,3},{2,0},{3,1},{4,6},{5,7},{6,4},{7,5},{8,10},{9,11},{10,... | collective-permute-start | bytes 331784 | tf_op jit(solution)/shard_map/ppermute | solution.py:619
  79.5 1.9 %collective-permute-start.12 = (bf16[4,432,128]{2,1,0:T(8,128)(2,1)S(1)}, bf16[4,432,128]{2,1,0:T(8,128)(2,1)S(1)}, u32[]{:S(2)}, u32[]{:S(2)}) collective-permute-start(bf16[4,432,128]{2,1,0:T(8,128)(2,1)S(1)} %pad_maximum_fusion.pieces_ref), channel_id=1, source_target_pairs={{0,1},{1,0},{2,3},{3,2},{4,5},{5,4},{6,7},{7,6},{8,9},{9,8},{10,11... | collective-permute-start | bytes 1327112 | tf_op jit(solution)/shard_map/ppermute | solution.py:619

commit v5 on v4

--- a/solution.py
+++ b/solution.py
@@ -105,6 +105,8 @@
     carry = jnp.zeros((regions, 1), F32)
     ranks = []
     for start in range(0, points, LANES):
+        if start == points // 2:
+            early = carry
         seg = marks[:, start : start + LANES]
         pre = jnp.dot(marks_bf[:, start : start + LANES], earlier, preferred_element_type=F32)
         ranks.append(jnp.sum((pre + carry) * seg, axis=0, keepdims=True))
@@ -117,17 +119,22 @@
     row = iota((LANES, points), 0, F32).astype(BF)
     one = jnp.where(row == within, jnp.ones_like(row), jnp.zeros_like(row))
     copies[2].wait()
-    feats = feats_ref[...]
+    halves = jnp.concatenate([feats_ref[0 : points // 2], feats_ref[points // 2 : points]], axis=1)
+    rank_row = iota((cap_rows, LANES), 0, F32)
     chunk = math.lcm(cap_rows, LANES)
     for start in range(0, regions * cap_rows, chunk):
         picks = [
             jnp.where(block == jnp.asarray(q, BF), one, jnp.zeros_like(one))
             for q in range(start // LANES, (start + chunk) // LANES)
         ]
+        picks = [pick[:, 0 : points // 2] + pick[:, points // 2 : points] for pick in picks]
         picker = jnp.concatenate(picks, axis=0)
-        rows = jnp.dot(picker, feats, preferred_element_type=F32).astype(BF)
+        both = jnp.dot(picker, halves, preferred_element_type=F32)
         for i in range(chunk // cap_rows):
-            msg_ref[start // cap_rows + i, 0:cap_rows, :] = rows[i * cap_rows : (i + 1) * cap_rows]
+            o = start // cap_rows + i
+            late = rank_row >= jnp.broadcast_to(early[o : o + 1], (cap_rows, LANES))
+            rows = both[i * cap_rows : (i + 1) * cap_rows]
+            msg_ref[o, 0:cap_rows, :] = jnp.where(late, rows[:, LANES:], rows[:, 0:LANES]).astype(BF)
     high = jnp.where(mine, (slot >> 7) + 1, 0).astype(F32)
     low = jnp.where(mine, slot & (LANES - 1), 0).astype(F32)
     values = jnp.concatenate([high, low], axis=0).astype(BF)

time: 82.9 us -> 82.2 us (level)
  no operation moved by 1% of the time
where the time goes in v5:
time: 82.2 us; the launch traced here: 81.8 us
  Pallas kernels  30.1 us (37%)
  starting transfers between devices  27.5 us (33%)
  waiting for transfers between devices  17.3 us (21%)
  local copies, waits for them, and re-layouts  5.53 us (7%)
  between operations  1.08 us (1%)
    pallas_call x10, Pallas kernels, call(): pl.pallas_call(body, out_shape=outs, in_specs=[SMEM if i in smem else FAR...  28.2 us
    all_to_all x2, starting transfers between devices, exchange(): lax.all_to_all(array, 'region', split_axis=0, concat_axis=0, tiled=True)  14.5 us
    ppermute x11, starting transfers between devices, swapped(): return lax.ppermute(array, 'region', [(i, i ^ bit) for i in range(count)])  11.5 us
    ppermute x11, waiting for transfers between devices, swapped(): return lax.ppermute(array, 'region', [(i, i ^ bit) for i in range(count)])  11.3 us
    all_to_all x2, waiting for transfers between devices, exchange(): lax.all_to_all(array, 'region', split_axis=0, concat_axis=0, tiled=True)  6.01 us
    transpose x2, local copies, waits for them, and re-layouts, local(): jnp.transpose(kernel[::-1], (0, 2, 1)).reshape(KOFF * channels, channels)  2.89 us
    unnamed x22, local copies, waits for them, and re-layouts  2.64 us
    pallas_call x2, Pallas kernels, last_step(): pl.pallas_call(functools.partial(last_body, other), out_shape=jax.ShapeDt...  1.91 us
  transfers between devices with their start and end apart: 15, of which 6 were waited for; matrix products, arithmetic and copies ran while one was open for 4% of the time, Pallas kernels for 24%

profile of v5, /device:TPU:0, one launch (start us, length us, event | category | flops | bytes accessed | tf_op | source)
XLA Modules:
  0.0 81.8 jit_solution(12871653913495811319)
XLA Ops:
  0.7 3.0 %shard_map.85 = (bf16[16,176,128]{2,1,0:T(8,128)(2,1)}, f32[8,1024]{1,0:T(8,128)}) custom-call(s32[1,1024]{1,0:T(1,128)} %bitcast.20, s32[1,1024]{1,0:T(1,128)} %bitcast.21, bf16[1024,128]{1,0:T(8,128)(2,1)} %feats_far.1), custom_call_target="tpu_custom_call" | custom-call | flops 671088640 | bytes 1024000 | tf_op jit(solution)/shard_map/pallas_call | solution.py:46
  3.6 7.4 %all-to-all-start = ((bf16[16,176,128]{2,1,0:T(8,128)(2,1)}), bf16[16,176,128]{2,1,0:T(8,128)(2,1)}, u32[]{:S(2)}, u32[]{:S(2)}) async-start(bf16[16,176,128]{2,1,0:T(8,128)(2,1)} %get-tuple-element.37), calls=%async_computation | async-start | bytes 1441792 | tf_op jit(solution)/shard_map/all_to_all | solution.py:705
  11.1 0.9 %shard_map.86 = (bf16[8,256,128]{2,1,0:T(8,128)(2,1)S(1)}, bf16[256,128]{1,0:T(8,128)(2,1)S(1)}, bf16[256,128]{1,0:T(8,128)(2,1)S(1)}) custom-call(s32[16,27]{1,0:T(8,128)S(1)} %copy-done.5, bf16[16,128,128]{2,1,0:T(8,128)(2,1)S(1)} %copy-done.3), custom_call_target="tpu_custom_call" | custom-call | bytes 1181376 | tf_op jit(solution)/shard_map/pallas_call | solution.py:46
  12.4 0.7 collective-permute-start.1
  13.1 1.0 %reverse_bitcast_fusion = bf16[27,128,128]{1,2,0:T(8,128)(2,1)} fusion(bf16[27,128,128]{2,1,0:T(8,128)(2,1)S(1)} %copy-done), kind=kLoop, calls=%fused_computation | loop fusion | bytes 1769472 | tf_op jit(solution)/shard_map/transpose | solution.py:720
  14.1 1.9 %copy.10 = bf16[27,128,128]{2,1,0:T(8,128)(2,1)S(1)} copy(bf16[27,128,128]{1,2,0:T(8,128)(2,1)} %reverse_bitcast_fusion) | data formatting | bytes 1769472 | tf_op jit(solution)/shard_map/transpose | solution.py:720
  16.0 4.1 %shard_map.87.grad_far = f32[6,256,128]{2,1,0:T(8,128)S(1)} custom-call(bf16[8,256,128]{2,1,0:T(8,128)(2,1)S(1)} %get-tuple-element.38.dense_ref, bf16[3456,128]{1,0:T(8,128)(2,1)S(1)} %bitcast.13), custom_call_target="tpu_custom_call" | custom-call | flops 1358954496 | bytes 2195456 | tf_op jit(solution)/shard_map/pallas_call | solution.py:46
  20.1 0.9 %copy-done.7 = f32[6,256,128]{2,1,0:T(8,128)} copy-done((f32[6,256,128]{2,1,0:T(8,128)}, f32[6,256,128]{2,1,0:T(8,128)S(1)}, u32[]{:S(2)}) %copy-start.7) | copy-done | bytes 786456
  21.0 1.1 %shard_map.88.edge_far = f32[2,256,128]{2,1,0:T(8,128)S(1)} custom-call(bf16[8,256,128]{2,1,0:T(8,128)(2,1)S(1)} %get-tuple-element.38.dense_ref, bf16[256,128]{1,0:T(8,128)(2,1)S(1)} %collective-permute-done.near_ref, bf16[256,128]{1,0:T(8,128)(2,1)S(1)} %collective-permute-done.1.away_ref, bf16[3456,128]{1,0:T(8,128)(2,1)S(1)} %bitcast.14), custom_call_target="tpu_custom_call" | custom-call | flops 452984832 | bytes 1802240 | tf_op jit(solution)/shard_map/pallas_call | solution.py:46
  22.1 0.7 copy-done.4
  22.8 6.0 %all-to-all-done.msg_far = bf16[16,176,128]{2,1,0:T(8,128)(2,1)} async-done(((bf16[16,176,128]{2,1,0:T(8,128)(2,1)}), bf16[16,176,128]{2,1,0:T(8,128)(2,1)}, u32[]{:S(2)}, u32[]{:S(2)}) %all-to-all-start) | async-done | bytes 720928 | tf_op jit(solution)/shard_map/all_to_all | solution.py:705
  28.8 6.5 %shard_map.89 = (bf16[128,2048]{1,0:T(8,128)(2,1)}, bf16[128,256]{1,0:T(8,128)(2,1)}, bf16[128,256]{1,0:T(8,128)(2,1)}, bf16[16,160,128]{2,1,0:T(8,128)(2,1)}) custom-call(s32[16,27]{1,0:T(8,128)} %adj_ref.3, bf16[16,176,128]{2,1,0:T(8,128)(2,1)} %all-to-all-done.msg_far, f32[6,256,128]{2,1,0:T(8,128)} %copy-done.7, f32[2,256,128]{2,1,0:T(8,128)} %copy-done.4), custom_call_target="tpu_custom_call" | custom-call | flops 2684354560 | bytes 3081920 | tf_op jit(solution)/shard_map/pallas_call | solution.py:46
  35.2 7.1 %all-to-all-start.1 = ((bf16[16,160,128]{2,1,0:T(8,128)(2,1)}), bf16[16,160,128]{2,1,0:T(8,128)(2,1)S(1)}, u32[]{:S(2)}, u32[]{:S(2)}) async-start(bf16[16,160,128]{2,1,0:T(8,128)(2,1)} %get-tuple-element.53), calls=%async_computation.1 | async-start | bytes 1310720 | tf_op jit(solution)/shard_map/all_to_all | solution.py:705
  42.4 1.0 %copy-done.1 = bf16[128,2048]{1,0:T(8,128)(2,1)S(1)} copy-done((bf16[128,2048]{1,0:T(8,128)(2,1)S(1)}, bf16[128,2048]{1,0:T(8,128)(2,1)}, u32[]{:S(2)}) %copy-start.1) | copy-done | bytes 524312
  43.4 2.6 %shard_map.90 = (f32[1728,128]{1,0:T(8,128)S(1)}, f32[1728,128]{1,0:T(8,128)S(1)}) custom-call(bf16[128,2048]{1,0:T(8,128)(2,1)S(1)} %copy-done.1, bf16[256,128]{1,0:T(8,128)(2,1)S(1)} %collective-permute-done.near_ref, bf16[256,128]{1,0:T(8,128)(2,1)S(1)} %collective-permute-done.1.away_ref, bf16[8,256,128]{2,1,0:T(8,128)(2,1)S(1)} %get-tuple-element.38.dense_ref), custom_call_target="tpu_custom_call" | custom-call | flops 1811939328 | bytes 2949120 | tf_op jit(solution)/shard_map/pallas_call | solution.py:46
  46.1 0.5 collective-permute-start.2
  46.5 2.1 %collective-permute-done.2.got_ref = f32[1728,128]{1,0:T(8,128)S(1)} collective-permute-done((f32[1728,128]{1,0:T(8,128)S(1)}, f32[1728,128]{1,0:T(8,128)S(1)}, u32[]{:S(2)}, u32[]{:S(2)}) %collective-permute-start.2) | collective-permute-done | bytes 884768 | tf_op jit(solution)/shard_map/ppermute | solution.py:626
  48.7 2.0 %collective-permute-start.3 = (bf16[432,128]{1,0:T(8,128)(2,1)S(1)}, bf16[432,128]{1,0:T(8,128)(2,1)S(1)}, u32[]{:S(2)}, u32[]{:S(2)}) collective-permute-start(bf16[432,128]{1,0:T(8,128)(2,1)S(1)} %get-tuple-element.50), channel_id=1, source_target_pairs={{0,2},{1,3},{2,0},{3,1},{4,6},{5,7},{6,4},{7,5},{8,10},{9,11},{10,... | collective-permute-start | bytes 331784 | tf_op jit(solution)/shard_map/ppermute | solution.py:626
  50.6 1.5 %collective-permute-start.4 = (bf16[432,128]{1,0:T(8,128)(2,1)S(1)}, bf16[432,128]{1,0:T(8,128)(2,1)S(1)}, u32[]{:S(2)}, u32[]{:S(2)}) collective-permute-start(bf16[432,128]{1,0:T(8,128)(2,1)S(1)} %get-tuple-element.51), channel_id=1, source_target_pairs={{0,4},{1,5},{2,6},{3,7},{4,0},{5,1},{6,2},{7,3},{8,12},{9,13},{10,... | collective-permute-start | bytes 331784 | tf_op jit(solution)/shard_map/ppermute | solution.py:626
  52.3 0.8 %collective-permute-start.7 = (bf16[128,256]{1,0:T(8,128)(2,1)S(1)}, bf16[128,256]{1,0:T(8,128)(2,1)S(1)}, u32[]{:S(2)}, u32[]{:S(2)}) collective-permute-start(bf16[128,256]{1,0:T(8,128)(2,1)S(1)} %copy-done.9), channel_id=1, source_target_pairs={{1,2},{3,4},{5,6},{7,8},{9,10},{11,12},{13,14},{2,1},{4,3},{6,5},{... | collective-permute-start | bytes 196616 | tf_op jit(solution)/shard_map/ppermute | solution.py:621
  53.1 4.4 %shard_map.92.inner_far = bf16[6,256,128]{2,1,0:T(8,128)(2,1)S(1)} custom-call(bf16[128,2048]{1,0:T(8,128)(2,1)S(1)} %copy-done.2, bf16[3456,128]{1,0:T(8,128)(2,1)S(1)} %bitcast.11), custom_call_target="tpu_custom_call" | custom-call | bytes 1024 | tf_op jit(solution)/shard_map/pallas_call | solution.py:46
  57.5 4.1 %collective-permute-done.5 = bf16[432,128]{1,0:T(8,128)(2,1)S(1)} collective-permute-done((bf16[432,128]{1,0:T(8,128)(2,1)S(1)}, bf16[432,128]{1,0:T(8,128)(2,1)S(1)}, u32[]{:S(2)}, u32[]{:S(2)}) %collective-permute-start.5) | collective-permute-done | bytes 110624 | tf_op jit(solution)/shard_map/ppermute | solution.py:626
  61.8 3.4 %collective-permute-start.8 = (bf16[432,128]{1,0:T(8,128)(2,1)S(1)}, bf16[432,128]{1,0:T(8,128)(2,1)S(1)}, u32[]{:S(2)}, u32[]{:S(2)}) collective-permute-start(bf16[432,128]{1,0:T(8,128)(2,1)S(1)} %add_convert_fusion.1), channel_id=1, source_target_pairs={{0,8},{1,9},{2,10},{3,11},{4,12},{5,13},{6,14},{7,15},{8,0},{9,1},... | collective-permute-start | bytes 331784 | tf_op jit(solution)/shard_map/ppermute | solution.py:626
  65.2 2.4 %shard_map.93 = bf16[1024,128]{1,0:T(8,128)(2,1)} custom-call(f32[8,1024]{1,0:T(8,128)S(1)} %copy-done.8, bf16[16,160,128]{2,1,0:T(8,128)(2,1)S(1)} %all-to-all-done.1.rows_ref), custom_call_target="tpu_custom_call" | custom-call | flops 671088640 | bytes 950272 | tf_op jit(solution)/shard_map/pallas_call | solution.py:46
  67.6 3.3 %collective-permute-done.8 = bf16[432,128]{1,0:T(8,128)(2,1)S(1)} collective-permute-done((bf16[432,128]{1,0:T(8,128)(2,1)S(1)}, bf16[432,128]{1,0:T(8,128)(2,1)S(1)}, u32[]{:S(2)}, u32[]{:S(2)}) %collective-permute-start.8) | collective-permute-done | bytes 110624 | tf_op jit(solution)/shard_map/ppermute | solution.py:626
  71.3 1.7 %collective-permute-start.10 = (bf16[432,128]{1,0:T(8,128)(2,1)S(1)}, bf16[432,128]{1,0:T(8,128)(2,1)S(1)}, u32[]{:S(2)}, u32[]{:S(2)}) collective-permute-start(bf16[432,128]{1,0:T(8,128)(2,1)S(1)} %add_convert_fusion), channel_id=1, source_target_pairs={{0,4},{1,5},{2,6},{3,7},{4,0},{5,1},{6,2},{7,3},{8,12},{9,13},{10,... | collective-permute-start | bytes 331784 | tf_op jit(solution)/shard_map/ppermute | solution.py:626
  73.0 1.5 %collective-permute-start.9 = (bf16[432,128]{1,0:T(8,128)(2,1)S(1)}, bf16[432,128]{1,0:T(8,128)(2,1)S(1)}, u32[]{:S(2)}, u32[]{:S(2)}) collective-permute-start(bf16[432,128]{1,0:T(8,128)(2,1)S(1)} %add_convert_fusion), channel_id=1, source_target_pairs={{0,2},{1,3},{2,0},{3,1},{4,6},{5,7},{6,4},{7,5},{8,10},{9,11},{10,... | collective-permute-start | bytes 331784 | tf_op jit(solution)/shard_map/ppermute | solution.py:626
  74.4 3.2 %shard_map.94 = bf16[16,128,128]{2,1,0:T(8,128)(2,1)} custom-call(s32[16,27]{1,0:T(8,128)S(1)} %copy-done.6, bf16[128,2048]{1,0:T(8,128)(2,1)S(1)} %copy-done.2, bf16[128,256]{1,0:T(8,128)(2,1)S(1)} %collective-permute-done.6.near_ref, bf16[128,256]{1,0:T(8,128)(2,1)S(1)} %collective-permute-done.7.away_ref, bf16[3456,128]{1,0:T(8,128)(2,1)S(1)} %bitcast.12, ...), custom_call_target="tpu_custom_call" | custom-call | flops 452984832 | bytes 2459328 | tf_op jit(solution)/shard_map/pallas_call | solution.py:46
  77.7 1.0 %collective-permute-done.9 = bf16[432,128]{1,0:T(8,128)(2,1)S(1)} collective-permute-done((bf16[432,128]{1,0:T(8,128)(2,1)S(1)}, bf16[432,128]{1,0:T(8,128)(2,1)S(1)}, u32[]{:S(2)}, u32[]{:S(2)}) %collective-permute-start.9) | collective-permute-done | bytes 110624 | tf_op jit(solution)/shard_map/ppermute | solution.py:626
  78.9 1.0 %shard_map.95.refs_0_ = f32[3456,128]{1,0:T(8,128)} custom-call(bf16[4,432,128]{2,1,0:T(8,128)(2,1)S(1)} %pad_maximum_fusion.pieces_ref), custom_call_target="tpu_custom_call" | custom-call | bytes 1327104 | tf_op jit(solution)/shard_map/pallas_call | solution.py:689
  79.8 0.8 collective-permute-done.12.pieces_ref
  80.7 1.0 %shard_map.96 = f32[3456,128]{1,0:T(8,128)} custom-call(bf16[4,432,128]{2,1,0:T(8,128)(2,1)S(1)} %collective-permute-done.12.pieces_ref, f32[3456,128]{1,0:T(8,128)} %shard_map.95.refs_0_), custom_call_target="tpu_custom_call", output_to_operand_aliasing={{}: (1, {})} | custom-call | bytes 1327104 | tf_op jit(solution)/shard_map/pallas_call | solution.py:689
  (37 shorter events, 1.4 us)
Async XLA Ops:
  0.6 10.4 %copy-start.3 = (bf16[16,128,128]{2,1,0:T(8,128)(2,1)S(1)}, bf16[16,128,128]{2,1,0:T(8,128)(2,1)}, u32[]{:S(2)}) copy-start(bf16[16,128,128]{2,1,0:T(8,128)(2,1)} %bricks_ref.1) | copy-start | bytes 1572868
  0.6 10.4 %copy-start.5 = (s32[16,27]{1,0:T(8,128)S(1)}, s32[16,27]{1,0:T(8,128)}, u32[]{:S(2)}) copy-start(s32[16,27]{1,0:T(8,128)} %adj_ref.3) | copy-start | bytes 5188
  0.7 12.4 %copy-start = (bf16[27,128,128]{2,1,0:T(8,128)(2,1)S(1)}, bf16[27,128,128]{2,1,0:T(8,128)(2,1)}, u32[]{:S(2)}) copy-start(bf16[27,128,128]{2,1,0:T(8,128)(2,1)} %param.10) | copy-start | bytes 2654212
  3.6 25.1 %all-to-all-start = ((bf16[16,176,128]{2,1,0:T(8,128)(2,1)}), bf16[16,176,128]{2,1,0:T(8,128)(2,1)}, u32[]{:S(2)}, u32[]{:S(2)}) async-start(bf16[16,176,128]{2,1,0:T(8,128)(2,1)} %get-tuple-element.37), calls=%async_computation | async-start | bytes 1441792 | tf_op jit(solution)/shard_map/all_to_all | solution.py:705
  12.0 9.0 %collective-permute-start = (bf16[256,128]{1,0:T(8,128)(2,1)S(1)}, bf16[256,128]{1,0:T(8,128)(2,1)S(1)}, u32[]{:S(2)}, u32[]{:S(2)}) collective-permute-start(bf16[256,128]{1,0:T(8,128)(2,1)S(1)} %get-tuple-element.39), channel_id=1, source_target_pairs={{0,1},{1,0},{2,3},{3,2},{4,5},{5,4},{6,7},{7,6},{8,9},{9,8},{10,11... | collective-permute-start | bytes 196616 | tf_op jit(solution)/shard_map/ppermute | solution.py:626
  12.4 8.6 %collective-permute-start.1 = (bf16[256,128]{1,0:T(8,128)(2,1)S(1)}, bf16[256,128]{1,0:T(8,128)(2,1)S(1)}, u32[]{:S(2)}, u32[]{:S(2)}) collective-permute-start(bf16[256,128]{1,0:T(8,128)(2,1)S(1)} %get-tuple-element.40), channel_id=1, source_target_pairs={{1,2},{3,4},{5,6},{7,8},{9,10},{11,12},{13,14},{2,1},{4,3},{6,5},{... | collective-permute-start | bytes 196616 | tf_op jit(solution)/shard_map/ppermute | solution.py:621
  20.1 0.9 %copy-start.7 = (f32[6,256,128]{2,1,0:T(8,128)}, f32[6,256,128]{2,1,0:T(8,128)S(1)}, u32[]{:S(2)}) copy-start(f32[6,256,128]{2,1,0:T(8,128)S(1)} %shard_map.87.grad_far) | copy-start | bytes 2359300
  22.1 0.7 copy-start.4
  35.2 26.4 %all-to-all-start.1 = ((bf16[16,160,128]{2,1,0:T(8,128)(2,1)}), bf16[16,160,128]{2,1,0:T(8,128)(2,1)S(1)}, u32[]{:S(2)}, u32[]{:S(2)}) async-start(bf16[16,160,128]{2,1,0:T(8,128)(2,1)} %get-tuple-element.53), calls=%async_computation.1 | async-start | bytes 1310720 | tf_op jit(solution)/shard_map/all_to_all | solution.py:705
  42.4 1.0 %copy-start.1 = (bf16[128,2048]{1,0:T(8,128)(2,1)S(1)}, bf16[128,2048]{1,0:T(8,128)(2,1)}, u32[]{:S(2)}) copy-start(bf16[128,2048]{1,0:T(8,128)(2,1)} %get-tuple-element.54.turned_ref.turned_far) | copy-start | bytes 1572868
  46.0 6.2 %copy-start.10 = (bf16[128,256]{1,0:T(8,128)(2,1)S(1)}, bf16[128,256]{1,0:T(8,128)(2,1)}, u32[]{:S(2)}) copy-start(bf16[128,256]{1,0:T(8,128)(2,1)} %get-tuple-element.55) | copy-start | bytes 196612
  46.0 6.2 %copy-start.9 = (bf16[128,256]{1,0:T(8,128)(2,1)S(1)}, bf16[128,256]{1,0:T(8,128)(2,1)}, u32[]{:S(2)}) copy-start(bf16[128,256]{1,0:T(8,128)(2,1)} %get-tuple-element.56) | copy-start | bytes 196612
  46.1 7.1 %copy-start.2 = (bf16[128,2048]{1,0:T(8,128)(2,1)S(1)}, bf16[128,2048]{1,0:T(8,128)(2,1)}, u32[]{:S(2)}) copy-start(bf16[128,2048]{1,0:T(8,128)(2,1)} %get-tuple-element.54.turned_ref.turned_far) | copy-start | bytes 1572868
  46.1 2.5 %collective-permute-start.2 = (f32[1728,128]{1,0:T(8,128)S(1)}, f32[1728,128]{1,0:T(8,128)S(1)}, u32[]{:S(2)}, u32[]{:S(2)}) collective-permute-start(f32[1728,128]{1,0:T(8,128)S(1)} %get-tuple-element.43), channel_id=1, source_target_pairs={{0,1},{1,0},{2,3},{3,2},{4,5},{5,4},{6,7},{7,6},{8,9},{9,8},{10,11... | collective-permute-start | bytes 2654216 | tf_op jit(solution)/shard_map/ppermute | solution.py:626
  48.6 16.6 %copy-start.8 = (f32[8,1024]{1,0:T(8,128)S(1)}, f32[8,1024]{1,0:T(8,128)}, u32[]{:S(2)}) copy-start(f32[8,1024]{1,0:T(8,128)} %get-tuple-element.62.place_ref) | copy-start | bytes 98308
  48.7 8.8 %collective-permute-start.3 = (bf16[432,128]{1,0:T(8,128)(2,1)S(1)}, bf16[432,128]{1,0:T(8,128)(2,1)S(1)}, u32[]{:S(2)}, u32[]{:S(2)}) collective-permute-start(bf16[432,128]{1,0:T(8,128)(2,1)S(1)} %get-tuple-element.50), channel_id=1, source_target_pairs={{0,2},{1,3},{2,0},{3,1},{4,6},{5,7},{6,4},{7,5},{8,10},{9,11},{10,... | collective-permute-start | bytes 331784 | tf_op jit(solution)/shard_map/ppermute | solution.py:626
  50.6 6.9 %collective-permute-start.4 = (bf16[432,128]{1,0:T(8,128)(2,1)S(1)}, bf16[432,128]{1,0:T(8,128)(2,1)S(1)}, u32[]{:S(2)}, u32[]{:S(2)}) collective-permute-start(bf16[432,128]{1,0:T(8,128)(2,1)S(1)} %get-tuple-element.51), channel_id=1, source_target_pairs={{0,4},{1,5},{2,6},{3,7},{4,0},{5,1},{6,2},{7,3},{8,12},{9,13},{10,... | collective-permute-start | bytes 331784 | tf_op jit(solution)/shard_map/ppermute | solution.py:626
  52.1 9.6 %collective-permute-start.5 = (bf16[432,128]{1,0:T(8,128)(2,1)S(1)}, bf16[432,128]{1,0:T(8,128)(2,1)S(1)}, u32[]{:S(2)}, u32[]{:S(2)}) collective-permute-start(bf16[432,128]{1,0:T(8,128)(2,1)S(1)} %get-tuple-element.52), channel_id=1, source_target_pairs={{0,6},{1,7},{2,4},{3,5},{4,2},{5,3},{6,0},{7,1},{8,14},{9,15},{10,... | collective-permute-start | bytes 331784 | tf_op jit(solution)/shard_map/ppermute | solution.py:626
  52.3 5.2 %collective-permute-start.6 = (bf16[128,256]{1,0:T(8,128)(2,1)S(1)}, bf16[128,256]{1,0:T(8,128)(2,1)S(1)}, u32[]{:S(2)}, u32[]{:S(2)}) collective-permute-start(bf16[128,256]{1,0:T(8,128)(2,1)S(1)} %copy-done.10), channel_id=1, source_target_pairs={{0,1},{1,0},{2,3},{3,2},{4,5},{5,4},{6,7},{7,6},{8,9},{9,8},{10,11... | collective-permute-start | bytes 196616 | tf_op jit(solution)/shard_map/ppermute | solution.py:626
  52.3 5.3 %collective-permute-start.7 = (bf16[128,256]{1,0:T(8,128)(2,1)S(1)}, bf16[128,256]{1,0:T(8,128)(2,1)S(1)}, u32[]{:S(2)}, u32[]{:S(2)}) collective-permute-start(bf16[128,256]{1,0:T(8,128)(2,1)S(1)} %copy-done.9), channel_id=1, source_target_pairs={{1,2},{3,4},{5,6},{7,8},{9,10},{11,12},{13,14},{2,1},{4,3},{6,5},{... | collective-permute-start | bytes 196616 | tf_op jit(solution)/shard_map/ppermute | solution.py:621
  61.7 12.7 %copy-start.6 = (s32[16,27]{1,0:T(8,128)S(1)}, s32[16,27]{1,0:T(8,128)}, u32[]{:S(2)}) copy-start(s32[16,27]{1,0:T(8,128)} %adj_ref.3) | copy-start | bytes 5188
  61.8 9.1 %collective-permute-start.8 = (bf16[432,128]{1,0:T(8,128)(2,1)S(1)}, bf16[432,128]{1,0:T(8,128)(2,1)S(1)}, u32[]{:S(2)}, u32[]{:S(2)}) collective-permute-start(bf16[432,128]{1,0:T(8,128)(2,1)S(1)} %add_convert_fusion.1), channel_id=1, source_target_pairs={{0,8},{1,9},{2,10},{3,11},{4,12},{5,13},{6,14},{7,15},{8,0},{9,1},... | collective-permute-start | bytes 331784 | tf_op jit(solution)/shard_map/ppermute | solution.py:626
  70.9 6.8 %collective-permute-start.11 = (bf16[432,128]{1,0:T(8,128)(2,1)S(1)}, bf16[432,128]{1,0:T(8,128)(2,1)S(1)}, u32[]{:S(2)}, u32[]{:S(2)}) collective-permute-start(bf16[432,128]{1,0:T(8,128)(2,1)S(1)} %add_convert_fusion), channel_id=1, source_target_pairs={{0,6},{1,7},{2,4},{3,5},{4,2},{5,3},{6,0},{7,1},{8,14},{9,15},{10,... | collective-permute-start | bytes 331784 | tf_op jit(solution)/shard_map/ppermute | solution.py:626
  71.3 6.4 %collective-permute-start.10 = (bf16[432,128]{1,0:T(8,128)(2,1)S(1)}, bf16[432,128]{1,0:T(8,128)(2,1)S(1)}, u32[]{:S(2)}, u32[]{:S(2)}) collective-permute-start(bf16[432,128]{1,0:T(8,128)(2,1)S(1)} %add_convert_fusion), channel_id=1, source_target_pairs={{0,4},{1,5},{2,6},{3,7},{4,0},{5,1},{6,2},{7,3},{8,12},{9,13},{10,... | collective-permute-start | bytes 331784 | tf_op jit(solution)/shard_map/ppermute | solution.py:626
  73.0 5.8 %collective-permute-start.9 = (bf16[432,128]{1,0:T(8,128)(2,1)S(1)}, bf16[432,128]{1,0:T(8,128)(2,1)S(1)}, u32[]{:S(2)}, u32[]{:S(2)}) collective-permute-start(bf16[432,128]{1,0:T(8,128)(2,1)S(1)} %add_convert_fusion), channel_id=1, source_target_pairs={{0,2},{1,3},{2,0},{3,1},{4,6},{5,7},{6,4},{7,5},{8,10},{9,11},{10,... | collective-permute-start | bytes 331784 | tf_op jit(solution)/shard_map/ppermute | solution.py:626
  78.8 1.9 %collective-permute-start.12 = (bf16[4,432,128]{2,1,0:T(8,128)(2,1)S(1)}, bf16[4,432,128]{2,1,0:T(8,128)(2,1)S(1)}, u32[]{:S(2)}, u32[]{:S(2)}) collective-permute-start(bf16[4,432,128]{2,1,0:T(8,128)(2,1)S(1)} %pad_maximum_fusion.pieces_ref), channel_id=1, source_target_pairs={{0,1},{1,0},{2,3},{3,2},{4,5},{5,4},{6,7},{7,6},{8,9},{9,8},{10,11... | collective-permute-start | bytes 1327112 | tf_op jit(solution)/shard_map/ppermute | solution.py:626

commit v6 on v5

--- a/solution.py
+++ b/solution.py
@@ -668,37 +668,39 @@
     return found
 
 
-def last_body(other, pieces_ref, *refs):
+def last_body(size, places, *refs):
     out_far, wide_ref, sems = refs[-3:]
-    size, rows, channels = pieces_ref.shape
+    rows = refs[0].shape[0]
     core = this_core()
-    half = 1 - core if other else core
     side = lax.rem(lax.axis_index("region") // 2, size)
     copies = []
-    for i in range(size):
-        wide_ref[i] = pieces_ref[i].astype(F32)
+    for n, (other, i) in enumerate(places):
+        wide_ref[n] = refs[n][...].astype(F32)
+        half = 1 - core if other else core
         at = pl.multiple_of((half * size + (side ^ i)) * rows, 16)
-        copies += start_all([(wide_ref.at[i], out_far.at[pl.ds(at, rows)])], sems.at[i : i + 1])
+        copies += start_all([(wide_ref.at[n], out_far.at[pl.ds(at, rows)])], sems.at[n : n + 1])
     for copy in copies:
         copy.wait()
 
 
-def last_step(pieces, out=None):
-    size, rows, channels = pieces.shape
-    other = out is not None
+def last_step(size, places, pieces, out=None):
+    count, (rows, channels) = len(pieces), pieces[0].shape
+    again = out is not None
     return pl.pallas_call(
-        functools.partial(last_body, other),
+        functools.partial(last_body, size, places),
         out_shape=jax.ShapeDtypeStruct((2 * size * rows, channels), F32),
-        in_specs=[VMEM] + [FAR] * other,
+        in_specs=[VMEM] * count + [FAR] * again,
         out_specs=FAR,
         scratch_shapes=[
-            pltpu.VMEM((size, rows, channels), F32),
-            pltpu.SemaphoreType.DMA((size,)),
+            pltpu.VMEM((count, rows, channels), F32),
+            pltpu.SemaphoreType.DMA((count,)),
         ],
-        input_output_aliases={1: 0} if other else {},
+        input_output_aliases={count: 0} if again else {},
         compiler_params=pltpu.CompilerParams(vmem_limit_bytes=16 * MIB),
-        cost_estimate=pl.CostEstimate(flops=0, bytes_accessed=6 * size * rows * channels, transcendentals=0),
-    )(pieces, *([out] if other else []))
+        cost_estimate=pl.CostEstimate(
+            flops=0, bytes_accessed=6 * count * rows * channels, transcendentals=0
+        ),
+    )(*pieces, *([out] if again else []))
 
 
 def exchange(array):
@@ -742,16 +744,22 @@
     for bit, size in groups[1:-1]:
         term = reduce_group(term, bit, size)
     bit, size = groups[-1]
-    term, returned = exchange_group(term, bit, size, returned)
+    term, (returned, feats_near, feats_away) = exchange_group(
+        term, bit, size, (returned, feats_near, feats_away)
+    )
     grad_points = unpack(place, returned, points)
+    out_tiles = edge_forward(adjacency, turned, feats_near, feats_away, weights, inner, tiles)
     for bit, size in groups[-2:0:-1]:
         side = (lax.axis_index("region") // bit) % size
         term = in_order(gather_group(term, bit, size), side)
-    term, grad_points = lax.optimization_barrier((term, grad_points))
-    out_tiles = edge_forward(adjacency, turned, feats_near, feats_away, weights, inner, tiles)
-    own = jnp.stack(gather_group(term, *groups[0]))
-    own, out_tiles = lax.optimization_barrier((own, out_tiles))
-    grad_weight = last_step(swapped(own, 1), last_step(own)).reshape(KOFF, channels, channels)
+    term, grad_points, out_tiles = lax.optimization_barrier((term, grad_points, out_tiles))
+    bit, size = groups[0]
+    own = gather_group(term, bit, size)
+    others = [swapped(piece, 1) for piece in own]
+    first = [(False, i) for i in range(size)] + [(True, 0)]
+    summed = last_step(size, first, own + others[:1])
+    summed = last_step(size, [(True, i) for i in range(1, size)], others[1:], summed)
+    grad_weight = summed.reshape(KOFF, channels, channels)
     return out_tiles, grad_points, grad_weight
 
 

time: 82.2 us -> 81.8 us (level)
    ppermute x11 -> x14, waiting for transfers between devices: 11.3 us -> 10.5 us  [swapped(): return lax.ppermute(array, 'region', [(i, i ^ bit) for i in range(count)])]
    ppermute x11 -> x14, starting transfers between devices: 11.5 us -> 11.9 us  [swapped(): return lax.ppermute(array, 'region', [(i, i ^ bit) for i in range(count)])]
  transfers between devices with their start and end apart: 15 -> 18, of which waited for: 6 -> 6; matrix products, arithmetic and copies ran while one was open for 4% -> 4% of each run, Pallas kernels for 24% -> 24%
where the time goes in v6:
time: 81.8 us; the launch traced here: 81.3 us
  Pallas kernels  30.1 us (37%)
  starting transfers between devices  28 us (34%)
  waiting for transfers between devices  16.5 us (20%)
  local copies, waits for them, and re-layouts  5.53 us (7%)
  between operations  1.09 us (1%)
    pallas_call x10, Pallas kernels, call(): pl.pallas_call(body, out_shape=outs, in_specs=[SMEM if i in smem else FAR...  28.2 us
    all_to_all x2, starting transfers between devices, exchange(): lax.all_to_all(array, 'region', split_axis=0, concat_axis=0, tiled=True)  14.5 us
    ppermute x14, starting transfers between devices, swapped(): return lax.ppermute(array, 'region', [(i, i ^ bit) for i in range(count)])  11.9 us
    ppermute x14, waiting for transfers between devices, swapped(): return lax.ppermute(array, 'region', [(i, i ^ bit) for i in range(count)])  10.5 us
    all_to_all x2, waiting for transfers between devices, exchange(): lax.all_to_all(array, 'region', split_axis=0, concat_axis=0, tiled=True)  6.02 us
    transpose x2, local copies, waits for them, and re-layouts, local(): jnp.transpose(kernel[::-1], (0, 2, 1)).reshape(KOFF * channels, channels)  2.89 us
    unnamed x22, local copies, waits for them, and re-layouts  2.65 us
    pallas_call x2, Pallas kernels, last_step(): pl.pallas_call(functools.partial(last_body, size, places), out_shape=jax....  1.91 us
  transfers between devices with their start and end apart: 18, of which 6 were waited for; matrix products, arithmetic and copies ran while one was open for 4% of the time, Pallas kernels for 24%

profile of v6, /device:TPU:0, one launch (start us, length us, event | category | flops | bytes accessed | tf_op | source)
XLA Modules:
  0.0 81.3 jit_solution(2674256808390791982)
XLA Ops:
  0.7 3.0 %shard_map.85 = (bf16[16,176,128]{2,1,0:T(8,128)(2,1)}, f32[8,1024]{1,0:T(8,128)}) custom-call(s32[1,1024]{1,0:T(1,128)} %bitcast.12, s32[1,1024]{1,0:T(1,128)} %bitcast.13, bf16[1024,128]{1,0:T(8,128)(2,1)} %feats_far.1), custom_call_target="tpu_custom_call" | custom-call | flops 671088640 | bytes 1024000 | tf_op jit(solution)/shard_map/pallas_call | solution.py:46
  3.7 7.4 %all-to-all-start = ((bf16[16,176,128]{2,1,0:T(8,128)(2,1)}), bf16[16,176,128]{2,1,0:T(8,128)(2,1)}, u32[]{:S(2)}, u32[]{:S(2)}) async-start(bf16[16,176,128]{2,1,0:T(8,128)(2,1)} %get-tuple-element.38), calls=%async_computation | async-start | bytes 1441792 | tf_op jit(solution)/shard_map/all_to_all | solution.py:707
  11.1 0.9 %shard_map.86 = (bf16[8,256,128]{2,1,0:T(8,128)(2,1)S(1)}, bf16[256,128]{1,0:T(8,128)(2,1)S(1)}, bf16[256,128]{1,0:T(8,128)(2,1)S(1)}) custom-call(s32[16,27]{1,0:T(8,128)S(1)} %copy-done.5, bf16[16,128,128]{2,1,0:T(8,128)(2,1)S(1)} %copy-done.3), custom_call_target="tpu_custom_call" | custom-call | bytes 1181376 | tf_op jit(solution)/shard_map/pallas_call | solution.py:46
  12.4 0.7 collective-permute-start.1
  13.1 1.0 %reverse_bitcast_fusion = bf16[27,128,128]{1,2,0:T(8,128)(2,1)} fusion(bf16[27,128,128]{2,1,0:T(8,128)(2,1)S(1)} %copy-done), kind=kLoop, calls=%fused_computation | loop fusion | bytes 1769472 | tf_op jit(solution)/shard_map/transpose | solution.py:722
  14.1 1.9 %copy.10 = bf16[27,128,128]{2,1,0:T(8,128)(2,1)S(1)} copy(bf16[27,128,128]{1,2,0:T(8,128)(2,1)} %reverse_bitcast_fusion) | data formatting | bytes 1769472 | tf_op jit(solution)/shard_map/transpose | solution.py:722
  16.0 4.1 %shard_map.87.grad_far = f32[6,256,128]{2,1,0:T(8,128)S(1)} custom-call(bf16[8,256,128]{2,1,0:T(8,128)(2,1)S(1)} %get-tuple-element.39.dense_ref, bf16[3456,128]{1,0:T(8,128)(2,1)S(1)} %bitcast.9), custom_call_target="tpu_custom_call" | custom-call | flops 1358954496 | bytes 2195456 | tf_op jit(solution)/shard_map/pallas_call | solution.py:46
  20.1 0.9 %copy-done.7 = f32[6,256,128]{2,1,0:T(8,128)} copy-done((f32[6,256,128]{2,1,0:T(8,128)}, f32[6,256,128]{2,1,0:T(8,128)S(1)}, u32[]{:S(2)}) %copy-start.7) | copy-done | bytes 786456
  21.0 1.1 %shard_map.88.edge_far = f32[2,256,128]{2,1,0:T(8,128)S(1)} custom-call(bf16[8,256,128]{2,1,0:T(8,128)(2,1)S(1)} %get-tuple-element.39.dense_ref, bf16[256,128]{1,0:T(8,128)(2,1)S(1)} %collective-permute-done.near_ref, bf16[256,128]{1,0:T(8,128)(2,1)S(1)} %collective-permute-done.1.away_ref, bf16[3456,128]{1,0:T(8,128)(2,1)S(1)} %bitcast.10), custom_call_target="tpu_custom_call" | custom-call | flops 452984832 | bytes 1802240 | tf_op jit(solution)/shard_map/pallas_call | solution.py:46
  22.1 0.7 copy-done.4
  22.8 6.0 %all-to-all-done.msg_far = bf16[16,176,128]{2,1,0:T(8,128)(2,1)} async-done(((bf16[16,176,128]{2,1,0:T(8,128)(2,1)}), bf16[16,176,128]{2,1,0:T(8,128)(2,1)}, u32[]{:S(2)}, u32[]{:S(2)}) %all-to-all-start) | async-done | bytes 720928 | tf_op jit(solution)/shard_map/all_to_all | solution.py:707
  28.8 6.4 %shard_map.89 = (bf16[128,2048]{1,0:T(8,128)(2,1)}, bf16[128,256]{1,0:T(8,128)(2,1)}, bf16[128,256]{1,0:T(8,128)(2,1)}, bf16[16,160,128]{2,1,0:T(8,128)(2,1)}) custom-call(s32[16,27]{1,0:T(8,128)} %adj_ref.3, bf16[16,176,128]{2,1,0:T(8,128)(2,1)} %all-to-all-done.msg_far, f32[6,256,128]{2,1,0:T(8,128)} %copy-done.7, f32[2,256,128]{2,1,0:T(8,128)} %copy-done.4), custom_call_target="tpu_custom_call" | custom-call | flops 2684354560 | bytes 3081920 | tf_op jit(solution)/shard_map/pallas_call | solution.py:46
  35.2 7.1 %all-to-all-start.1 = ((bf16[16,160,128]{2,1,0:T(8,128)(2,1)}), bf16[16,160,128]{2,1,0:T(8,128)(2,1)S(1)}, u32[]{:S(2)}, u32[]{:S(2)}) async-start(bf16[16,160,128]{2,1,0:T(8,128)(2,1)} %get-tuple-element.54), calls=%async_computation.1 | async-start | bytes 1310720 | tf_op jit(solution)/shard_map/all_to_all | solution.py:707
  42.4 1.0 %copy-done.1 = bf16[128,2048]{1,0:T(8,128)(2,1)S(1)} copy-done((bf16[128,2048]{1,0:T(8,128)(2,1)S(1)}, bf16[128,2048]{1,0:T(8,128)(2,1)}, u32[]{:S(2)}) %copy-start.1) | copy-done | bytes 524312
  43.4 2.6 %shard_map.90 = (f32[1728,128]{1,0:T(8,128)S(1)}, f32[1728,128]{1,0:T(8,128)S(1)}) custom-call(bf16[128,2048]{1,0:T(8,128)(2,1)S(1)} %copy-done.1, bf16[256,128]{1,0:T(8,128)(2,1)S(1)} %collective-permute-done.near_ref, bf16[256,128]{1,0:T(8,128)(2,1)S(1)} %collective-permute-done.1.away_ref, bf16[8,256,128]{2,1,0:T(8,128)(2,1)S(1)} %get-tuple-element.39.dense_ref), custom_call_target="tpu_custom_call" | custom-call | flops 1811939328 | bytes 2949120 | tf_op jit(solution)/shard_map/pallas_call | solution.py:46
  46.5 2.1 %collective-permute-done.2.got_ref = f32[1728,128]{1,0:T(8,128)S(1)} collective-permute-done((f32[1728,128]{1,0:T(8,128)S(1)}, f32[1728,128]{1,0:T(8,128)S(1)}, u32[]{:S(2)}, u32[]{:S(2)}) %collective-permute-start.2) | collective-permute-done | bytes 884768 | tf_op jit(solution)/shard_map/ppermute | solution.py:626
  48.7 2.0 %collective-permute-start.3 = (bf16[432,128]{1,0:T(8,128)(2,1)S(1)}, bf16[432,128]{1,0:T(8,128)(2,1)S(1)}, u32[]{:S(2)}, u32[]{:S(2)}) collective-permute-start(bf16[432,128]{1,0:T(8,128)(2,1)S(1)} %get-tuple-element.51), channel_id=1, source_target_pairs={{0,2},{1,3},{2,0},{3,1},{4,6},{5,7},{6,4},{7,5},{8,10},{9,11},{10,... | collective-permute-start | bytes 331784 | tf_op jit(solution)/shard_map/ppermute | solution.py:626
  50.6 1.5 %collective-permute-start.4 = (bf16[432,128]{1,0:T(8,128)(2,1)S(1)}, bf16[432,128]{1,0:T(8,128)(2,1)S(1)}, u32[]{:S(2)}, u32[]{:S(2)}) collective-permute-start(bf16[432,128]{1,0:T(8,128)(2,1)S(1)} %get-tuple-element.52), channel_id=1, source_target_pairs={{0,4},{1,5},{2,6},{3,7},{4,0},{5,1},{6,2},{7,3},{8,12},{9,13},{10,... | collective-permute-start | bytes 331784 | tf_op jit(solution)/shard_map/ppermute | solution.py:626
  52.3 0.8 %collective-permute-start.7 = (bf16[128,256]{1,0:T(8,128)(2,1)S(1)}, bf16[128,256]{1,0:T(8,128)(2,1)S(1)}, u32[]{:S(2)}, u32[]{:S(2)}) collective-permute-start(bf16[128,256]{1,0:T(8,128)(2,1)S(1)} %copy-done.9), channel_id=1, source_target_pairs={{1,2},{3,4},{5,6},{7,8},{9,10},{11,12},{13,14},{2,1},{4,3},{6,5},{... | collective-permute-start | bytes 196616 | tf_op jit(solution)/shard_map/ppermute | solution.py:621
  53.1 4.4 %shard_map.92.inner_far = bf16[6,256,128]{2,1,0:T(8,128)(2,1)S(1)} custom-call(bf16[128,2048]{1,0:T(8,128)(2,1)S(1)} %copy-done.2, bf16[3456,128]{1,0:T(8,128)(2,1)S(1)} %bitcast.7), custom_call_target="tpu_custom_call" | custom-call | bytes 1024 | tf_op jit(solution)/shard_map/pallas_call | solution.py:46
  57.6 4.1 %collective-permute-done.5 = bf16[432,128]{1,0:T(8,128)(2,1)S(1)} collective-permute-done((bf16[432,128]{1,0:T(8,128)(2,1)S(1)}, bf16[432,128]{1,0:T(8,128)(2,1)S(1)}, u32[]{:S(2)}, u32[]{:S(2)}) %collective-permute-start.5) | collective-permute-done | bytes 110624 | tf_op jit(solution)/shard_map/ppermute | solution.py:626
  61.8 3.4 %collective-permute-start.8 = (bf16[432,128]{1,0:T(8,128)(2,1)S(1)}, bf16[432,128]{1,0:T(8,128)(2,1)S(1)}, u32[]{:S(2)}, u32[]{:S(2)}) collective-permute-start(bf16[432,128]{1,0:T(8,128)(2,1)S(1)} %add_convert_fusion.1), channel_id=1, source_target_pairs={{0,8},{1,9},{2,10},{3,11},{4,12},{5,13},{6,14},{7,15},{8,0},{9,1},... | collective-permute-start | bytes 331784 | tf_op jit(solution)/shard_map/ppermute | solution.py:626
  65.2 3.2 %shard_map.94 = bf16[16,128,128]{2,1,0:T(8,128)(2,1)} custom-call(s32[16,27]{1,0:T(8,128)S(1)} %copy-done.6, bf16[128,2048]{1,0:T(8,128)(2,1)S(1)} %copy-done.2, bf16[128,256]{1,0:T(8,128)(2,1)S(1)} %collective-permute-done.6.near_ref, bf16[128,256]{1,0:T(8,128)(2,1)S(1)} %collective-permute-done.7.away_ref, bf16[3456,128]{1,0:T(8,128)(2,1)S(1)} %bitcast.8, ...), custom_call_target="tpu_custom_call" | custom-call | flops 452984832 | bytes 2459328 | tf_op jit(solution)/shard_map/pallas_call | solution.py:46
  68.4 2.4 %shard_map.93 = bf16[1024,128]{1,0:T(8,128)(2,1)} custom-call(f32[8,1024]{1,0:T(8,128)S(1)} %copy-done.8, bf16[16,160,128]{2,1,0:T(8,128)(2,1)S(1)} %all-to-all-done.1.rows_ref), custom_call_target="tpu_custom_call" | custom-call | flops 671088640 | bytes 950272 | tf_op jit(solution)/shard_map/pallas_call | solution.py:46
  70.9 1.4 %collective-permute-start.13 = (bf16[432,128]{1,0:T(8,128)(2,1)S(1)}, bf16[432,128]{1,0:T(8,128)(2,1)S(1)}, u32[]{:S(2)}, u32[]{:S(2)}) collective-permute-start(bf16[432,128]{1,0:T(8,128)(2,1)S(1)} %add_convert_fusion.refs_0_), channel_id=1, source_target_pairs={{0,6},{1,7},{2,4},{3,5},{4,2},{5,3},{6,0},{7,1},{8,14},{9,15},{10,... | collective-permute-start | bytes 331784 | tf_op jit(solution)/shard_map/ppermute | solution.py:626
  72.3 0.7 collective-permute-start.11
  73.0 1.5 %collective-permute-start.9 = (bf16[432,128]{1,0:T(8,128)(2,1)S(1)}, bf16[432,128]{1,0:T(8,128)(2,1)S(1)}, u32[]{:S(2)}, u32[]{:S(2)}) collective-permute-start(bf16[432,128]{1,0:T(8,128)(2,1)S(1)} %add_convert_fusion.refs_0_), channel_id=1, source_target_pairs={{0,2},{1,3},{2,0},{3,1},{4,6},{5,7},{6,4},{7,5},{8,10},{9,11},{10,... | collective-permute-start | bytes 331784 | tf_op jit(solution)/shard_map/ppermute | solution.py:626
  74.4 3.4 %collective-permute-done.13.refs_3_ = bf16[432,128]{1,0:T(8,128)(2,1)S(1)} collective-permute-done((bf16[432,128]{1,0:T(8,128)(2,1)S(1)}, bf16[432,128]{1,0:T(8,128)(2,1)S(1)}, u32[]{:S(2)}, u32[]{:S(2)}) %collective-permute-start.13) | collective-permute-done | bytes 110624 | tf_op jit(solution)/shard_map/ppermute | solution.py:626
  77.8 0.5 collective-permute-start.12
  78.3 0.7 collective-permute-done.9.refs_1_
  79.0 1.0 %shard_map.95.refs_3_ = f32[3456,128]{1,0:T(8,128)} custom-call(bf16[432,128]{1,0:T(8,128)(2,1)S(1)} %add_convert_fusion.refs_0_, bf16[432,128]{1,0:T(8,128)(2,1)S(1)} %collective-permute-done.9.refs_1_, bf16[432,128]{1,0:T(8,128)(2,1)S(1)} %collective-permute-done.11.refs_2_, bf16[432,128]{1,0:T(8,128)(2,1)S(1)} %collective-permute-done.13.refs_3_, ...), custom_call_target="tpu_custom_call" | custom-call | bytes 1658880 | tf_op jit(solution)/shard_map/pallas_call | solution.py:689
  80.3 0.9 %shard_map.96 = f32[3456,128]{1,0:T(8,128)} custom-call(bf16[432,128]{1,0:T(8,128)(2,1)S(1)} %collective-permute-done.10.refs_0_, bf16[432,128]{1,0:T(8,128)(2,1)S(1)} %collective-permute-done.12.refs_1_, bf16[432,128]{1,0:T(8,128)(2,1)S(1)} %collective-permute-done.14.refs_2_, f32[3456,128]{1,0:T(8,128)} %shard_map.95.refs_3_), custom_call_target="tpu_custom_call", output_to_operand_aliasing={{}: (3, {})} | custom-call | bytes 995328 | tf_op jit(solution)/shard_map/pallas_call | solution.py:689
  (42 shorter events, 1.6 us)
Async XLA Ops:
  0.6 10.5 %copy-start.3 = (bf16[16,128,128]{2,1,0:T(8,128)(2,1)S(1)}, bf16[16,128,128]{2,1,0:T(8,128)(2,1)}, u32[]{:S(2)}) copy-start(bf16[16,128,128]{2,1,0:T(8,128)(2,1)} %bricks_ref.1) | copy-start | bytes 1572868
  0.6 10.5 %copy-start.5 = (s32[16,27]{1,0:T(8,128)S(1)}, s32[16,27]{1,0:T(8,128)}, u32[]{:S(2)}) copy-start(s32[16,27]{1,0:T(8,128)} %adj_ref.3) | copy-start | bytes 5188
  0.7 12.4 %copy-start = (bf16[27,128,128]{2,1,0:T(8,128)(2,1)S(1)}, bf16[27,128,128]{2,1,0:T(8,128)(2,1)}, u32[]{:S(2)}) copy-start(bf16[27,128,128]{2,1,0:T(8,128)(2,1)} %param.10) | copy-start | bytes 2654212
  3.7 25.1 %all-to-all-start = ((bf16[16,176,128]{2,1,0:T(8,128)(2,1)}), bf16[16,176,128]{2,1,0:T(8,128)(2,1)}, u32[]{:S(2)}, u32[]{:S(2)}) async-start(bf16[16,176,128]{2,1,0:T(8,128)(2,1)} %get-tuple-element.38), calls=%async_computation | async-start | bytes 1441792 | tf_op jit(solution)/shard_map/all_to_all | solution.py:707
  12.0 9.0 %collective-permute-start = (bf16[256,128]{1,0:T(8,128)(2,1)S(1)}, bf16[256,128]{1,0:T(8,128)(2,1)S(1)}, u32[]{:S(2)}, u32[]{:S(2)}) collective-permute-start(bf16[256,128]{1,0:T(8,128)(2,1)S(1)} %get-tuple-element.40), channel_id=1, source_target_pairs={{0,1},{1,0},{2,3},{3,2},{4,5},{5,4},{6,7},{7,6},{8,9},{9,8},{10,11... | collective-permute-start | bytes 196616 | tf_op jit(solution)/shard_map/ppermute | solution.py:626
  12.4 8.6 %collective-permute-start.1 = (bf16[256,128]{1,0:T(8,128)(2,1)S(1)}, bf16[256,128]{1,0:T(8,128)(2,1)S(1)}, u32[]{:S(2)}, u32[]{:S(2)}) collective-permute-start(bf16[256,128]{1,0:T(8,128)(2,1)S(1)} %get-tuple-element.41), channel_id=1, source_target_pairs={{1,2},{3,4},{5,6},{7,8},{9,10},{11,12},{13,14},{2,1},{4,3},{6,5},{... | collective-permute-start | bytes 196616 | tf_op jit(solution)/shard_map/ppermute | solution.py:621
  20.1 0.9 %copy-start.7 = (f32[6,256,128]{2,1,0:T(8,128)}, f32[6,256,128]{2,1,0:T(8,128)S(1)}, u32[]{:S(2)}) copy-start(f32[6,256,128]{2,1,0:T(8,128)S(1)} %shard_map.87.grad_far) | copy-start | bytes 2359300
  22.1 0.7 copy-start.4
  35.2 26.4 %all-to-all-start.1 = ((bf16[16,160,128]{2,1,0:T(8,128)(2,1)}), bf16[16,160,128]{2,1,0:T(8,128)(2,1)S(1)}, u32[]{:S(2)}, u32[]{:S(2)}) async-start(bf16[16,160,128]{2,1,0:T(8,128)(2,1)} %get-tuple-element.54), calls=%async_computation.1 | async-start | bytes 1310720 | tf_op jit(solution)/shard_map/all_to_all | solution.py:707
  42.4 1.0 %copy-start.1 = (bf16[128,2048]{1,0:T(8,128)(2,1)S(1)}, bf16[128,2048]{1,0:T(8,128)(2,1)}, u32[]{:S(2)}) copy-start(bf16[128,2048]{1,0:T(8,128)(2,1)} %get-tuple-element.55.turned_ref.turned_far) | copy-start | bytes 1572868
  46.0 6.2 %copy-start.10 = (bf16[128,256]{1,0:T(8,128)(2,1)S(1)}, bf16[128,256]{1,0:T(8,128)(2,1)}, u32[]{:S(2)}) copy-start(bf16[128,256]{1,0:T(8,128)(2,1)} %get-tuple-element.56) | copy-start | bytes 196612
  46.0 6.2 %copy-start.9 = (bf16[128,256]{1,0:T(8,128)(2,1)S(1)}, bf16[128,256]{1,0:T(8,128)(2,1)}, u32[]{:S(2)}) copy-start(bf16[128,256]{1,0:T(8,128)(2,1)} %get-tuple-element.57) | copy-start | bytes 196612
  46.1 7.1 %copy-start.2 = (bf16[128,2048]{1,0:T(8,128)(2,1)S(1)}, bf16[128,2048]{1,0:T(8,128)(2,1)}, u32[]{:S(2)}) copy-start(bf16[128,2048]{1,0:T(8,128)(2,1)} %get-tuple-element.55.turned_ref.turned_far) | copy-start | bytes 1572868
  46.1 2.5 %collective-permute-start.2 = (f32[1728,128]{1,0:T(8,128)S(1)}, f32[1728,128]{1,0:T(8,128)S(1)}, u32[]{:S(2)}, u32[]{:S(2)}) collective-permute-start(f32[1728,128]{1,0:T(8,128)S(1)} %get-tuple-element.44), channel_id=1, source_target_pairs={{0,1},{1,0},{2,3},{3,2},{4,5},{5,4},{6,7},{7,6},{8,9},{9,8},{10,11... | collective-permute-start | bytes 2654216 | tf_op jit(solution)/shard_map/ppermute | solution.py:626
  48.6 16.6 %copy-start.6 = (s32[16,27]{1,0:T(8,128)S(1)}, s32[16,27]{1,0:T(8,128)}, u32[]{:S(2)}) copy-start(s32[16,27]{1,0:T(8,128)} %adj_ref.3) | copy-start | bytes 5188
  48.7 8.9 %collective-permute-start.3 = (bf16[432,128]{1,0:T(8,128)(2,1)S(1)}, bf16[432,128]{1,0:T(8,128)(2,1)S(1)}, u32[]{:S(2)}, u32[]{:S(2)}) collective-permute-start(bf16[432,128]{1,0:T(8,128)(2,1)S(1)} %get-tuple-element.51), channel_id=1, source_target_pairs={{0,2},{1,3},{2,0},{3,1},{4,6},{5,7},{6,4},{7,5},{8,10},{9,11},{10,... | collective-permute-start | bytes 331784 | tf_op jit(solution)/shard_map/ppermute | solution.py:626
  50.6 6.9 %collective-permute-start.4 = (bf16[432,128]{1,0:T(8,128)(2,1)S(1)}, bf16[432,128]{1,0:T(8,128)(2,1)S(1)}, u32[]{:S(2)}, u32[]{:S(2)}) collective-permute-start(bf16[432,128]{1,0:T(8,128)(2,1)S(1)} %get-tuple-element.52), channel_id=1, source_target_pairs={{0,4},{1,5},{2,6},{3,7},{4,0},{5,1},{6,2},{7,3},{8,12},{9,13},{10,... | collective-permute-start | bytes 331784 | tf_op jit(solution)/shard_map/ppermute | solution.py:626
  52.1 9.6 %collective-permute-start.5 = (bf16[432,128]{1,0:T(8,128)(2,1)S(1)}, bf16[432,128]{1,0:T(8,128)(2,1)S(1)}, u32[]{:S(2)}, u32[]{:S(2)}) collective-permute-start(bf16[432,128]{1,0:T(8,128)(2,1)S(1)} %get-tuple-element.53), channel_id=1, source_target_pairs={{0,6},{1,7},{2,4},{3,5},{4,2},{5,3},{6,0},{7,1},{8,14},{9,15},{10,... | collective-permute-start | bytes 331784 | tf_op jit(solution)/shard_map/ppermute | solution.py:626
  52.3 5.3 %collective-permute-start.6 = (bf16[128,256]{1,0:T(8,128)(2,1)S(1)}, bf16[128,256]{1,0:T(8,128)(2,1)S(1)}, u32[]{:S(2)}, u32[]{:S(2)}) collective-permute-start(bf16[128,256]{1,0:T(8,128)(2,1)S(1)} %copy-done.10), channel_id=1, source_target_pairs={{0,1},{1,0},{2,3},{3,2},{4,5},{5,4},{6,7},{7,6},{8,9},{9,8},{10,11... | collective-permute-start | bytes 196616 | tf_op jit(solution)/shard_map/ppermute | solution.py:626
  52.3 5.3 %collective-permute-start.7 = (bf16[128,256]{1,0:T(8,128)(2,1)S(1)}, bf16[128,256]{1,0:T(8,128)(2,1)S(1)}, u32[]{:S(2)}, u32[]{:S(2)}) collective-permute-start(bf16[128,256]{1,0:T(8,128)(2,1)S(1)} %copy-done.9), channel_id=1, source_target_pairs={{1,2},{3,4},{5,6},{7,8},{9,10},{11,12},{13,14},{2,1},{4,3},{6,5},{... | collective-permute-start | bytes 196616 | tf_op jit(solution)/shard_map/ppermute | solution.py:621
  57.5 10.9 %copy-start.8 = (f32[8,1024]{1,0:T(8,128)S(1)}, f32[8,1024]{1,0:T(8,128)}, u32[]{:S(2)}) copy-start(f32[8,1024]{1,0:T(8,128)} %get-tuple-element.65.place_ref) | copy-start | bytes 98308
  61.8 9.1 %collective-permute-start.8 = (bf16[432,128]{1,0:T(8,128)(2,1)S(1)}, bf16[432,128]{1,0:T(8,128)(2,1)S(1)}, u32[]{:S(2)}, u32[]{:S(2)}) collective-permute-start(bf16[432,128]{1,0:T(8,128)(2,1)S(1)} %add_convert_fusion.1), channel_id=1, source_target_pairs={{0,8},{1,9},{2,10},{3,11},{4,12},{5,13},{6,14},{7,15},{8,0},{9,1},... | collective-permute-start | bytes 331784 | tf_op jit(solution)/shard_map/ppermute | solution.py:626
  70.9 6.9 %collective-permute-start.13 = (bf16[432,128]{1,0:T(8,128)(2,1)S(1)}, bf16[432,128]{1,0:T(8,128)(2,1)S(1)}, u32[]{:S(2)}, u32[]{:S(2)}) collective-permute-start(bf16[432,128]{1,0:T(8,128)(2,1)S(1)} %add_convert_fusion.refs_0_), channel_id=1, source_target_pairs={{0,6},{1,7},{2,4},{3,5},{4,2},{5,3},{6,0},{7,1},{8,14},{9,15},{10,... | collective-permute-start | bytes 331784 | tf_op jit(solution)/shard_map/ppermute | solution.py:626
  72.3 5.5 %collective-permute-start.11 = (bf16[432,128]{1,0:T(8,128)(2,1)S(1)}, bf16[432,128]{1,0:T(8,128)(2,1)S(1)}, u32[]{:S(2)}, u32[]{:S(2)}) collective-permute-start(bf16[432,128]{1,0:T(8,128)(2,1)S(1)} %add_convert_fusion.refs_0_), channel_id=1, source_target_pairs={{0,4},{1,5},{2,6},{3,7},{4,0},{5,1},{6,2},{7,3},{8,12},{9,13},{10,... | collective-permute-start | bytes 331784 | tf_op jit(solution)/shard_map/ppermute | solution.py:626
  73.0 6.0 %collective-permute-start.9 = (bf16[432,128]{1,0:T(8,128)(2,1)S(1)}, bf16[432,128]{1,0:T(8,128)(2,1)S(1)}, u32[]{:S(2)}, u32[]{:S(2)}) collective-permute-start(bf16[432,128]{1,0:T(8,128)(2,1)S(1)} %add_convert_fusion.refs_0_), channel_id=1, source_target_pairs={{0,2},{1,3},{2,0},{3,1},{4,6},{5,7},{6,4},{7,5},{8,10},{9,11},{10,... | collective-permute-start | bytes 331784 | tf_op jit(solution)/shard_map/ppermute | solution.py:626
  74.4 4.5 %collective-permute-start.15 = (bf16[432,128]{1,0:T(8,128)(2,1)S(1)}, bf16[432,128]{1,0:T(8,128)(2,1)S(1)}, u32[]{:S(2)}, u32[]{:S(2)}) collective-permute-start(bf16[432,128]{1,0:T(8,128)(2,1)S(1)} %add_convert_fusion.refs_0_), channel_id=1, source_target_pairs={{0,1},{1,0},{2,3},{3,2},{4,5},{5,4},{6,7},{7,6},{8,9},{9,8},{10,11... | collective-permute-start | bytes 331784 | tf_op jit(solution)/shard_map/ppermute | solution.py:626
  77.8 2.2 %collective-permute-start.14 = (bf16[432,128]{1,0:T(8,128)(2,1)S(1)}, bf16[432,128]{1,0:T(8,128)(2,1)S(1)}, u32[]{:S(2)}, u32[]{:S(2)}) collective-permute-start(bf16[432,128]{1,0:T(8,128)(2,1)S(1)} %collective-permute-done.13.refs_3_), channel_id=1, source_target_pairs={{0,1},{1,0},{2,3},{3,2},{4,5},{5,4},{6,7},{7,6},{8,9},{9,8},{10,11... | collective-permute-start | bytes 331784 | tf_op jit(solution)/shard_map/ppermute | solution.py:626
  77.8 2.2 %collective-permute-start.12 = (bf16[432,128]{1,0:T(8,128)(2,1)S(1)}, bf16[432,128]{1,0:T(8,128)(2,1)S(1)}, u32[]{:S(2)}, u32[]{:S(2)}) collective-permute-start(bf16[432,128]{1,0:T(8,128)(2,1)S(1)} %collective-permute-done.11.refs_2_), channel_id=1, source_target_pairs={{0,1},{1,0},{2,3},{3,2},{4,5},{5,4},{6,7},{7,6},{8,9},{9,8},{10,11... | collective-permute-start | bytes 331784 | tf_op jit(solution)/shard_map/ppermute | solution.py:626
  79.0 1.3 %collective-permute-start.10 = (bf16[432,128]{1,0:T(8,128)(2,1)S(1)}, bf16[432,128]{1,0:T(8,128)(2,1)S(1)}, u32[]{:S(2)}, u32[]{:S(2)}) collective-permute-start(bf16[432,128]{1,0:T(8,128)(2,1)S(1)} %collective-permute-done.9.refs_1_), channel_id=1, source_target_pairs={{0,1},{1,0},{2,3},{3,2},{4,5},{5,4},{6,7},{7,6},{8,9},{9,8},{10,11... | collective-permute-start | bytes 331784 | tf_op jit(solution)/shard_map/ppermute | solution.py:626

commit v7 on v6

--- a/solution.py
+++ b/solution.py
@@ -518,7 +518,7 @@
             pltpu.SemaphoreType.DMA((7,)),
         ],
         flops=4 * total * DENSE * channels,
-        limit=60,
+        limit=52,
     )
 
 

time: 81.8 us -> 81 us (level)
  waiting for transfers between devices: 16.5 us -> 18.3 us
  local copies, waits for them, and re-layouts: 5.53 us -> 3.74 us
  starting transfers between devices: 28 us -> 26.7 us
    unnamed x22 -> x10, local copies, waits for them, and re-layouts: 2.65 us -> 0.89 us
    ppermute x14, waiting for transfers between devices: 10.5 us -> 11.5 us  [swapped(): return lax.ppermute(array, 'region', [(i, i ^ bit) for i in range(count)])]
  transfers between devices with their start and end apart: 18 -> 18, of which waited for: 6 -> 8; matrix products, arithmetic and copies ran while one was open for 4% -> 4% of each run, Pallas kernels for 24% -> 25%
where the time goes in v7:
time: 81 us; the launch traced here: 80.7 us
  Pallas kernels  30.8 us (38%)
  starting transfers between devices  26.7 us (33%)
  waiting for transfers between devices  18.3 us (23%)
  local copies, waits for them, and re-layouts  3.74 us (5%)
  between operations  1.03 us (1%)
    pallas_call x10, Pallas kernels, call(): pl.pallas_call(body, out_shape=outs, in_specs=[SMEM if i in smem else FAR...  28.9 us
    all_to_all x2, starting transfers between devices, exchange(): lax.all_to_all(array, 'region', split_axis=0, concat_axis=0, tiled=True)  13.9 us
    ppermute x14, waiting for transfers between devices, swapped(): return lax.ppermute(array, 'region', [(i, i ^ bit) for i in range(count)])  11.5 us
    ppermute x14, starting transfers between devices, swapped(): return lax.ppermute(array, 'region', [(i, i ^ bit) for i in range(count)])  11.3 us
    all_to_all x2, waiting for transfers between devices, exchange(): lax.all_to_all(array, 'region', split_axis=0, concat_axis=0, tiled=True)  6.72 us
    transpose x2, local copies, waits for them, and re-layouts, local(): jnp.transpose(kernel[::-1], (0, 2, 1)).reshape(KOFF * channels, channels)  2.85 us
    pallas_call x2, Pallas kernels, last_step(): pl.pallas_call(functools.partial(last_body, size, places), out_shape=jax....  1.91 us
  transfers between devices with their start and end apart: 18, of which 8 were waited for; matrix products, arithmetic and copies ran while one was open for 4% of the time, Pallas kernels for 25%

profile of v7, /device:TPU:0, one launch (start us, length us, event | category | flops | bytes accessed | tf_op | source)
XLA Modules:
  0.0 80.7 jit_solution(3451045887383954674)
XLA Ops:
  0.7 3.0 %shard_map.85 = (bf16[16,176,128]{2,1,0:T(8,128)(2,1)}, f32[8,1024]{1,0:T(8,128)}) custom-call(s32[1,1024]{1,0:T(1,128)} %bitcast.12, s32[1,1024]{1,0:T(1,128)} %bitcast.13, bf16[1024,128]{1,0:T(8,128)(2,1)} %feats_far.1), custom_call_target="tpu_custom_call" | custom-call | flops 671088640 | bytes 1024000 | tf_op jit(solution)/shard_map/pallas_call | solution.py:46
  3.7 7.4 %all-to-all-start = ((bf16[16,176,128]{2,1,0:T(8,128)(2,1)}), bf16[16,176,128]{2,1,0:T(8,128)(2,1)}, u32[]{:S(2)}, u32[]{:S(2)}) async-start(bf16[16,176,128]{2,1,0:T(8,128)(2,1)} %get-tuple-element.38), calls=%async_computation | async-start | bytes 1441792 | tf_op jit(solution)/shard_map/all_to_all | solution.py:707
  11.1 0.9 %shard_map.86 = (bf16[8,256,128]{2,1,0:T(8,128)(2,1)S(1)}, bf16[256,128]{1,0:T(8,128)(2,1)S(1)}, bf16[256,128]{1,0:T(8,128)(2,1)S(1)}) custom-call(s32[16,27]{1,0:T(8,128)S(1)} %copy-done.2, bf16[16,128,128]{2,1,0:T(8,128)(2,1)S(1)} %copy-done.1), custom_call_target="tpu_custom_call" | custom-call | bytes 1181376 | tf_op jit(solution)/shard_map/pallas_call | solution.py:46
  12.4 0.7 collective-permute-start.1
  13.1 1.0 %reverse_bitcast_fusion = bf16[27,128,128]{1,2,0:T(8,128)(2,1)} fusion(bf16[27,128,128]{2,1,0:T(8,128)(2,1)S(1)} %copy-done), kind=kLoop, calls=%fused_computation | loop fusion | bytes 1769472 | tf_op jit(solution)/shard_map/transpose | solution.py:722
  14.1 1.9 %copy.10 = bf16[27,128,128]{2,1,0:T(8,128)(2,1)S(1)} copy(bf16[27,128,128]{1,2,0:T(8,128)(2,1)} %reverse_bitcast_fusion) | data formatting | bytes 1769472 | tf_op jit(solution)/shard_map/transpose | solution.py:722
  15.9 4.1 %shard_map.87.grad_far = f32[6,256,128]{2,1,0:T(8,128)S(1)} custom-call(bf16[8,256,128]{2,1,0:T(8,128)(2,1)S(1)} %get-tuple-element.39.dense_ref, bf16[3456,128]{1,0:T(8,128)(2,1)S(1)} %bitcast.9), custom_call_target="tpu_custom_call" | custom-call | flops 1358954496 | bytes 2195456 | tf_op jit(solution)/shard_map/pallas_call | solution.py:46
  20.1 0.9 %copy-done.3 = f32[6,256,128]{2,1,0:T(8,128)} copy-done((f32[6,256,128]{2,1,0:T(8,128)}, f32[6,256,128]{2,1,0:T(8,128)S(1)}, u32[]{:S(2)}) %copy-start.3) | copy-done | bytes 786456
  20.9 1.1 %shard_map.88.edge_far = f32[2,256,128]{2,1,0:T(8,128)S(1)} custom-call(bf16[8,256,128]{2,1,0:T(8,128)(2,1)S(1)} %get-tuple-element.39.dense_ref, bf16[256,128]{1,0:T(8,128)(2,1)S(1)} %collective-permute-done.near_ref, bf16[256,128]{1,0:T(8,128)(2,1)S(1)} %collective-permute-done.1.away_ref, bf16[3456,128]{1,0:T(8,128)(2,1)S(1)} %bitcast.10), custom_call_target="tpu_custom_call" | custom-call | flops 452984832 | bytes 1802240 | tf_op jit(solution)/shard_map/pallas_call | solution.py:46
  22.1 6.7 %all-to-all-done.msg_far = bf16[16,176,128]{2,1,0:T(8,128)(2,1)} async-done(((bf16[16,176,128]{2,1,0:T(8,128)(2,1)}), bf16[16,176,128]{2,1,0:T(8,128)(2,1)}, u32[]{:S(2)}, u32[]{:S(2)}) %all-to-all-start) | async-done | bytes 720928 | tf_op jit(solution)/shard_map/all_to_all | solution.py:707
  28.8 7.0 %shard_map.89 = (bf16[128,2048]{1,0:T(8,128)(2,1)S(1)}, bf16[128,256]{1,0:T(8,128)(2,1)S(1)}, bf16[128,256]{1,0:T(8,128)(2,1)S(1)}, bf16[16,160,128]{2,1,0:T(8,128)(2,1)}) custom-call(s32[16,27]{1,0:T(8,128)S(1)} %copy-done.2, bf16[16,176,128]{2,1,0:T(8,128)(2,1)} %all-to-all-done.msg_far, f32[6,256,128]{2,1,0:T(8,128)} %copy-done.3, ...), custom_call_target="tpu_custom_call" | custom-call | flops 2684354560 | bytes 3081920 | tf_op jit(solution)/shard_map/pallas_call | solution.py:46
  35.8 6.5 %all-to-all-start.1 = ((bf16[16,160,128]{2,1,0:T(8,128)(2,1)}), bf16[16,160,128]{2,1,0:T(8,128)(2,1)S(1)}, u32[]{:S(2)}, u32[]{:S(2)}) async-start(bf16[16,160,128]{2,1,0:T(8,128)(2,1)} %get-tuple-element.54), calls=%async_computation.1 | async-start | bytes 1310720 | tf_op jit(solution)/shard_map/all_to_all | solution.py:707
  42.3 2.7 %shard_map.90 = (f32[1728,128]{1,0:T(8,128)S(1)}, f32[1728,128]{1,0:T(8,128)S(1)}) custom-call(bf16[128,2048]{1,0:T(8,128)(2,1)S(1)} %get-tuple-element.55.turned_ref.turned_far, bf16[256,128]{1,0:T(8,128)(2,1)S(1)} %collective-permute-done.near_ref, bf16[256,128]{1,0:T(8,128)(2,1)S(1)} %collective-permute-done.1.away_ref, ...), custom_call_target="tpu_custom_call" | custom-call | flops 1811939328 | bytes 2949120 | tf_op jit(solution)/shard_map/pallas_call | solution.py:46
  45.0 0.5 collective-permute-start.2
  45.5 2.1 %collective-permute-done.2.got_ref = f32[1728,128]{1,0:T(8,128)S(1)} collective-permute-done((f32[1728,128]{1,0:T(8,128)S(1)}, f32[1728,128]{1,0:T(8,128)S(1)}, u32[]{:S(2)}, u32[]{:S(2)}) %collective-permute-start.2) | collective-permute-done | bytes 884768 | tf_op jit(solution)/shard_map/ppermute | solution.py:626
  47.6 1.9 %collective-permute-start.3 = (bf16[432,128]{1,0:T(8,128)(2,1)S(1)}, bf16[432,128]{1,0:T(8,128)(2,1)S(1)}, u32[]{:S(2)}, u32[]{:S(2)}) collective-permute-start(bf16[432,128]{1,0:T(8,128)(2,1)S(1)} %get-tuple-element.51), channel_id=1, source_target_pairs={{0,2},{1,3},{2,0},{3,1},{4,6},{5,7},{6,4},{7,5},{8,10},{9,11},{10,... | collective-permute-start | bytes 331784 | tf_op jit(solution)/shard_map/ppermute | solution.py:626
  49.6 1.5 %collective-permute-start.4 = (bf16[432,128]{1,0:T(8,128)(2,1)S(1)}, bf16[432,128]{1,0:T(8,128)(2,1)S(1)}, u32[]{:S(2)}, u32[]{:S(2)}) collective-permute-start(bf16[432,128]{1,0:T(8,128)(2,1)S(1)} %get-tuple-element.52), channel_id=1, source_target_pairs={{0,4},{1,5},{2,6},{3,7},{4,0},{5,1},{6,2},{7,3},{8,12},{9,13},{10,... | collective-permute-start | bytes 331784 | tf_op jit(solution)/shard_map/ppermute | solution.py:626
  51.2 0.8 %collective-permute-start.7 = (bf16[128,256]{1,0:T(8,128)(2,1)S(1)}, bf16[128,256]{1,0:T(8,128)(2,1)S(1)}, u32[]{:S(2)}, u32[]{:S(2)}) collective-permute-start(bf16[128,256]{1,0:T(8,128)(2,1)S(1)} %get-tuple-element.57), channel_id=1, source_target_pairs={{1,2},{3,4},{5,6},{7,8},{9,10},{11,12},{13,14},{2,1},{4,3},{6,5},{... | collective-permute-start | bytes 196616 | tf_op jit(solution)/shard_map/ppermute | solution.py:621
  52.0 4.3 %shard_map.92.inner_far = bf16[6,256,128]{2,1,0:T(8,128)(2,1)S(1)} custom-call(bf16[128,2048]{1,0:T(8,128)(2,1)S(1)} %get-tuple-element.55.turned_ref.turned_far, bf16[3456,128]{1,0:T(8,128)(2,1)S(1)} %bitcast.7), custom_call_target="tpu_custom_call" | custom-call | bytes 1024 | tf_op jit(solution)/shard_map/pallas_call | solution.py:46
  56.4 0.9 %collective-permute-done.4 = bf16[432,128]{1,0:T(8,128)(2,1)S(1)} collective-permute-done((bf16[432,128]{1,0:T(8,128)(2,1)S(1)}, bf16[432,128]{1,0:T(8,128)(2,1)S(1)}, u32[]{:S(2)}, u32[]{:S(2)}) %collective-permute-start.4) | collective-permute-done | bytes 110624 | tf_op jit(solution)/shard_map/ppermute | solution.py:626
  57.3 4.3 %collective-permute-done.5 = bf16[432,128]{1,0:T(8,128)(2,1)S(1)} collective-permute-done((bf16[432,128]{1,0:T(8,128)(2,1)S(1)}, bf16[432,128]{1,0:T(8,128)(2,1)S(1)}, u32[]{:S(2)}, u32[]{:S(2)}) %collective-permute-start.5) | collective-permute-done | bytes 110624 | tf_op jit(solution)/shard_map/ppermute | solution.py:626
  61.7 3.3 %collective-permute-start.8 = (bf16[432,128]{1,0:T(8,128)(2,1)S(1)}, bf16[432,128]{1,0:T(8,128)(2,1)S(1)}, u32[]{:S(2)}, u32[]{:S(2)}) collective-permute-start(bf16[432,128]{1,0:T(8,128)(2,1)S(1)} %add_convert_fusion.1), channel_id=1, source_target_pairs={{0,8},{1,9},{2,10},{3,11},{4,12},{5,13},{6,14},{7,15},{8,0},{9,1},... | collective-permute-start | bytes 331784 | tf_op jit(solution)/shard_map/ppermute | solution.py:626
  65.0 3.2 %shard_map.94 = bf16[16,128,128]{2,1,0:T(8,128)(2,1)} custom-call(s32[16,27]{1,0:T(8,128)S(1)} %copy-done.2, bf16[128,2048]{1,0:T(8,128)(2,1)S(1)} %get-tuple-element.55.turned_ref.turned_far, bf16[128,256]{1,0:T(8,128)(2,1)S(1)} %collective-permute-done.6.near_ref, bf16[128,256]{1,0:T(8,128)(2,1)S(1)} %collective-permute-done.7.away_ref, ...), custom_call_target="tpu_custom_call" | custom-call | flops 452984832 | bytes 2459328 | tf_op jit(solution)/shard_map/pallas_call | solution.py:46
  68.2 2.4 %shard_map.93 = bf16[1024,128]{1,0:T(8,128)(2,1)} custom-call(f32[8,1024]{1,0:T(8,128)S(1)} %copy-done.4, bf16[16,160,128]{2,1,0:T(8,128)(2,1)S(1)} %all-to-all-done.1.rows_ref), custom_call_target="tpu_custom_call" | custom-call | flops 671088640 | bytes 950272 | tf_op jit(solution)/shard_map/pallas_call | solution.py:46
  70.7 0.5 collective-permute-start.13
  71.2 1.4 %collective-permute-start.11 = (bf16[432,128]{1,0:T(8,128)(2,1)S(1)}, bf16[432,128]{1,0:T(8,128)(2,1)S(1)}, u32[]{:S(2)}, u32[]{:S(2)}) collective-permute-start(bf16[432,128]{1,0:T(8,128)(2,1)S(1)} %add_convert_fusion.refs_0_), channel_id=1, source_target_pairs={{0,4},{1,5},{2,6},{3,7},{4,0},{5,1},{6,2},{7,3},{8,12},{9,13},{10,... | collective-permute-start | bytes 331784 | tf_op jit(solution)/shard_map/ppermute | solution.py:626
  72.7 1.6 %collective-permute-start.9 = (bf16[432,128]{1,0:T(8,128)(2,1)S(1)}, bf16[432,128]{1,0:T(8,128)(2,1)S(1)}, u32[]{:S(2)}, u32[]{:S(2)}) collective-permute-start(bf16[432,128]{1,0:T(8,128)(2,1)S(1)} %add_convert_fusion.refs_0_), channel_id=1, source_target_pairs={{0,2},{1,3},{2,0},{3,1},{4,6},{5,7},{6,4},{7,5},{8,10},{9,11},{10,... | collective-permute-start | bytes 331784 | tf_op jit(solution)/shard_map/ppermute | solution.py:626
  74.3 3.0 %collective-permute-done.13.refs_3_ = bf16[432,128]{1,0:T(8,128)(2,1)S(1)} collective-permute-done((bf16[432,128]{1,0:T(8,128)(2,1)S(1)}, bf16[432,128]{1,0:T(8,128)(2,1)S(1)}, u32[]{:S(2)}, u32[]{:S(2)}) %collective-permute-start.13) | collective-permute-done | bytes 110624 | tf_op jit(solution)/shard_map/ppermute | solution.py:626
  77.2 0.5 collective-permute-done.11.refs_2_
  77.7 0.6 collective-permute-done.9.refs_1_
  78.3 1.0 %shard_map.95.refs_3_ = f32[3456,128]{1,0:T(8,128)} custom-call(bf16[432,128]{1,0:T(8,128)(2,1)S(1)} %add_convert_fusion.refs_0_, bf16[432,128]{1,0:T(8,128)(2,1)S(1)} %collective-permute-done.9.refs_1_, bf16[432,128]{1,0:T(8,128)(2,1)S(1)} %collective-permute-done.11.refs_2_, bf16[432,128]{1,0:T(8,128)(2,1)S(1)} %collective-permute-done.13.refs_3_, ...), custom_call_target="tpu_custom_call" | custom-call | bytes 1658880 | tf_op jit(solution)/shard_map/pallas_call | solution.py:689
  79.6 0.9 %shard_map.96 = f32[3456,128]{1,0:T(8,128)} custom-call(bf16[432,128]{1,0:T(8,128)(2,1)S(1)} %collective-permute-done.10.refs_0_, bf16[432,128]{1,0:T(8,128)(2,1)S(1)} %collective-permute-done.12.refs_1_, bf16[432,128]{1,0:T(8,128)(2,1)S(1)} %collective-permute-done.14.refs_2_, f32[3456,128]{1,0:T(8,128)} %shard_map.95.refs_3_), custom_call_target="tpu_custom_call", output_to_operand_aliasing={{}: (3, {})} | custom-call | bytes 995328 | tf_op jit(solution)/shard_map/pallas_call | solution.py:689
  (30 shorter events, 1.1 us)
Async XLA Ops:
  0.6 10.4 %copy-start.1 = (bf16[16,128,128]{2,1,0:T(8,128)(2,1)S(1)}, bf16[16,128,128]{2,1,0:T(8,128)(2,1)}, u32[]{:S(2)}) copy-start(bf16[16,128,128]{2,1,0:T(8,128)(2,1)} %bricks_ref.1) | copy-start | bytes 1572868
  0.6 10.4 %copy-start.2 = (s32[16,27]{1,0:T(8,128)S(1)}, s32[16,27]{1,0:T(8,128)}, u32[]{:S(2)}) copy-start(s32[16,27]{1,0:T(8,128)} %adj_ref.3) | copy-start | bytes 5188
  0.7 12.4 %copy-start = (bf16[27,128,128]{2,1,0:T(8,128)(2,1)S(1)}, bf16[27,128,128]{2,1,0:T(8,128)(2,1)}, u32[]{:S(2)}) copy-start(bf16[27,128,128]{2,1,0:T(8,128)(2,1)} %param.10) | copy-start | bytes 2654212
  3.7 25.1 %all-to-all-start = ((bf16[16,176,128]{2,1,0:T(8,128)(2,1)}), bf16[16,176,128]{2,1,0:T(8,128)(2,1)}, u32[]{:S(2)}, u32[]{:S(2)}) async-start(bf16[16,176,128]{2,1,0:T(8,128)(2,1)} %get-tuple-element.38), calls=%async_computation | async-start | bytes 1441792 | tf_op jit(solution)/shard_map/all_to_all | solution.py:707
  12.0 9.0 %collective-permute-start = (bf16[256,128]{1,0:T(8,128)(2,1)S(1)}, bf16[256,128]{1,0:T(8,128)(2,1)S(1)}, u32[]{:S(2)}, u32[]{:S(2)}) collective-permute-start(bf16[256,128]{1,0:T(8,128)(2,1)S(1)} %get-tuple-element.40), channel_id=1, source_target_pairs={{0,1},{1,0},{2,3},{3,2},{4,5},{5,4},{6,7},{7,6},{8,9},{9,8},{10,11... | collective-permute-start | bytes 196616 | tf_op jit(solution)/shard_map/ppermute | solution.py:626
  12.4 8.5 %collective-permute-start.1 = (bf16[256,128]{1,0:T(8,128)(2,1)S(1)}, bf16[256,128]{1,0:T(8,128)(2,1)S(1)}, u32[]{:S(2)}, u32[]{:S(2)}) collective-permute-start(bf16[256,128]{1,0:T(8,128)(2,1)S(1)} %get-tuple-element.41), channel_id=1, source_target_pairs={{1,2},{3,4},{5,6},{7,8},{9,10},{11,12},{13,14},{2,1},{4,3},{6,5},{... | collective-permute-start | bytes 196616 | tf_op jit(solution)/shard_map/ppermute | solution.py:621
  20.1 0.9 %copy-start.3 = (f32[6,256,128]{2,1,0:T(8,128)}, f32[6,256,128]{2,1,0:T(8,128)S(1)}, u32[]{:S(2)}) copy-start(f32[6,256,128]{2,1,0:T(8,128)S(1)} %shard_map.87.grad_far) | copy-start | bytes 2359300
  35.8 25.8 %all-to-all-start.1 = ((bf16[16,160,128]{2,1,0:T(8,128)(2,1)}), bf16[16,160,128]{2,1,0:T(8,128)(2,1)S(1)}, u32[]{:S(2)}, u32[]{:S(2)}) async-start(bf16[16,160,128]{2,1,0:T(8,128)(2,1)} %get-tuple-element.54), calls=%async_computation.1 | async-start | bytes 1310720 | tf_op jit(solution)/shard_map/all_to_all | solution.py:707
  45.0 2.5 %collective-permute-start.2 = (f32[1728,128]{1,0:T(8,128)S(1)}, f32[1728,128]{1,0:T(8,128)S(1)}, u32[]{:S(2)}, u32[]{:S(2)}) collective-permute-start(f32[1728,128]{1,0:T(8,128)S(1)} %get-tuple-element.44), channel_id=1, source_target_pairs={{0,1},{1,0},{2,3},{3,2},{4,5},{5,4},{6,7},{7,6},{8,9},{9,8},{10,11... | collective-permute-start | bytes 2654216 | tf_op jit(solution)/shard_map/ppermute | solution.py:626
  47.6 8.8 %collective-permute-start.3 = (bf16[432,128]{1,0:T(8,128)(2,1)S(1)}, bf16[432,128]{1,0:T(8,128)(2,1)S(1)}, u32[]{:S(2)}, u32[]{:S(2)}) collective-permute-start(bf16[432,128]{1,0:T(8,128)(2,1)S(1)} %get-tuple-element.51), channel_id=1, source_target_pairs={{0,2},{1,3},{2,0},{3,1},{4,6},{5,7},{6,4},{7,5},{8,10},{9,11},{10,... | collective-permute-start | bytes 331784 | tf_op jit(solution)/shard_map/ppermute | solution.py:626
  49.6 7.8 %collective-permute-start.4 = (bf16[432,128]{1,0:T(8,128)(2,1)S(1)}, bf16[432,128]{1,0:T(8,128)(2,1)S(1)}, u32[]{:S(2)}, u32[]{:S(2)}) collective-permute-start(bf16[432,128]{1,0:T(8,128)(2,1)S(1)} %get-tuple-element.52), channel_id=1, source_target_pairs={{0,4},{1,5},{2,6},{3,7},{4,0},{5,1},{6,2},{7,3},{8,12},{9,13},{10,... | collective-permute-start | bytes 331784 | tf_op jit(solution)/shard_map/ppermute | solution.py:626
  51.0 10.6 %collective-permute-start.5 = (bf16[432,128]{1,0:T(8,128)(2,1)S(1)}, bf16[432,128]{1,0:T(8,128)(2,1)S(1)}, u32[]{:S(2)}, u32[]{:S(2)}) collective-permute-start(bf16[432,128]{1,0:T(8,128)(2,1)S(1)} %get-tuple-element.53), channel_id=1, source_target_pairs={{0,6},{1,7},{2,4},{3,5},{4,2},{5,3},{6,0},{7,1},{8,14},{9,15},{10,... | collective-permute-start | bytes 331784 | tf_op jit(solution)/shard_map/ppermute | solution.py:626
  51.2 5.2 %collective-permute-start.6 = (bf16[128,256]{1,0:T(8,128)(2,1)S(1)}, bf16[128,256]{1,0:T(8,128)(2,1)S(1)}, u32[]{:S(2)}, u32[]{:S(2)}) collective-permute-start(bf16[128,256]{1,0:T(8,128)(2,1)S(1)} %get-tuple-element.56), channel_id=1, source_target_pairs={{0,1},{1,0},{2,3},{3,2},{4,5},{5,4},{6,7},{7,6},{8,9},{9,8},{10,11... | collective-permute-start | bytes 196616 | tf_op jit(solution)/shard_map/ppermute | solution.py:626
  51.2 5.2 %collective-permute-start.7 = (bf16[128,256]{1,0:T(8,128)(2,1)S(1)}, bf16[128,256]{1,0:T(8,128)(2,1)S(1)}, u32[]{:S(2)}, u32[]{:S(2)}) collective-permute-start(bf16[128,256]{1,0:T(8,128)(2,1)S(1)} %get-tuple-element.57), channel_id=1, source_target_pairs={{1,2},{3,4},{5,6},{7,8},{9,10},{11,12},{13,14},{2,1},{4,3},{6,5},{... | collective-permute-start | bytes 196616 | tf_op jit(solution)/shard_map/ppermute | solution.py:621
  56.4 11.8 %copy-start.4 = (f32[8,1024]{1,0:T(8,128)S(1)}, f32[8,1024]{1,0:T(8,128)}, u32[]{:S(2)}) copy-start(f32[8,1024]{1,0:T(8,128)} %get-tuple-element.65.place_ref) | copy-start | bytes 98308
  61.7 9.0 %collective-permute-start.8 = (bf16[432,128]{1,0:T(8,128)(2,1)S(1)}, bf16[432,128]{1,0:T(8,128)(2,1)S(1)}, u32[]{:S(2)}, u32[]{:S(2)}) collective-permute-start(bf16[432,128]{1,0:T(8,128)(2,1)S(1)} %add_convert_fusion.1), channel_id=1, source_target_pairs={{0,8},{1,9},{2,10},{3,11},{4,12},{5,13},{6,14},{7,15},{8,0},{9,1},... | collective-permute-start | bytes 331784 | tf_op jit(solution)/shard_map/ppermute | solution.py:626
  70.7 6.5 %collective-permute-start.13 = (bf16[432,128]{1,0:T(8,128)(2,1)S(1)}, bf16[432,128]{1,0:T(8,128)(2,1)S(1)}, u32[]{:S(2)}, u32[]{:S(2)}) collective-permute-start(bf16[432,128]{1,0:T(8,128)(2,1)S(1)} %add_convert_fusion.refs_0_), channel_id=1, source_target_pairs={{0,6},{1,7},{2,4},{3,5},{4,2},{5,3},{6,0},{7,1},{8,14},{9,15},{10,... | collective-permute-start | bytes 331784 | tf_op jit(solution)/shard_map/ppermute | solution.py:626
  71.2 6.5 %collective-permute-start.11 = (bf16[432,128]{1,0:T(8,128)(2,1)S(1)}, bf16[432,128]{1,0:T(8,128)(2,1)S(1)}, u32[]{:S(2)}, u32[]{:S(2)}) collective-permute-start(bf16[432,128]{1,0:T(8,128)(2,1)S(1)} %add_convert_fusion.refs_0_), channel_id=1, source_target_pairs={{0,4},{1,5},{2,6},{3,7},{4,0},{5,1},{6,2},{7,3},{8,12},{9,13},{10,... | collective-permute-start | bytes 331784 | tf_op jit(solution)/shard_map/ppermute | solution.py:626
  72.7 5.6 %collective-permute-start.9 = (bf16[432,128]{1,0:T(8,128)(2,1)S(1)}, bf16[432,128]{1,0:T(8,128)(2,1)S(1)}, u32[]{:S(2)}, u32[]{:S(2)}) collective-permute-start(bf16[432,128]{1,0:T(8,128)(2,1)S(1)} %add_convert_fusion.refs_0_), channel_id=1, source_target_pairs={{0,2},{1,3},{2,0},{3,1},{4,6},{5,7},{6,4},{7,5},{8,10},{9,11},{10,... | collective-permute-start | bytes 331784 | tf_op jit(solution)/shard_map/ppermute | solution.py:626
  74.3 4.1 %collective-permute-start.15 = (bf16[432,128]{1,0:T(8,128)(2,1)S(1)}, bf16[432,128]{1,0:T(8,128)(2,1)S(1)}, u32[]{:S(2)}, u32[]{:S(2)}) collective-permute-start(bf16[432,128]{1,0:T(8,128)(2,1)S(1)} %add_convert_fusion.refs_0_), channel_id=1, source_target_pairs={{0,1},{1,0},{2,3},{3,2},{4,5},{5,4},{6,7},{7,6},{8,9},{9,8},{10,11... | collective-permute-start | bytes 331784 | tf_op jit(solution)/shard_map/ppermute | solution.py:626
  77.2 2.1 %collective-permute-start.14 = (bf16[432,128]{1,0:T(8,128)(2,1)S(1)}, bf16[432,128]{1,0:T(8,128)(2,1)S(1)}, u32[]{:S(2)}, u32[]{:S(2)}) collective-permute-start(bf16[432,128]{1,0:T(8,128)(2,1)S(1)} %collective-permute-done.13.refs_3_), channel_id=1, source_target_pairs={{0,1},{1,0},{2,3},{3,2},{4,5},{5,4},{6,7},{7,6},{8,9},{9,8},{10,11... | collective-permute-start | bytes 331784 | tf_op jit(solution)/shard_map/ppermute | solution.py:626
  77.7 1.6 %collective-permute-start.12 = (bf16[432,128]{1,0:T(8,128)(2,1)S(1)}, bf16[432,128]{1,0:T(8,128)(2,1)S(1)}, u32[]{:S(2)}, u32[]{:S(2)}) collective-permute-start(bf16[432,128]{1,0:T(8,128)(2,1)S(1)} %collective-permute-done.11.refs_2_), channel_id=1, source_target_pairs={{0,1},{1,0},{2,3},{3,2},{4,5},{5,4},{6,7},{7,6},{8,9},{9,8},{10,11... | collective-permute-start | bytes 331784 | tf_op jit(solution)/shard_map/ppermute | solution.py:626
  78.3 1.3 %collective-permute-start.10 = (bf16[432,128]{1,0:T(8,128)(2,1)S(1)}, bf16[432,128]{1,0:T(8,128)(2,1)S(1)}, u32[]{:S(2)}, u32[]{:S(2)}) collective-permute-start(bf16[432,128]{1,0:T(8,128)(2,1)S(1)} %collective-permute-done.9.refs_1_), channel_id=1, source_target_pairs={{0,1},{1,0},{2,3},{3,2},{4,5},{5,4},{6,7},{7,6},{8,9},{9,8},{10,11... | collective-permute-start | bytes 331784 | tf_op jit(solution)/shard_map/ppermute | solution.py:626
